TPU v7x, 32 devices: a whole 2x2x4 slice. The times are simulated.
32 devices in a mesh: replica: 8 (over z, x), shard: 4 (over y, core).
Axes of the slice: x: 2, y: 2, z: 4, core: 2. Of those that a mesh axis runs over, the one named last changes fastest.
Arguments:
- tokens: bfloat16 [16, 1024, 1024], P('replica', 'shard'), may hold values from -6 to 6
- qkv_weight: bfloat16 [1024, 3072], P('shard'), may hold values from -0.25 to 0.25
- qv_bias: bfloat16 [2048], P('shard'), may hold values from -3 to 3
- proj_weight: bfloat16 [1024, 1024], P('shard'), may hold values from -0.5 to 0.5
- proj_bias: bfloat16 [1024], P('shard'), may hold values from -3 to 3
- up_weight: bfloat16 [1024, 4096], P('shard'), may hold values from -0.1875 to 0.1875
- up_bias: bfloat16 [4096], P('shard'), may hold values from -3 to 3
- down_weight: bfloat16 [4096, 1024], P('shard'), may hold values from -0.09375 to 0.09375
- down_bias: bfloat16 [1024], P('shard'), may hold values from -3 to 3
- attn_gain: bfloat16 [1024], P('shard'), may hold values from 0.5 to 1.5
- attn_shift: bfloat16 [1024], P('shard'), may hold values from -3 to 3
- mlp_gain: bfloat16 [1024], P('shard'), may hold values from 0.5 to 1.5
- mlp_shift: bfloat16 [1024], P('shard'), may hold values from -3 to 3
- attn_scale: bfloat16 [1024], P('shard'), may hold values from 0.25 to 1.75
- mlp_scale: bfloat16 [1024], P('shard'), may hold values from 0.25 to 1.75
- cotangent: bfloat16 [16, 1024, 1024], P('replica', 'shard'), may hold values from -6 to 6
- image_count: int32 [8], replicated, may hold values from 1 to 2, 10 in all
Outputs:
- output: bfloat16 [16, 1024, 1024], P('replica', 'shard')
- grad_tokens: float32 [16, 1024, 1024], P('replica', 'shard')
- grad_qkv_weight: float32 [1024, 3072], P('shard')
- grad_qv_bias: float32 [2048], P('shard')
- grad_proj_weight: float32 [1024, 1024], P('shard')
- grad_proj_bias: float32 [1024], P('shard')
- grad_up_weight: float32 [1024, 4096], P('shard')
- grad_up_bias: float32 [4096], P('shard')
- grad_down_weight: float32 [4096, 1024], P('shard')
- grad_down_bias: float32 [1024], P('shard')
- grad_attn_gain: float32 [1024], P('shard')
- grad_attn_shift: float32 [1024], P('shard')
- grad_mlp_gain: float32 [1024], P('shard')
- grad_mlp_shift: float32 [1024], P('shard')
- grad_attn_scale: float32 [1024], P('shard')
- grad_mlp_scale: float32 [1024], P('shard')
Inputs may be any that keep to these rules, and one draw needn't show every extreme that they name: image_count[g] images are live in group g, in its first slots; the busiest group holds exactly 2; the counts sum to 10.
All inputs are finite; a program needn't handle non-finite values.
Results may differ from a plain program's by a relative error of at most 0.012.
The roundings to bfloat16 on the way count: a program that leaves them out, or rounds other values in their place, can miss the bound.
Values may be sent and summed in bfloat16 or wider, within the bound.
A program may use at most 320 MiB of HBM per device.

v0:
```python
import jax
import jax.numpy as jnp
from jax import lax
from jax.sharding import PartitionSpec as P

HEAD_DIM = 64


EPS = 1e-06


def normalize(values, gain, shift):
    centre = values - jnp.mean(values, axis=-1, keepdims=True)
    spread = jnp.mean(centre * centre, axis=-1, keepdims=True)
    return centre * lax.rsqrt(spread + EPS) * gain + shift


def gelu_exact(values):
    return jax.nn.gelu(values, approximate=False)


def inner_rows(left, right):
    return lax.dot_general(
        left, right, (((0,), (0,)), ((), ())), preferred_element_type=jnp.float32
    )


def outer_cols(left, right):
    return lax.dot_general(
        left, right, (((1,), (1,)), ((), ())), preferred_element_type=jnp.float32
    )


def column_sum(values):
    return jnp.sum(values.astype(jnp.float32), axis=0)


def attend_forward(items):
    query, key, value = items
    factor = HEAD_DIM ** (-0.5)
    scores = jnp.einsum("qhd,khd->hqk", query, key, preferred_element_type=jnp.float32) * factor
    highest = jnp.max(scores, axis=-1, keepdims=True)
    expos = jnp.exp(scores - highest)
    denom = jnp.sum(expos, axis=-1, keepdims=True)
    probs = expos / denom
    logsum = highest + jnp.log(denom)
    attended = jnp.einsum(
        "hqk,khd->qhd", probs.astype(jnp.bfloat16), value, preferred_element_type=jnp.float32
    )
    return (attended, logsum)


def attend_backward(items):
    query, key, value, grad_att, logsum = items
    factor = HEAD_DIM ** (-0.5)
    scores = jnp.einsum("qhd,khd->hqk", query, key, preferred_element_type=jnp.float32) * factor
    probs = jnp.exp(scores - logsum)
    grad_values = jnp.einsum(
        "hqk,qhd->khd", probs.astype(jnp.bfloat16), grad_att, preferred_element_type=jnp.float32
    )
    grad_probs = jnp.einsum("qhd,khd->hqk", grad_att, value, preferred_element_type=jnp.float32)
    centre = jnp.sum(grad_probs * probs, axis=-1, keepdims=True)
    grad_scores = (probs * (grad_probs - centre)).astype(jnp.bfloat16)
    grad_queries = (
        jnp.einsum("hqk,khd->qhd", grad_scores, key, preferred_element_type=jnp.float32) * factor
    )
    grad_keys = (
        jnp.einsum("hqk,qhd->khd", grad_scores, query, preferred_element_type=jnp.float32) * factor
    )
    return (grad_queries, grad_keys, grad_values)


def on_device(
    tokens,
    qkv_weight,
    qv_bias,
    proj_weight,
    proj_bias,
    up_weight,
    up_bias,
    down_weight,
    down_bias,
    attn_gain,
    attn_shift,
    mlp_gain,
    mlp_shift,
    attn_scale,
    mlp_scale,
    cotangent,
    image_count,
):
    shards = (
        qkv_weight,
        qv_bias,
        proj_weight,
        proj_bias,
        up_weight,
        up_bias,
        down_weight,
        down_bias,
        attn_gain,
        attn_shift,
        mlp_gain,
        mlp_shift,
        attn_scale,
        mlp_scale,
    )
    gathered = (
        lax.all_gather(shards[0], "shard", axis=0, tiled=True),
        lax.all_gather(shards[1], "shard", axis=0, tiled=True),
        lax.all_gather(shards[2], "shard", axis=0, tiled=True),
        lax.all_gather(shards[3], "shard", axis=0, tiled=True),
        lax.all_gather(shards[4], "shard", axis=0, tiled=True),
        lax.all_gather(shards[5], "shard", axis=0, tiled=True),
        lax.all_gather(shards[6], "shard", axis=0, tiled=True),
        lax.all_gather(shards[7], "shard", axis=0, tiled=True),
        lax.all_gather(shards[8], "shard", axis=0, tiled=True),
        lax.all_gather(shards[9], "shard", axis=0, tiled=True),
        lax.all_gather(shards[10], "shard", axis=0, tiled=True),
        lax.all_gather(shards[11], "shard", axis=0, tiled=True),
        lax.all_gather(shards[12], "shard", axis=0, tiled=True),
        lax.all_gather(shards[13], "shard", axis=0, tiled=True),
    )
    qkv_full, proj_full, up_full, down_full = (gathered[0], gathered[2], gathered[4], gathered[6])
    (
        qv_shift,
        proj_shift,
        up_shift,
        down_shift,
        gain_first,
        shift_first,
        gain_second,
        shift_second,
        scale_first,
        scale_second,
    ) = [gathered[place].astype(jnp.float32) for place in (1, 3, 5, 7, 8, 9, 10, 11, 12, 13)]
    slots, rows, width = tokens.shape
    total_rows = slots * rows
    inputs = tokens.astype(jnp.float32).reshape(total_rows, width)
    present = image_count[lax.axis_index("replica")]
    live_slots = (jnp.arange(slots, dtype=jnp.int32) < present).astype(jnp.float32)
    live_rows = jnp.repeat(live_slots, rows)[:, None]
    normed_low = normalize(inputs, gain_first, shift_first).astype(jnp.bfloat16)
    projected = jnp.dot(normed_low, qkv_full, preferred_element_type=jnp.float32)
    queries = (
        (projected[:, :width] + qv_shift[:width]).astype(jnp.bfloat16).reshape(slots, rows, width)
    )
    keys_local = projected[:, width : 2 * width].astype(jnp.bfloat16).reshape(slots, rows, width)
    values_local = (
        (projected[:, 2 * width :] + qv_shift[width:])
        .astype(jnp.bfloat16)
        .reshape(slots, rows, width)
    )
    keys_all, values_all = (
        lax.all_gather(keys_local, "shard", axis=1, tiled=True),
        lax.all_gather(values_local, "shard", axis=1, tiled=True),
    )
    query_heads = queries.reshape(slots, rows, -1, HEAD_DIM)
    key_heads = keys_all.reshape(slots, -1, width // HEAD_DIM, HEAD_DIM)
    value_heads = values_all.reshape(slots, -1, width // HEAD_DIM, HEAD_DIM)
    attended, logsum = lax.map(attend_forward, (query_heads, key_heads, value_heads))
    attended_low = attended.reshape(total_rows, width).astype(jnp.bfloat16)
    branch = jnp.dot(attended_low, proj_full, preferred_element_type=jnp.float32) + proj_shift
    middle = inputs + scale_first * branch
    second_low = normalize(middle, gain_second, shift_second).astype(jnp.bfloat16)
    hidden_pre = jnp.dot(second_low, up_full, preferred_element_type=jnp.float32) + up_shift
    act_low = gelu_exact(hidden_pre).astype(jnp.bfloat16)
    feed = jnp.dot(act_low, down_full, preferred_element_type=jnp.float32) + down_shift
    result = middle + scale_second * feed
    output = (result * live_rows).astype(jnp.bfloat16).reshape(tokens.shape)
    regathered = (
        lax.all_gather(shards[0], "shard", axis=0, tiled=True),
        lax.all_gather(shards[1], "shard", axis=0, tiled=True),
        lax.all_gather(shards[2], "shard", axis=0, tiled=True),
        lax.all_gather(shards[3], "shard", axis=0, tiled=True),
        lax.all_gather(shards[4], "shard", axis=0, tiled=True),
        lax.all_gather(shards[5], "shard", axis=0, tiled=True),
        lax.all_gather(shards[6], "shard", axis=0, tiled=True),
        lax.all_gather(shards[7], "shard", axis=0, tiled=True),
        lax.all_gather(shards[8], "shard", axis=0, tiled=True),
        lax.all_gather(shards[9], "shard", axis=0, tiled=True),
        lax.all_gather(shards[10], "shard", axis=0, tiled=True),
        lax.all_gather(shards[11], "shard", axis=0, tiled=True),
        lax.all_gather(shards[12], "shard", axis=0, tiled=True),
        lax.all_gather(shards[13], "shard", axis=0, tiled=True),
    )
    qkv_back, proj_back, up_back, down_back = (
        regathered[0],
        regathered[2],
        regathered[4],
        regathered[6],
    )
    grad_result = cotangent.astype(jnp.float32).reshape(total_rows, width) * live_rows
    grad_scale_second = jnp.sum(grad_result * feed, axis=0)
    grad_feed = (grad_result * scale_second).astype(jnp.bfloat16)
    grad_down_shift = column_sum(grad_feed)
    grad_down = inner_rows(act_low, grad_feed)
    grad_act = outer_cols(grad_feed, down_back)
    _, gelu_back = jax.vjp(gelu_exact, hidden_pre)
    grad_pre = gelu_back(grad_act)[0].astype(jnp.bfloat16)
    grad_up_shift = column_sum(grad_pre)
    grad_up = inner_rows(second_low, grad_pre)
    grad_second = outer_cols(grad_pre, up_back)
    _, second_back = jax.vjp(normalize, middle, gain_second, shift_second)
    grad_middle_norm, grad_gain_second, grad_shift_second = second_back(grad_second)
    grad_middle = grad_result + grad_middle_norm
    grad_scale_first = jnp.sum(grad_middle * branch, axis=0)
    grad_branch = (grad_middle * scale_first).astype(jnp.bfloat16)
    grad_proj_shift = column_sum(grad_branch)
    grad_proj = inner_rows(attended_low, grad_branch)
    grad_attended = (
        outer_cols(grad_branch, proj_back).astype(jnp.bfloat16).reshape(slots, rows, width)
    )
    grad_att_heads = grad_attended.reshape(slots, rows, -1, HEAD_DIM)
    grad_queries, grad_keys_part, grad_values_part = lax.map(
        attend_backward, (query_heads, key_heads, value_heads, grad_att_heads, logsum)
    )
    grad_keys, grad_values = (
        lax.psum_scatter(
            grad_keys_part.reshape(slots, -1, width), "shard", scatter_dimension=1, tiled=True
        ),
        lax.psum_scatter(
            grad_values_part.reshape(slots, -1, width), "shard", scatter_dimension=1, tiled=True
        ),
    )
    query_low = grad_queries.reshape(total_rows, width).astype(jnp.bfloat16)
    key_low = grad_keys.reshape(total_rows, width).astype(jnp.bfloat16)
    value_low = grad_values.reshape(total_rows, width).astype(jnp.bfloat16)
    grad_qkv = jnp.concatenate([query_low, key_low, value_low], axis=1)
    grad_qv_shift = jnp.concatenate([column_sum(query_low), column_sum(value_low)])
    grad_qkv_full = inner_rows(normed_low, grad_qkv)
    grad_first = outer_cols(grad_qkv, qkv_back)
    _, first_back = jax.vjp(normalize, inputs, gain_first, shift_first)
    grad_inputs_norm, grad_gain_first, grad_shift_first = first_back(grad_first)
    grad_inputs = grad_middle + grad_inputs_norm
    owned = (
        lax.psum_scatter(grad_qkv_full, "shard", scatter_dimension=0, tiled=True),
        lax.psum_scatter(grad_qv_shift, "shard", scatter_dimension=0, tiled=True),
        lax.psum_scatter(grad_proj, "shard", scatter_dimension=0, tiled=True),
        lax.psum_scatter(grad_proj_shift, "shard", scatter_dimension=0, tiled=True),
        lax.psum_scatter(grad_up, "shard", scatter_dimension=0, tiled=True),
        lax.psum_scatter(grad_up_shift, "shard", scatter_dimension=0, tiled=True),
        lax.psum_scatter(grad_down, "shard", scatter_dimension=0, tiled=True),
        lax.psum_scatter(grad_down_shift, "shard", scatter_dimension=0, tiled=True),
        lax.psum_scatter(grad_gain_first, "shard", scatter_dimension=0, tiled=True),
        lax.psum_scatter(grad_shift_first, "shard", scatter_dimension=0, tiled=True),
        lax.psum_scatter(grad_gain_second, "shard", scatter_dimension=0, tiled=True),
        lax.psum_scatter(grad_shift_second, "shard", scatter_dimension=0, tiled=True),
        lax.psum_scatter(grad_scale_first, "shard", scatter_dimension=0, tiled=True),
        lax.psum_scatter(grad_scale_second, "shard", scatter_dimension=0, tiled=True),
    )
    summed = lax.psum(tuple(owned), "replica")
    return (output, grad_inputs.reshape(tokens.shape)) + tuple(summed)


def solution(mesh):
    in_specs = (
        P("replica", "shard", None),
        P("shard", None),
        P("shard"),
        P("shard", None),
        P("shard"),
        P("shard", None),
        P("shard"),
        P("shard", None),
        P("shard"),
        P("shard"),
        P("shard"),
        P("shard"),
        P("shard"),
        P("shard"),
        P("shard"),
        P("replica", "shard", None),
        P(),
    )
    out_specs = (
        P("replica", "shard", None),
        P("replica", "shard", None),
        P("shard", None),
        P("shard"),
        P("shard", None),
        P("shard"),
        P("shard", None),
        P("shard"),
        P("shard", None),
        P("shard"),
        P("shard"),
        P("shard"),
        P("shard"),
        P("shard"),
        P("shard"),
        P("shard"),
    )
    return jax.shard_map(
        on_device, mesh=mesh, in_specs=in_specs, out_specs=out_specs, check_vma=False
    )
```

profile of v0, /device:TPU:0, one launch (start us, length us, event | category | flops | bytes accessed | tf_op | source)
XLA Modules:
  0.0 1395.3 jit_solution(16869158761444600378)
XLA Ops:
  12.4 6.0 all-gather.2
  18.5 5.3 all-gather.1
  24.9 33.8 %all-gather.16.cloned.1.call-done = bf16[1024,3072]{1,0:T(8,128)(2,1)} async-done(((bf16[256,3072]{1,0:T(8,128)(2,1)}), bf16[1024,3072]{1,0:T(8,128)(2,1)}) %all-gather.16.cloned.1.call-update) | async-done | bytes 6291472 | tf_op jit(solution)/shard_map/all_gather | solution.py:109
  58.7 5.5 fusion.90
  64.2 2.6 copy-done.14
  68.1 5.2 all-gather.3
  73.3 4.5 fusion.63
  81.6 5.1 all-gather.5
  86.7 5.1 all-gather
  92.3 5.1 all-gather.7
  98.0 5.1 all-gather.6
  103.6 5.1 all-gather.4
  109.3 5.4 all_gather.65
  116.5 2.9 reshape.245
  121.2 6.2 copy.66
  127.4 12.0 all-gather.18.cloned.1.call-done
  139.4 6.2 copy.64
  145.7 26.7 %while.26 = (s32[]{:T(128)}, bf16[2,256,16,64]{1,3,2,0:T(8,128)(2,1)S(1)}, f32[2,16,256,1]{2,1,3,0:T(8,128)S(1)}, bf16[2,1024,16,64]{1,3,2,0:T(8,128)(2,1)}, bf1...) while((s32[]{:T(128)}, bf16[2,256,16,64]{1,3,2,0:T(8,128)(2,1)S(1)}, ...), condition=%wide.region_5.6_spmd, body=%wide.region_2.5_spmd.sunk | while | flops 1111486464 | bytes 56232024 | solution.py:161
  145.7 4.2 multiply_reduce_fusion.9
  149.9 3.6 fusion.129
  153.5 5.4 fusion.130
  159.0 4.1 multiply_reduce_fusion.9
  163.0 3.6 fusion.129
  166.7 5.4 fusion.130
  173.8 4.8 fusion.88
  180.4 42.8 %all-gather.24.cloned.1.call-done = bf16[1024,4096]{1,0:T(8,128)(2,1)} async-done(((bf16[256,4096]{1,0:T(8,128)(2,1)}), bf16[1024,4096]{1,0:T(8,128)(2,1)}) %all-gather.24.cloned.1.call-update) | async-done | bytes 8388624 | tf_op jit(solution)/shard_map/all_gather | solution.py:113
  223.2 13.1 fusion.84
  236.3 46.6 %all-gather.26.cloned.1.call-done = bf16[4096,1024]{1,0:T(8,128)(2,1)} async-done(((bf16[1024,1024]{1,0:T(8,128)(2,1)}), bf16[4096,1024]{1,0:T(8,128)(2,1)}) %all-gather.26.cloned.1.call-update) | async-done | bytes 8388624 | tf_op jit(solution)/shard_map/all_gather | solution.py:115
  282.9 29.2 %convert_reduce_fusion = (f32[4096]{0:T(1024)}, bf16[512,4096]{1,0:T(8,128)(2,1)S(1)}, f32[512,4096]{1,0:T(8,128)}) fusion(f32[512,4096]{1,0:T(8,128)} %fusion.84, f32[4096]{0:T(1024)S(1)} %copy-done.27, bf16[512,1024]{1,0:T(8,128)(2,1)} %multiply_convert_fusion.4, bf16[4096,1024]{1,0:T(8,128)(2,1)} %all-gather.26.cloned.1.call-done), kind=kOutput, calls=%fused_computation.56 | convolution fusion | flops 4452249600 | bytes 30441472 | tf_op jit(solution)/shard_map/dot_general | solution.py:29
  312.2 5.5 multiply_reduce_fusion.4
  324.6 2.8 copy.71
  327.5 89.9 %while.27 = (s32[]{:T(128)}, bf16[2,256,16,64]{1,3,2,0:T(8,128)(2,1)S(1)}, f32[2,1024,16,64]{1,3,2,0:T(8,128)}, f32[2,1024,16,64]{1,3,2,0:T(8,128)}, bf16[2,1024...) while((s32[]{:T(128)}, ...), condition=%wide.region_12.13_spmd, body=%wide.region_10.12_spmd.sunk | while | flops 2735992832 | bytes 227660960 | solution.py:215
  327.7 4.0 fusion.139
  331.7 5.7 copy-done
  337.4 4.6 bitcast_dynamic-update-slice_fusion.8
  342.0 12.2 multiply_reduce_fusion.10
  354.2 12.0 multiply_convert_fusion.8
  366.3 2.7 fusion.140
  369.0 3.7 bitcast_dynamic-update-slice_fusion.7
  372.6 4.0 fusion.139
  376.6 5.7 copy-done
  382.3 4.6 bitcast_dynamic-update-slice_fusion.8
  386.9 12.3 multiply_reduce_fusion.10
  399.2 12.0 multiply_convert_fusion.8
  411.3 2.7 fusion.140
  413.9 3.5 bitcast_dynamic-update-slice_fusion.7
  419.1 3.3 fusion.91
  424.3 12.2 fusion.83
  437.2 8.6 multiply_convert_fusion.1
  447.8 8.3 fusion.92
  458.5 30.8 %reduce-scatter.7.cloned.1.call-done = f32[2,256,1024]{1,2,0:T(8,128)} async-done(((f32[2,1024,1024]{1,2,0:T(8,128)}), f32[2,256,1024]{1,2,0:T(8,128)}) %reduce-scatter.7.cloned.1.call-update) | async-done | bytes 2097168 | tf_op jit(solution)/shard_map/reduce_scatter | solution.py:219
  492.9 71.0 %reduce-scatter.9.cloned.1.call-done = f32[2,256,1024]{1,2,0:T(8,128)} async-done(((f32[2,1024,1024]{1,2,0:T(8,128)}), f32[2,256,1024]{1,2,0:T(8,128)}) %reduce-scatter.9.cloned.1.call-update) | async-done | bytes 2097168 | tf_op jit(solution)/shard_map/reduce_scatter | solution.py:222
  566.8 11.3 fusion.76
  578.2 33.4 %reduce-scatter.13.cloned.1.call-done = f32[256,1024]{1,0:T(8,128)} async-done(((f32[1024,1024]{1,0:T(8,128)}), f32[256,1024]{1,0:T(8,128)}) %reduce-scatter.13.cloned.1.call-update) | async-done | bytes 1048592 | tf_op jit(solution)/shard_map/reduce_scatter | solution.py:239
  611.6 128.8 %reduce-scatter.15.cloned.1.call-done = f32[256,4096]{1,0:T(8,128)} async-done(((f32[1024,4096]{1,0:T(8,128)}), f32[256,4096]{1,0:T(8,128)}) %reduce-scatter.15.cloned.1.call-update) | async-done | bytes 4194320 | tf_op jit(solution)/shard_map/reduce_scatter | solution.py:241
  740.4 128.8 %reduce-scatter.17.cloned.1.call-done = f32[1024,1024]{1,0:T(8,128)} async-done(((f32[4096,1024]{1,0:T(8,128)}), f32[1024,1024]{1,0:T(8,128)}) %reduce-scatter.17.cloned.1.call-update) | async-done | bytes 4194320 | tf_op jit(solution)/shard_map/reduce_scatter | solution.py:243
  869.2 101.7 %reduce-scatter.11.cloned.1.call-done = f32[256,3072]{1,0:T(8,128)} async-done(((f32[1024,3072]{1,0:T(8,128)}), f32[256,3072]{1,0:T(8,128)}) %reduce-scatter.11.cloned.1.call-update) | async-done | bytes 3145744 | tf_op jit(solution)/shard_map/reduce_scatter | solution.py:237
  974.1 5.1 all-gather.8
  980.0 8.7 fusion.85
  989.8 10.7 multiply_reduce_fusion.2
  1000.5 11.7 all-reduce.12
  1012.9 39.6 %all-reduce.10 = (f32[512]{0:T(512)}, f32[256]{0:T(256)}, f32[1024]{0:T(1024)}, f32[256]{0:T(256)}, f32[256]{0:T(256)}, /*index=5*/f32[256]{0:T(256)}, f32[256]{...) all-reduce(f32[512]{0:T(512)S(1)} %dynamic-slice.1, ...), channel_id=1, replica_groups=mesh['replica'=8,'shard'=4] {'replica'}, use_global_device_ids=true, to_apply=%region_22.23 | all-reduce | flops 3584 | bytes 28672 | tf_op jit(solution)/shard_map/psum | solution.py:252
  1052.5 325.0 %all-reduce.15.cloned.1.call-done = (f32[256,3072]{1,0:T(8,128)}, f32[256,1024]{1,0:T(8,128)}, f32[256,4096]{1,0:T(8,128)}, f32[1024,1024]{1,0:T(8,128)}) async-done(((f32[256,3072]{1,0:T(8,128)}, f32[256,1024]{1,0:T(8,128)}, f32[256,4096]{1,0:T(8,128)}, f32[1024,1024]{1,0:T(8,128)}), (f32[256,3072]{1,0:T(8,128)}, f32[256,1024]{1,0:T(8,128)}, f32[256,4096]{1,0:T(8,128)}, ...) | async-done | bytes 12582928 | tf_op jit(solution)/shard_map/psum | solution.py:252
  1377.6 4.0 copy.118
  (262 shorter events, 52.7 us)
Async XLA Ops:
  7.2 17.2 %copy-start.2 = (bf16[2,256,1024]{2,1,0:T(8,128)(2,1)S(1)}, bf16[2,256,1024]{2,1,0:T(8,128)(2,1)}, u32[]{:S(2)}) copy-start(bf16[2,256,1024]{2,1,0:T(8,128)(2,1)} %param.21) | copy-start | bytes 3145732
  7.2 51.5 %all-gather.16.cloned.1.call-start = ((), (), s32[]{:S(2)}) async-start(), calls=%async_computation.6 | async-start | bytes 7864320 | tf_op jit(solution)/shard_map/all_gather | solution.py:109
  7.9 113.3 %all-gather.20.cloned.1.call-start = ((), (), s32[]{:S(2)}) async-start(), calls=%async_computation.8 | async-start | bytes 5242880 | tf_op jit(solution)/shard_map/all_gather | solution.py:155
  10.7 13.1 copy-start.38
  12.4 11.4 copy-start.36
  12.4 11.4 copy-start.40
  24.9 39.4 %copy-start.22 = (bf16[512,1024]{1,0:T(8,128)(2,1)}, bf16[512,1024]{1,0:T(8,128)(2,1)S(1)}, u32[]{:S(2)}) copy-start(bf16[512,1024]{1,0:T(8,128)(2,1)S(1)} %fusion.71) | copy-start | bytes 3145732
  24.9 43.2 %copy-start.62 = (bf16[512]{0:T(512)(128)(2,1)S(1)}, bf16[512]{0:T(512)(128)(2,1)}, u32[]{:S(2)}) copy-start(bf16[512]{0:T(512)(128)(2,1)} %param.23) | copy-start | bytes 3076
  64.2 2.6 copy-start.14
  68.0 71.4 %all-gather.18.cloned.1.call-start = ((), (), s32[]{:S(2)}) async-start(), calls=%async_computation.7 | async-start | bytes 5242880 | tf_op jit(solution)/shard_map/all_gather | solution.py:156
  77.9 31.4 %copy-start.61 = (bf16[1024]{0:T(1024)(128)(2,1)S(1)}, bf16[1024]{0:T(1024)(128)(2,1)}, u32[]{:S(2)}) copy-start(bf16[1024]{0:T(1024)(128)(2,1)} %param.27) | copy-start | bytes 6148
  77.9 37.4 %copy-start.5 = (bf16[2,256,1024]{2,1,0:T(8,128)(2,1)S(1)}, bf16[2,256,1024]{2,1,0:T(8,128)(2,1)}, u32[]{:S(2)}) copy-start(bf16[2,256,1024]{2,1,0:T(8,128)(2,1)} %param.36) | copy-start | bytes 3145732
  77.9 95.9 %all-gather.22.cloned.1.call-start = ((), (), s32[]{:S(2)}) async-start(), calls=%async_computation.9 | async-start | bytes 2621440 | tf_op jit(solution)/shard_map/all_gather | solution.py:111
  78.5 144.7 %all-gather.24.cloned.1.call-start = ((), (), s32[]{:S(2)}) async-start(), calls=%async_computation.10 | async-start | bytes 10485760 | tf_op jit(solution)/shard_map/all_gather | solution.py:113
  79.1 203.8 %all-gather.26.cloned.1.call-start = ((), (), s32[]{:S(2)}) async-start(), calls=%async_computation.11 | async-start | bytes 10485760 | tf_op jit(solution)/shard_map/all_gather | solution.py:115
  79.6 409.7 %reduce-scatter.7.cloned.1.call-start = ((), (), s32[]{:S(2)}) async-start(), calls=%async_computation.12 | async-start | bytes 10485760 | tf_op jit(solution)/shard_map/reduce_scatter | solution.py:219
  81.6 34.9 %copy-start.33 = (f32[1,2,2,128]{3,1,2,0:T(2,128)}, f32[1,2,2,128]{3,1,2,0:T(2,128)S(1)}, u32[]{:S(2)}) copy-start(f32[1,2,2,128]{3,1,2,0:T(2,128)S(1)} %copy.84) | copy-start | bytes 6148
  86.7 29.9 %copy-start.31 = (f32[4,1,256]{2,1,0:T(1,128)}, f32[4,1,256]{2,1,0:T(1,128)S(1)}, u32[]{:S(2)}) copy-start(f32[4,1,256]{2,1,0:T(1,128)S(1)} %convert_element_type.168) | copy-start | bytes 12292
  173.7 4.9 copy-start.24
  173.8 49.3 %copy-start.47 = (f32[4,1,256]{2,1,0:T(1,128)S(1)}, f32[4,1,256]{2,1,0:T(1,128)}, u32[]{:S(2)}) copy-start(f32[4,1,256]{2,1,0:T(1,128)} %convert_element_type.169) | copy-start | bytes 12292
  173.8 49.3 %copy-start.57 = (f32[4,1,256]{2,1,0:T(1,128)S(1)}, f32[4,1,256]{2,1,0:T(1,128)}, u32[]{:S(2)}) copy-start(f32[4,1,256]{2,1,0:T(1,128)} %convert_element_type.170) | copy-start | bytes 12292
  178.7 139.0 %copy-start.42 = (f32[512]{0:T(512)}, f32[512]{0:T(512)S(1)}, u32[]{:S(2)}) copy-start(f32[512]{0:T(512)S(1)} %broadcast_multiply_fusion) | copy-start | bytes 6148
  180.3 137.3 %copy-start.51 = (f32[512]{0:T(512)}, f32[512]{0:T(512)S(1)}, u32[]{:S(2)}) copy-start(f32[512]{0:T(512)S(1)} %fusion.78) | copy-start | bytes 6148
  223.2 59.7 %copy-start.27 = (f32[4096]{0:T(1024)S(1)}, f32[4096]{0:T(1024)}, u32[]{:S(2)}) copy-start(f32[4096]{0:T(1024)} %convert_element_type.141) | copy-start | bytes 49156
  236.3 75.9 %copy-start.11 = (f32[512,1024]{1,0:T(8,128)S(1)}, f32[512,1024]{1,0:T(8,128)}, u32[]{:S(2)}) copy-start(f32[512,1024]{1,0:T(8,128)} %copy-done.10) | copy-start | bytes 6291460
  282.9 29.3 %copy-start.63 = (bf16[1024,4096]{1,0:T(8,128)(2,1)S(1)}, bf16[1024,4096]{1,0:T(8,128)(2,1)}, u32[]{:S(2)}) copy-start(bf16[1024,4096]{1,0:T(8,128)(2,1)} %all-gather.24.cloned.1.call-done) | copy-start | bytes 25165828
  312.2 5.5 copy-start.74
  317.7 3.3 copy-start.64
  318.4 3.8 copy-start.49
  331.7 5.7 copy-start
  354.2 12.1 copy-start.1
  376.6 5.7 copy-start
  399.2 12.1 copy-start.1
  417.5 146.4 %reduce-scatter.9.cloned.1.call-start = ((), (), s32[]{:S(2)}) async-start(), calls=%async_computation.13 | async-start | bytes 10485760 | tf_op jit(solution)/shard_map/reduce_scatter | solution.py:222
  418.2 193.3 %reduce-scatter.13.cloned.1.call-start = ((), (), s32[]{:S(2)}) async-start(), calls=%async_computation.15 | async-start | bytes 5242880 | tf_op jit(solution)/shard_map/reduce_scatter | solution.py:239
  422.4 318.0 %reduce-scatter.15.cloned.1.call-start = ((), (), s32[]{:S(2)}) async-start(), calls=%async_computation.16 | async-start | bytes 20971520 | tf_op jit(solution)/shard_map/reduce_scatter | solution.py:241
  436.5 432.6 %reduce-scatter.17.cloned.1.call-start = ((), (), s32[]{:S(2)}) async-start(), calls=%async_computation.17 | async-start | bytes 20971520 | tf_op jit(solution)/shard_map/reduce_scatter | solution.py:243
  437.2 10.6 copy-start.21
  456.2 514.7 %reduce-scatter.11.cloned.1.call-start = ((), (), s32[]{:S(2)}) async-start(), calls=%async_computation.14 | async-start | bytes 15728640 | tf_op jit(solution)/shard_map/reduce_scatter | solution.py:237
  566.8 11.3 copy-start.26
  578.2 799.4 %all-reduce.15.cloned.1.call-start = ((), (), s32[]{:S(2)}) async-start(), calls=%async_computation.18 | async-start | bytes 25165824 | tf_op jit(solution)/shard_map/psum | solution.py:252
  970.9 3.2 copy-start.71
  970.9 8.3 copy-start.7
  970.9 8.3 copy-start.32
  970.9 8.3 copy-start.60
  970.9 9.0 copy-start.4
  970.9 9.0 copy-start.30
  970.9 9.0 copy-start.39
  979.9 8.8 copy-start.37
  979.9 8.8 copy-start.41
  979.9 9.8 copy-start.9
  979.9 9.8 copy-start.13
  979.9 9.8 copy-start.18
  979.9 9.8 copy-start.35
  979.9 9.8 copy-start.50
  979.9 9.8 copy-start.56
  980.0 9.8 copy-start.73
  989.8 10.7 copy-start.44
  989.8 10.7 copy-start.46
  989.8 10.7 copy-start.53
  989.8 10.7 copy-start.54
  1377.5 4.0 copy-start.23
  1377.5 5.0 copy-start.16
  1382.6 3.7 copy-start.15
  (26 other events, 39.6 us)
Sparse Core Ops, SparseCore 0:
  9.6 49.0 all-gather.15
  68.1 34.5 all-gather.19
  104.9 34.4 all-gather.17
  140.8 22.5 all-gather.21
  164.8 58.2 all-gather.23
  224.6 58.2 all-gather.25
  417.6 71.7 reduce-scatter.6
  492.1 71.7 reduce-scatter.8
  567.0 44.5 reduce-scatter.12
  614.2 126.1 reduce-scatter.14
  742.9 126.1 reduce-scatter.16
  871.8 99.0 reduce-scatter.10
  976.3 401.1 all-reduce.14
where the time goes:
time: 1400 us
  waiting for transfers between devices  958 us (68%)
  matrix products  187 us (13%)
  blocking collectives  104 us (7%)
  local copies, waits for them, and re-layouts  68.1 us (5%)
  other arithmetic  60.3 us (4%)
  between operations  17.3 us (1%)
    psum x1, waiting for transfers between devices, on_device(): summed = lax.psum(tuple(owned), 'replica')  325 us
    reduce_scatter x1, waiting for transfers between devices, on_device(): lax.psum_scatter(grad_up, 'shard', scatter_dimension=0, tiled=True)  129 us
    reduce_scatter x1, waiting for transfers between devices, on_device(): lax.psum_scatter(grad_down, 'shard', scatter_dimension=0, tiled=True)  129 us
    reduce_scatter x1, waiting for transfers between devices, on_device(): lax.psum_scatter(grad_qkv_full, 'shard', scatter_dimension=0, tiled=True)  102 us
    reduce_scatter x1, waiting for transfers between devices, on_device(): lax.psum_scatter(grad_values_part.reshape(slots, -1, width), 'shard', sca...  71 us
    all_gather x1, waiting for transfers between devices, on_device(): lax.all_gather(shards[6], 'shard', axis=0, tiled=True)  46.6 us
    dot_general x4, matrix products, outer_cols(): lax.dot_general(left, right, (((1,), (1,)), ((), ())), preferred_element_...  44.7 us
    all_gather x1, waiting for transfers between devices, on_device(): lax.all_gather(shards[4], 'shard', axis=0, tiled=True)  42.8 us
  transfers between devices with their start and end apart: 13, of which 11 were waited for; matrix products, arithmetic and copies ran while one was open for 11% of the time, Pallas kernels for 0%

commit v1 on v0

v1 whole, which is shorter than its diff:
```python
import functools

import jax
import jax.numpy as jnp
from jax import lax
from jax.experimental import pallas as pl
from jax.experimental.pallas import tpu as pltpu
from jax.sharding import PartitionSpec as P

HEAD_DIM = 64
EPS = 1e-06
BF = jnp.bfloat16
F32 = jnp.float32
MESH = pl.DeviceIdType.MESH
MIB = 1024 * 1024
SLOTS = 4


def matmul(left, right, dims=((1,), (0,))):
    return lax.dot_general(left, right, (dims, ((), ())), preferred_element_type=F32)


def column_sum(values):
    return jnp.sum(values.astype(F32), axis=0)


def attend_forward(q_ref, k_ref, v_ref, out_ref, lse_ref):
    lane = lax.broadcasted_iota(jnp.int32, (1, 128), 1)
    query, key, value = q_ref[...], k_ref[...], v_ref[...]
    value_t = value.T
    parts = []
    for head in range(2):
        mine = (lane < HEAD_DIM) if head == 0 else (lane >= HEAD_DIM)
        own = jnp.where(mine, query * BF(HEAD_DIM**-0.5), BF(0))
        scores = matmul(key, own, ((1,), (1,)))
        highest = jnp.max(scores, axis=0, keepdims=True)
        expos = jnp.exp(scores - highest)
        denom = jnp.sum(expos, axis=0, keepdims=True)
        probs = (expos * (1.0 / denom)).astype(BF)
        lse_ref[0, head : head + 1, :] = highest + jnp.log(denom)
        rows = slice(head * HEAD_DIM, (head + 1) * HEAD_DIM)
        parts.append(matmul(value_t[rows, :], probs))
    out_ref[...] = jnp.concatenate(parts, axis=0).T.astype(BF)


def attend_backward(q_ref, k_ref, v_ref, g_ref, lse_ref, gq_ref, gk_ref, gv_ref):
    lane = lax.broadcasted_iota(jnp.int32, (1, 128), 1)
    query, key, value, grad = q_ref[...], k_ref[...], v_ref[...], g_ref[...]
    key_t = key.T
    parts = []
    for head in range(2):
        mine = (lane < HEAD_DIM) if head == 0 else (lane >= HEAD_DIM)
        own = jnp.where(mine, query * BF(HEAD_DIM**-0.5), BF(0))
        own_grad = jnp.where(mine, grad, BF(0))
        scores = matmul(key, own, ((1,), (1,)))
        probs = jnp.exp(scores - lse_ref[0, head : head + 1, :])
        grad_probs = matmul(value, own_grad, ((1,), (1,)))
        centre = jnp.sum(grad_probs * probs, axis=0, keepdims=True)
        grad_scores = (probs * (grad_probs - centre)).astype(BF)
        gv = matmul(probs.astype(BF), own_grad)
        gk = matmul(grad_scores, own)
        if head == 0:
            gv_ref[...], gk_ref[...] = gv, gk
        else:
            gv_ref[...] += gv
            gk_ref[...] += gk
        rows = slice(head * HEAD_DIM, (head + 1) * HEAD_DIM)
        parts.append(matmul(key_t[rows, :], grad_scores))
    whole = jnp.concatenate(parts, axis=0) * (HEAD_DIM**-0.5)
    gq_ref[...] = whole.T.astype(BF)


def attention_forward(query, key, value):
    rows, width = query.shape
    keys = key.shape[0]
    pairs = width // 128
    part = lambda n: pl.BlockSpec((n, 128), lambda i: (0, i))
    return pl.pallas_call(
        attend_forward,
        grid=(pairs,),
        in_specs=[part(rows), part(keys), part(keys)],
        out_specs=[part(rows), pl.BlockSpec((1, 2, rows), lambda i: (i, 0, 0))],
        out_shape=[
            jax.ShapeDtypeStruct((rows, width), BF),
            jax.ShapeDtypeStruct((pairs, 2, rows), F32),
        ],
        compiler_params=pltpu.CompilerParams(vmem_limit_bytes=48 * MIB),
    )(query, key, value)


def attention_backward(query, key, value, grad, lse):
    rows, width = query.shape
    keys = key.shape[0]
    pairs = width // 128
    part = lambda n: pl.BlockSpec((n, 128), lambda i: (0, i))
    return pl.pallas_call(
        attend_backward,
        grid=(pairs,),
        in_specs=[
            part(rows),
            part(keys),
            part(keys),
            part(rows),
            pl.BlockSpec((1, 2, rows), lambda i: (i, 0, 0)),
        ],
        out_specs=[part(rows), part(keys), part(keys)],
        out_shape=[
            jax.ShapeDtypeStruct((rows, width), BF),
            jax.ShapeDtypeStruct((keys, width), F32),
            jax.ShapeDtypeStruct((keys, width), F32),
        ],
        compiler_params=pltpu.CompilerParams(vmem_limit_bytes=48 * MIB),
    )(query, key, value, grad, lse)


class Place:
    def __init__(self, replicas, shards):
        self.Z, self.Y = replicas // 2, shards // 2
        self.shards = shards
        replica, shard = lax.axis_index("replica"), lax.axis_index("shard")
        self.x, self.z = lax.rem(replica, 2), lax.div(replica, 2)
        self.c, self.y = lax.rem(shard, 2), lax.div(shard, 2)
        self.s = shard

    def part(self, y, c):
        return y * 2 + c

    def at(self, x=None, z=None, y=None, c=None):
        x = self.x if x is None else x
        z = self.z if z is None else z
        y = self.y if y is None else y
        c = self.c if c is None else c
        return (z * 2 + x, y * 2 + c)

    def ahead_z(self, k):
        return lax.rem(self.z + k, self.Z)

    def behind_z(self, k):
        return lax.rem(self.z + self.Z - k, self.Z)

    def ahead_y(self, k):
        return lax.rem(self.y + k, self.Y)

    def behind_y(self, k):
        return lax.rem(self.y + self.Y - k, self.Y)

    def greet(self, extra=()):
        others = [self.at(c=1 - self.c), self.at(x=1 - self.x)]
        others += [self.at(y=self.ahead_y(k)) for k in range(1, self.Y)]
        others += [self.at(z=self.ahead_z(k)) for k in range(1, self.Z)]
        others += list(extra)
        barrier = pltpu.get_barrier_semaphore()
        for other in others:
            pl.semaphore_signal(barrier, inc=1, device_id=other, device_id_type=MESH)
        pl.semaphore_wait(barrier, len(others))


def send(src, dst, send_sem, recv_sem, device):
    return pltpu.make_async_remote_copy(
        src_ref=src,
        dst_ref=dst,
        send_sem=send_sem,
        recv_sem=recv_sem,
        device_id=device,
        device_id_type=MESH,
    )


def gather_kernel(replicas, shards, count, *refs):
    ins, outs = refs[: count + 1], refs[count + 1 : 2 * count + 2]
    (local, small_s, small_r, ys, yr, zs, zr, xs, xr, cs, cr, os, orr) = refs[2 * count + 2 :]
    place = Place(replicas, shards)
    Y, Z = place.Y, place.Z
    s = place.s
    diagonal = [
        place.at(y=place.ahead_y(k), c=1 - place.c) for k in range(1, Y)
    ]
    place.greet(diagonal)

    keep = [pltpu.make_async_copy(ins[w], outs[w].at[s], local.at[w]) for w in range(count + 1)]
    for copy in keep:
        copy.start()
    small = []
    for k in range(1, shards):
        peer = lax.rem(s + k, shards)
        small.append(
            send(ins[count], outs[count].at[s], small_s.at[k - 1], small_r.at[k - 1],
                 (lax.axis_index("replica"), peer))
        )
        small[-1].start()

    def piece(w, z):
        rows, cols = ins[w].shape
        half, step = rows // 2, cols // Z
        return (pl.ds(pl.multiple_of(place.x * half, half), half),
                pl.ds(pl.multiple_of(z * step, 128), step))

    def y_copy(w, k):
        rows, cols = piece(w, place.z)
        return send(ins[w].at[rows, cols], outs[w].at[s, rows, cols], ys.at[w, k - 1], yr.at[w, k - 1],
                    place.at(y=place.ahead_y(k)))

    def z_copy(w, k, j):
        owner = place.part(place.behind_y(k), place.c)
        rows, cols = piece(w, place.z)
        block = outs[w].at[owner, rows, cols]
        return send(block, block, zs.at[w, k - 1, j - 1], zr.at[w, k - 1, j - 1],
                    place.at(z=place.ahead_z(j)))

    def x_copy(w, k):
        owner = place.part(place.behind_y(k), place.c)
        half = ins[w].shape[0] // 2
        block = outs[w].at[owner, pl.ds(pl.multiple_of(place.x * half, half), half)]
        return send(block, block, xs.at[w, k - 1], xr.at[w, k - 1], place.at(x=1 - place.x))

    def c_copy(w, k):
        owner = place.part(place.behind_y(k), place.c)
        block = outs[w].at[owner]
        return send(block, block, cs.at[w, k - 1], cr.at[w, k - 1], place.at(c=1 - place.c))

    def own_copy(w):
        return send(ins[w], outs[w].at[s], os.at[w], orr.at[w], place.at(c=1 - place.c))

    for w in range(count):
        for k in range(1, Y):
            y_copy(w, k).start()
    for w in range(count):
        own_copy(w).start()
    for t in range(count + 3):
        if t < count:
            for k in range(1, Y):
                y_copy(t, k).wait()
                for j in range(1, Z):
                    z_copy(t, k, j).start()
        if 0 <= t - 1 < count:
            for k in range(1, Y):
                for j in range(1, Z):
                    z_copy(t - 1, k, j).wait()
                x_copy(t - 1, k).start()
        if 0 <= t - 2 < count:
            for k in range(1, Y):
                x_copy(t - 2, k).wait()
                c_copy(t - 2, k).start()
        if 0 <= t - 3 < count:
            for k in range(1, Y):
                c_copy(t - 3, k).wait()
            own_copy(t - 3).wait()
    for copy in small + keep:
        copy.wait()


def gather_weights(replicas, shards, weights, small):
    count = len(weights)
    Y, Z = shards // 2, replicas // 2
    dma = pltpu.SemaphoreType.DMA
    arrays = list(weights) + [small]
    any_spec = pl.BlockSpec(memory_space=pl.ANY)
    return pl.pallas_call(
        functools.partial(gather_kernel, replicas, shards, count),
        in_specs=[any_spec] * (count + 1),
        out_specs=[any_spec] * (count + 1),
        out_shape=[jax.ShapeDtypeStruct((shards,) + a.shape, a.dtype) for a in arrays],
        scratch_shapes=[
            dma((count + 1,)),
            dma((shards - 1,)), dma((shards - 1,)),
            dma((count, Y - 1)), dma((count, Y - 1)),
            dma((count, Y - 1, Z - 1)), dma((count, Y - 1, Z - 1)),
            dma((count, Y - 1)), dma((count, Y - 1)),
            dma((count, Y - 1)), dma((count, Y - 1)),
            dma((count,)), dma((count,)),
        ],
        compiler_params=pltpu.CompilerParams(collective_id=0, has_side_effects=True),
    )(*arrays)


def reduce_kernel(replicas, shards, plan, *refs):
    n_ops = 2 * len(plan)
    ops, small_ref = refs[:n_ops], refs[n_ops]
    out, small_out = refs[n_ops + 1 : n_ops + 3]
    (part, crecv, ysum, yrecv, xsum, xrecv, zsum, zrecv, small_buf, tile,
     cs, cr, ys, yr, xs, xr, zs, zr, gs, gr, hs, hr, ss, sr) = refs[n_ops + 3 :]
    place = Place(replicas, shards)
    Y, Z = place.Y, place.Z
    CB = part.shape[3]
    W = part.shape[4]
    total = sum(item[2] for item in plan)
    place.greet()

    def core_copy(i):
        a = lax.rem(i, SLOTS)
        return send(part.at[lax.rem(i, 2), 1 - place.c], crecv.at[a], cs.at[a], cr.at[a],
                    place.at(c=1 - place.c))

    def y_copy(i, k):
        a = lax.rem(i, SLOTS)
        return send(ysum.at[a, place.ahead_y(k)], yrecv.at[a, k - 1], ys.at[a, k - 1], yr.at[a, k - 1],
                    place.at(y=place.ahead_y(k)))

    def x_copy(i):
        a = lax.rem(i, SLOTS)
        return send(xsum.at[a, 1 - place.x], xrecv.at[a], xs.at[a], xr.at[a], place.at(x=1 - place.x))

    def z_copy(i, k):
        a = lax.rem(i, SLOTS)
        return send(zsum.at[a, place.ahead_z(k)], zrecv.at[a, k - 1], zs.at[a, k - 1], zr.at[a, k - 1],
                    place.at(z=place.ahead_z(k)))

    def zg_copy(i, k):
        a = lax.rem(i, SLOTS)
        block = out.at[i, place.x, place.z]
        return send(block, block, gs.at[a, k - 1], gr.at[a, k - 1], place.at(z=place.ahead_z(k)))

    def xg_copy(i):
        a = lax.rem(i, SLOTS)
        block = out.at[i, place.x]
        return send(block, block, hs.at[a], hr.at[a], place.at(x=1 - place.x))

    def add(*terms):
        whole = terms[0].astype(F32)
        for term in terms[1:]:
            whole = whole + term.astype(F32)
        return whole.astype(BF)

    def product(left, first, cols):
        if CB % 128 == 0:
            return matmul(left[:, pl.ds(first, CB)], cols, ((0,), (0,))).astype(BF)
        start = pl.multiple_of(lax.div(first, 128) * 128, 128)
        tile[...] = matmul(left[:, pl.ds(start, 128)], cols, ((0,), (0,)))
        return tile[pl.ds(pl.multiple_of(first - start, CB), CB)].astype(BF)

    def tick(i):
        def stage(lag):
            j = i - lag
            return j, (j >= 0) & (j < total)

        j1, ok1 = stage(1)

        @pl.when(ok1)
        def _():
            core_copy(j1).wait()
            a = lax.rem(j1, SLOTS)
            for y in range(Y):
                ysum[a, y] = add(part[lax.rem(j1, 2), place.c, y], crecv[a, y])
            for k in range(1, Y):
                y_copy(j1, k).start()

        j2, ok2 = stage(2)

        @pl.when(ok2)
        def _():
            a = lax.rem(j2, SLOTS)
            for k in range(1, Y):
                y_copy(j2, k).wait()
            for h in range(2):
                rows = slice(h * CB // 2, (h + 1) * CB // 2)
                xsum[a, h] = add(ysum[a, place.y, rows], *[yrecv[a, k - 1, rows] for k in range(1, Y)])
            x_copy(j2).start()

        j3, ok3 = stage(3)

        @pl.when(ok3)
        def _():
            a = lax.rem(j3, SLOTS)
            x_copy(j3).wait()
            for z in range(Z):
                cols = slice(z * W // Z, (z + 1) * W // Z)
                zsum[a, z] = add(xsum[a, place.x, :, cols], xrecv[a, :, cols])
            for k in range(1, Z):
                z_copy(j3, k).start()

        j4, ok4 = stage(4)

        @pl.when(ok4)
        def _():
            a = lax.rem(j4, SLOTS)
            for k in range(1, Z):
                z_copy(j4, k).wait()
            out[j4, place.x, place.z] = add(zsum[a, place.z], *[zrecv[a, k - 1] for k in range(1, Z)])
            for k in range(1, Z):
                zg_copy(j4, k).start()

        j5, ok5 = stage(5)

        @pl.when(ok5)
        def _():
            for k in range(1, Z):
                zg_copy(j5, k).wait()
            xg_copy(j5).start()

        j6, ok6 = stage(6)

        @pl.when(ok6)
        def _():
            xg_copy(j6).wait()

    def small_send(step, devices):
        copies = []
        for k, device in enumerate(devices):
            copies.append(send(small_buf.at[step, 0], small_buf.at[step, k + 1],
                               ss.at[step, k], sr.at[step, k], device))
        return copies

    small_steps = [
        [place.at(c=1 - place.c)],
        [place.at(y=place.ahead_y(k)) for k in range(1, Y)],
        [place.at(x=1 - place.x)],
        [place.at(z=place.ahead_z(k)) for k in range(1, Z)],
    ]
    small_buf[0, 0] = small_ref[...]
    for copy in small_send(0, small_steps[0]):
        copy.start()

    base = 0
    for number, (rows, n_cols, chunks) in enumerate(plan):
        left, right = ops[2 * number], ops[2 * number + 1]
        blocks = rows // CB

        def body(i, _, base=base, rows=rows, left=left, right=right, blocks=blocks):
            local = i - base
            b, n = lax.rem(local, blocks), lax.div(local, blocks)
            slot = lax.rem(i, 2)
            cols = right[:, pl.ds(pl.multiple_of(n * W, 128), W)]
            for turn in range(2):
                c = 1 - place.c if turn == 0 else place.c
                for y in range(Y):
                    first = pl.multiple_of(place.part(y, c) * rows + b * CB, CB)
                    part[slot, c, y] = product(left, first, cols)
                if turn == 0:
                    core_copy(i).start()
            tick(i)
            return 0

        lax.fori_loop(base, base + chunks, body, 0)
        base += chunks
        for copy in small_send(number, small_steps[number]):
            copy.wait()
        whole = small_buf[number, 0]
        for k in range(len(small_steps[number])):
            whole = whole + small_buf[number, k + 1]
        if number < 3:
            small_buf[number + 1, 0] = whole
            for copy in small_send(number + 1, small_steps[number + 1]):
                copy.start()
        else:
            small_out[...] = whole

    def drain(i, _):
        tick(i)
        return 0

    lax.fori_loop(total, total + 6, drain, 0)


def reduce_gradients(replicas, shards, pairs, small):
    Y, Z = shards // 2, replicas // 2
    dma = pltpu.SemaphoreType.DMA
    W = 1024
    CB = min(128, 1024 // shards)
    plan, flat = [], []
    for left, right in pairs:
        rows, n_cols = left.shape[1] // shards, right.shape[1] // W
        plan.append((rows, n_cols, (rows // CB) * n_cols))
        flat += [left, right]
    total = sum(item[2] for item in plan)
    vmem = pl.BlockSpec(memory_space=pltpu.VMEM)
    peers = max(Y, Z, 2)
    out, small_out = pl.pallas_call(
        functools.partial(reduce_kernel, replicas, shards, tuple(plan)),
        in_specs=[vmem] * (len(flat) + 1),
        out_specs=[vmem, vmem],
        out_shape=[
            jax.ShapeDtypeStruct((total, 2, Z, CB // 2, W // Z), BF),
            jax.ShapeDtypeStruct(small.shape, F32),
        ],
        scratch_shapes=[
            pltpu.VMEM((2, 2, Y, CB, W), BF),
            pltpu.VMEM((SLOTS, Y, CB, W), BF),
            pltpu.VMEM((SLOTS, Y, CB, W), BF),
            pltpu.VMEM((SLOTS, Y - 1, CB, W), BF),
            pltpu.VMEM((SLOTS, 2, CB // 2, W), BF),
            pltpu.VMEM((SLOTS, CB // 2, W), BF),
            pltpu.VMEM((SLOTS, Z, CB // 2, W // Z), BF),
            pltpu.VMEM((SLOTS, Z - 1, CB // 2, W // Z), BF),
            pltpu.VMEM((4, peers) + small.shape, F32),
            pltpu.VMEM((128, W), F32),
            dma((SLOTS,)), dma((SLOTS,)),
            dma((SLOTS, Y - 1)), dma((SLOTS, Y - 1)),
            dma((SLOTS,)), dma((SLOTS,)),
            dma((SLOTS, Z - 1)), dma((SLOTS, Z - 1)),
            dma((SLOTS, Z - 1)), dma((SLOTS, Z - 1)),
            dma((SLOTS,)), dma((SLOTS,)),
            dma((4, peers - 1)), dma((4, peers - 1)),
        ],
        compiler_params=pltpu.CompilerParams(
            collective_id=1, has_side_effects=True, vmem_limit_bytes=60 * MIB
        ),
    )(*flat, small)
    grads, base = [], 0
    for rows, n_cols, chunks in plan:
        block = out[base : base + chunks].reshape(n_cols, rows // CB, 2, Z, CB // 2, W // Z)
        block = block.transpose(1, 2, 4, 0, 3, 5).reshape(rows, n_cols * W)
        grads.append(block.astype(F32))
        base += chunks
    return grads, small_out


def norm_parts(values):
    centre = values - jnp.mean(values, axis=-1, keepdims=True)
    scale = lax.rsqrt(jnp.mean(centre * centre, axis=-1, keepdims=True) + EPS)
    return centre * scale, scale


def norm_back(grad, unit, scale, gain):
    inner = grad * gain
    return scale * (
        inner
        - jnp.mean(inner, axis=-1, keepdims=True)
        - unit * jnp.mean(inner * unit, axis=-1, keepdims=True)
    )


def on_device(replicas, shards, tokens, qkv_weight, qv_bias, proj_weight, proj_bias, up_weight, up_bias,
              down_weight, down_bias, attn_gain, attn_shift, mlp_gain, mlp_shift, attn_scale, mlp_scale,
              cotangent, image_count):
    vectors = (qv_bias, proj_bias, up_bias, down_bias, attn_gain, attn_shift, mlp_gain, mlp_shift,
               attn_scale, mlp_scale)
    lengths = [v.shape[0] for v in vectors]
    n_small = sum(lengths)
    padded = -(-n_small // 2048) * 2048
    packed = jnp.pad(jnp.concatenate(vectors), (0, padded - n_small)).reshape(16, padded // 16)
    qkv_all, proj_all, up_all, down_all, small_all = gather_weights(
        replicas, shards, (qkv_weight, proj_weight, up_weight, down_weight), packed
    )
    width = tokens.shape[2]
    qkv_full, proj_full = qkv_all.reshape(width, -1), proj_all.reshape(width, -1)
    up_full, down_full = up_all.reshape(width, -1), down_all.reshape(-1, width)
    small_flat = small_all.reshape(shards, padded)
    full, place = [], 0
    for n in lengths:
        full.append(small_flat[:, place : place + n].reshape(-1).astype(F32))
        place += n
    (qv_shift, proj_shift, up_shift, down_shift, gain_first, shift_first, gain_second, shift_second,
     scale_first, scale_second) = full

    half = shards // 2
    shard = lax.axis_index("shard")
    mine = lax.div(shard, half)
    swap = [(i, (i + half) % shards) for i in range(shards)]

    def join(array):
        keep = lax.dynamic_index_in_dim(array, mine, 0, keepdims=False)
        give = lax.dynamic_index_in_dim(array, 1 - mine, 0, keepdims=False)
        return jnp.concatenate([keep, lax.ppermute(give, "shard", swap)], axis=0)

    def split(array):
        rows = array.shape[0] // 2
        got = lax.ppermute(array[rows:], "shard", swap)
        first = jnp.where(mine == 0, array[:rows], got)
        second = jnp.where(mine == 0, got, array[:rows])
        return jnp.stack([first, second])

    inputs = join(tokens).astype(F32)
    upstream = join(cotangent).astype(F32)
    live = (mine < image_count[lax.axis_index("replica")]).astype(F32)
    rows = inputs.shape[0]

    groups = [list(range(half)), list(range(half, shards))]
    other = [(i, i ^ 1) for i in range(shards)]

    def all_rows(array):
        if half == 2:
            return jnp.concatenate([array, lax.ppermute(array, "shard", other)], axis=0)
        return lax.all_gather(array, "shard", axis=0, tiled=True, axis_index_groups=groups)

    def sum_rows(array):
        if half == 2:
            got = lax.ppermute(array[rows:].astype(BF), "shard", other)
            return array[:rows] + got.astype(F32)
        return lax.psum_scatter(array, "shard", scatter_dimension=0, tiled=True, axis_index_groups=groups)

    unit_first, rstd_first = norm_parts(inputs)
    normed_low = (unit_first * gain_first + shift_first).astype(BF)
    projected = matmul(normed_low, qkv_full)
    queries = (projected[:, :width] + qv_shift[:width]).astype(BF)
    keys = projected[:, width : 2 * width].astype(BF)
    values = (projected[:, 2 * width :] + qv_shift[width:]).astype(BF)
    keys_all, values_all = all_rows(keys), all_rows(values)
    attended, lse = attention_forward(queries, keys_all, values_all)
    branch = matmul(attended, proj_full) + proj_shift
    middle = inputs + scale_first * branch
    unit_second, rstd_second = norm_parts(middle)
    second_low = (unit_second * gain_second + shift_second).astype(BF)
    hidden = matmul(second_low, up_full) + up_shift
    gate = 0.5 * (1.0 + lax.erf(hidden * (0.5**0.5)))
    act = (hidden * gate).astype(BF)
    slope = gate + hidden * (jnp.exp(-0.5 * hidden * hidden) * 0.3989422804014327)
    feed = matmul(act, down_full) + down_shift
    result = middle + scale_second * feed
    output = split((result * live).astype(BF))

    grad_result = upstream * live
    grad_scale_second = jnp.sum(grad_result * feed, axis=0)
    grad_feed = (grad_result * scale_second).astype(BF)
    grad_down_shift = column_sum(grad_feed)
    grad_act = matmul(grad_feed, down_full, ((1,), (1,)))
    grad_pre = (grad_act * slope).astype(BF)
    grad_up_shift = column_sum(grad_pre)
    grad_second = matmul(grad_pre, up_full, ((1,), (1,)))
    grad_gain_second = jnp.sum(grad_second * unit_second, axis=0)
    grad_shift_second = jnp.sum(grad_second, axis=0)
    grad_middle = grad_result + norm_back(grad_second, unit_second, rstd_second, gain_second)
    grad_scale_first = jnp.sum(grad_middle * branch, axis=0)
    grad_branch = (grad_middle * scale_first).astype(BF)
    grad_proj_shift = column_sum(grad_branch)
    grad_attended = matmul(grad_branch, proj_full, ((1,), (1,))).astype(BF)
    grad_queries, keys_part, values_part = attention_backward(
        queries, keys_all, values_all, grad_attended, lse
    )
    grad_keys, grad_values = sum_rows(keys_part).astype(BF), sum_rows(values_part).astype(BF)
    grad_qkv = jnp.concatenate([grad_queries, grad_keys, grad_values], axis=1)
    grad_qv_shift = jnp.concatenate([column_sum(grad_queries), column_sum(grad_values)])
    grad_first = matmul(grad_qkv, qkv_full, ((1,), (1,)))
    grad_gain_first = jnp.sum(grad_first * unit_first, axis=0)
    grad_shift_first = jnp.sum(grad_first, axis=0)
    grad_inputs = grad_middle + norm_back(grad_first, unit_first, rstd_first, gain_first)
    grad_tokens = split(grad_inputs)

    sums = (grad_qv_shift, grad_proj_shift, grad_up_shift, grad_down_shift, grad_gain_first,
            grad_shift_first, grad_gain_second, grad_shift_second, grad_scale_first, grad_scale_second)
    small = jnp.concatenate([v.reshape(shards, -1) for v in sums], axis=1)
    small = jnp.pad(small, ((0, 0), (0, padded - n_small))).reshape(shards * padded // 1024, 1024)
    pairs = ((act, grad_feed), (second_low, grad_pre), (attended, grad_branch), (normed_low, grad_qkv))
    (grad_down, grad_up, grad_proj, grad_qkv_weight), small = reduce_gradients(
        replicas, shards, pairs, small
    )
    own = lax.dynamic_index_in_dim(small.reshape(shards, padded), shard, 0, keepdims=False)
    done, start = [], 0
    for n in lengths:
        done.append(own[start : start + n])
        start += n
    (g_qv, g_pb, g_ub, g_db, g_ag, g_as, g_mg, g_ms, g_sa, g_sm) = done
    return (output, grad_tokens, grad_qkv_weight, g_qv, grad_proj, g_pb, grad_up, g_ub, grad_down, g_db,
            g_ag, g_as, g_mg, g_ms, g_sa, g_sm)


def solution(mesh):
    rows, vector = P("shard", None), P("shard")
    image = P("replica", "shard", None)
    in_specs = (image, rows, vector, rows, vector, rows, vector, rows, vector, vector, vector, vector,
                vector, vector, vector, image, P())
    out_specs = (image, image, rows, vector, rows, vector, rows, vector, rows, vector, vector, vector,
                 vector, vector, vector, vector)
    return jax.shard_map(
        functools.partial(on_device, mesh.shape["replica"], mesh.shape["shard"]),
        mesh=mesh, in_specs=in_specs, out_specs=out_specs, check_vma=False,
    )
```

time: 1400 us -> 614 us (0.44)
  waiting for transfers between devices: 958 us -> 23.1 us
  Pallas kernels: 0 us -> 435 us
  matrix products: 187 us -> 60.6 us
  blocking collectives: 104 us -> 0 us
  other arithmetic: 60.3 us -> 28.6 us
  local copies, waits for them, and re-layouts: 68.1 us -> 49.8 us
  between operations: 17.3 us -> 2.44 us
    reduce_scatter x6 -> x0, waiting for transfers between devices: 494 us -> none  [the longest x1 129 us: on_device(): lax.psum_scatter(grad_up, 'shard', scatter_dimension=0, tiled=True)]
    pallas_call x0 -> x4, Pallas kernels: none -> 435 us  [the longest x1 196 us: gather_weights(): pl.pallas_call(functools.partial(gather_kernel, replicas, shards, count),...]
    psum x1 -> x0, waiting for transfers between devices: 325 us -> none  [on_device(): summed = lax.psum(tuple(owned), 'replica')]
    all_gather x6 -> x0, waiting for transfers between devices: 135 us -> none  [the longest x1 46.6 us: on_device(): lax.all_gather(shards[6], 'shard', axis=0, tiled=True)]
    dot_general x26 -> x8, matrix products: 187 us -> 60.6 us  [matmul(): lax.dot_general(left, right, (dims, ((), ())), preferred_element_type=F32)]
    all_gather x10 -> x0, blocking collectives: 52.2 us -> none  [the longest x1 6.01 us: on_device(): lax.all_gather(shards[9], 'shard', axis=0, tiled=True)]
    psum x1 -> x0, blocking collectives: 39.6 us -> none  [on_device(): summed = lax.psum(tuple(owned), 'replica')]
    convert_element_type x17 -> x9, other arithmetic: 44.3 us -> 12 us  [the longest x4 7.95 us: reduce_gradients(): grads.append(block.astype(F32))]
  transfers between devices with their start and end apart: 13 -> 8, of which waited for: 11 -> 2; matrix products, arithmetic and copies ran while one was open for 11% -> 9% of each run, Pallas kernels for 0% -> 64%
where the time goes in v1:
time: 614 us; the launch traced here: 605 us
  Pallas kernels  435 us (71%)
  matrix products  60.6 us (10%)
  local copies, waits for them, and re-layouts  49.8 us (8%)
  other arithmetic  28.6 us (5%)
  waiting for transfers between devices  23.1 us (4%)
    pallas_call x1, Pallas kernels, gather_weights(): pl.pallas_call(functools.partial(gather_kernel, replicas, shards, count),...  196 us
    pallas_call x1, Pallas kernels, reduce_gradients(): pl.pallas_call(functools.partial(reduce_kernel, replicas, shards, tuple(p...  191 us
    dot_general x8, matrix products, matmul(): lax.dot_general(left, right, (dims, ((), ())), preferred_element_type=F32)  60.6 us
    pallas_call x1, Pallas kernels, attention_backward(): pl.pallas_call(attend_backward, grid=(pairs,), in_specs=[part(rows), part...  29.3 us
    convert_element_type x6, local copies, waits for them, and re-layouts, reduce_gradients(): grads.append(block.astype(F32))  22.4 us
    pallas_call x1, Pallas kernels, attention_forward(): pl.pallas_call(attend_forward, grid=(pairs,), in_specs=[part(rows), part(...  18.8 us
  transfers between devices with their start and end apart: 8, of which 2 were waited for; matrix products, arithmetic and copies ran while one was open for 9% of the time, Pallas kernels for 64%

profile of v1, /device:TPU:0, one launch (start us, length us, event | category | flops | bytes accessed | tf_op | source)
XLA Modules:
  0.0 605.2 jit_solution(2596246047357202448)
XLA Ops:
  0.8 1.3 dynamic-slice_bitcast_fusion.3
  2.1 3.0 collective-permute-start
  7.2 0.6 reshape.238.refs_4_
  7.9 196.1 %shard_map.288 = (bf16[4,256,3072]{2,1,0:T(8,128)(2,1)}, bf16[4,256,1024]{2,1,0:T(8,128)(2,1)}, bf16[4,256,4096]{2,1,0:T(8,128)(2,1)}, bf16[4,1024,1024]{2,1,0:T(8,128)(2,1)}, bf16[4,16,256]{2,1,0:T(8,128)(2,1)}) custom-call(bf16[256,3072]{1,0:T(8,128)(2,1)} %refs_0_.1, bf16[256,1024]{1,0:T(8,128)(2,1)} %refs_1_.1, bf16[256,4096]{1,0:T(8,128)(2,1)} %refs_2_.1, ...), custom_call_target="tpu_custom_call" | custom-call | tf_op jit(solution)/shard_map/pallas_call | solution.py:258
  204.0 0.8 copy.39
  205.1 0.4 fusion.19
  205.5 0.5 fusion.13.refs_6_
  206.0 5.9 fusion.25
  211.9 1.1 slice.253
  213.0 1.6 fusion.20
  214.6 0.5 collective-permute-start.2
  215.2 1.0 dynamic-slice_bitcast_fusion.1
  216.2 0.5 collective-permute-start.4
  216.7 0.6 dynamic_slice.22
  218.0 12.2 %collective-permute-done.4 = bf16[256,1024]{1,0:T(8,128)(2,1)S(1)} collective-permute-done((bf16[256,1024]{1,0:T(8,128)(2,1)}, bf16[256,1024]{1,0:T(8,128)(2,1)S(1)}, u32[]{:S(2)}, u32[]{:S(2)}) %collective-permute-start.4) | collective-permute-done | bytes 524320 | tf_op jit(solution)/shard_map/ppermute | solution.py:553
  230.2 0.8 copy-done.16
  231.1 1.6 convert_reduce_fusion.2
  232.6 2.1 pad_maximum_fusion.1.k_ref
  234.7 3.0 pad_maximum_fusion.2.v_ref
  237.8 18.8 %shard_map.289 = (bf16[512,1024]{1,0:T(8,128)(2,1)S(1)}, f32[8,2,512]{2,1,0:T(2,128)S(1)}) custom-call(bf16[512,1024]{1,0:T(8,128)(2,1)S(1)} %get-tuple-element.61.q_ref, bf16[1024,1024]{1,0:T(8,128)(2,1)S(1)} %pad_maximum_fusion.1.k_ref, bf16[1024,1024]{1,0:T(8,128)(2,1)} %pad_maximum_fusion.2.v_ref), custom_call_target="tpu_custom_call" | custom-call | tf_op jit(solution)/shard_map/pallas_call | solution.py:78
  256.6 2.7 fusion.23
  259.7 0.4 add_convert_fusion.2.refs_2_
  260.1 10.0 %multiply_convert_fusion = (bf16[512,4096]{1,0:T(8,128)(2,1)S(1)}, f32[512,4096]{1,0:T(8,128)}) fusion(f32[4096]{0:T(1024)S(1)} %bitcast.133, bf16[512,1024]{1,0:T(8,128)(2,1)S(1)} %add_convert_fusion.2.refs_2_, bf16[1024,4096]{1,0:T(8,128)(2,1)} %bitcast.150), kind=kOutput, calls=%fused_computation.8 | convolution fusion | flops 4307550208 | bytes 22036480 | tf_op jit(solution)/shard_map/dot_general | solution.py:20
  270.1 12.2 %convert_reduce_fusion = (f32[4096]{0:T(1024)S(1)}, bf16[512,4096]{1,0:T(8,128)(2,1)S(1)}) fusion(f32[512,4096]{1,0:T(8,128)} %get-tuple-element.94, f32[4096]{0:T(1024)S(1)} %bitcast.134, bf16[512,1024]{1,0:T(8,128)(2,1)S(1)} %get-tuple-element.51.refs_1_, bf16[4096,1024]{1,0:T(8,128)(2,1)} %bitcast.148), kind=kOutput, calls=%fused_computation.7 | convolution fusion | flops 4322226176 | bytes 22052864 | tf_op jit(solution)/shard_map/dot_general | solution.py:20
  282.4 11.2 %multiply_reduce_fusion.2 = (f32[1024]{0:T(1024)S(1)}, f32[512]{0:T(512)S(1)}, f32[512]{0:T(512)S(1)}, f32[1024]{0:T(1024)S(1)}, f32[512,1024]{1,0:T(8,128)}) fusion(f32[512,1024]{1,0:T(8,128)S(1)} %get-tuple-element.57, f32[512]{0:T(512)S(1)} %add_rsqrt_fusion, f32[512]{0:T(512)S(1)} %broadcast_multiply_fusion.4, f32[1024]{0:T(1024)S(1)} %bitcast.127, ...), kind=kOutput, calls=%fused_computation.43 | convolution fusion | flops 4299682816 | bytes 16797696 | tf_op jit(solution)/shard_map/dot_general | solution.py:20
  293.6 10.3 %multiply_reduce_fusion = (f32[1024]{0:T(1024)S(1)}, bf16[512,1024]{1,0:T(8,128)(2,1)S(1)}, f32[1024]{0:T(1024)S(1)}, f32[512,1024]{1,0:T(8,128)S(1)}) fusion(f32[]{:T(128)S(6)} %convert_element_type.240, f32[1024]{0:T(1024)S(1)} %bitcast.135, bf16[256,1024]{1,0:T(8,128)(2,1)S(1)} %copy-done.17, bf16[256,1024]{1,0:T(8,128)(2,1)S(1)} %copy-done.13, ...), kind=kOutput, calls=%fused_computation.41 | convolution fusion | flops 4307023872 | bytes 23101444 | tf_op jit(solution)/shard_map/dot_general | solution.py:20
  304.2 1.3 convolution_convert_fusion.g_ref
  305.6 29.3 %shard_map.290 = (bf16[512,1024]{1,0:T(8,128)(2,1)S(1)}, f32[1024,1024]{1,0:T(8,128)}, f32[1024,1024]{1,0:T(8,128)}) custom-call(bf16[512,1024]{1,0:T(8,128)(2,1)S(1)} %get-tuple-element.61.q_ref, bf16[1024,1024]{1,0:T(8,128)(2,1)S(1)} %pad_maximum_fusion.1.k_ref, bf16[1024,1024]{1,0:T(8,128)(2,1)} %pad_maximum_fusion.2.v_ref, ...), custom_call_target="tpu_custom_call" | custom-call | tf_op jit(solution)/shard_map/pallas_call | solution.py:96
  334.9 2.7 slice.251
  337.6 0.8 slice.217
  338.5 0.5 collective-permute-start.3
  339.0 2.7 slice.252
  342.2 10.9 %collective-permute-done.3 = bf16[256,1024]{1,0:T(8,128)(2,1)} collective-permute-done((bf16[256,1024]{1,0:T(8,128)(2,1)}, bf16[256,1024]{1,0:T(8,128)(2,1)}, u32[]{:S(2)}, u32[]{:S(2)}) %collective-permute-start.3) | collective-permute-done | bytes 524320 | tf_op jit(solution)/shard_map/ppermute | solution.py:557
  353.1 1.3 select_bitcast_fusion.3
  354.4 1.1 pad_maximum_fusion.5
  355.5 0.4 convert_reduce_fusion.4
  355.9 1.7 copy-done.12
  357.6 1.6 add_convert_fusion.1
  359.3 2.0 pad_maximum_fusion.refs_7_
  361.3 7.0 %fusion.18 = (f32[1024]{0:T(1024)S(1)}, f32[512]{0:T(512)S(1)}, f32[512]{0:T(512)S(1)}, f32[1024]{0:T(1024)S(1)}, f32[512,1024]{1,0:T(8,128)S(1)}) fusion(f32[512]{0:T(512)S(1)} %add_rsqrt_fusion.1, f32[512]{0:T(512)S(1)} %broadcast_multiply_fusion.5, bf16[256,1024]{1,0:T(8,128)(2,1)S(1)} %collective-permute-done, ...), kind=kOutput, calls=%fused_computation.29 | convolution fusion | flops 3237475328 | bytes 12603392 | tf_op jit(solution)/shard_map/dot_general | solution.py:20
  368.3 0.7 fusion.17
  369.1 1.3 copy-done.1
  370.4 1.1 slice.221
  371.4 0.5 collective-permute-start.7
  372.1 0.7 reshape.253.refs_8_
  372.7 191.1 %shard_map.291 = (bf16[24,2,4,64,256]{4,3,2,1,0:T(8,128)(2,1)}, f32[16,1024]{1,0:T(8,128)}) custom-call(bf16[512,4096]{1,0:T(8,128)(2,1)} %copy-done.9, bf16[512,1024]{1,0:T(8,128)(2,1)} %copy-done.6, bf16[512,1024]{1,0:T(8,128)(2,1)} %copy-done.8, bf16[512,4096]{1,0:T(8,128)(2,1)} %copy-done.10, bf16[512,1024]{1,0:T(8,128)(2,1)} %copy-done, ...), custom_call_target="tpu_custom_call" | custom-call | tf_op jit(solution)/shard_map/pallas_call | solution.py:467
  563.8 1.5 slice.177
  565.4 0.4 convert_bitcast_fusion.2
  565.8 2.1 convert_bitcast_fusion.3
  567.9 2.0 copy.35
  569.9 3.0 reshape.264
  573.0 1.9 copy.36
  574.9 1.2 copy.51
  576.1 4.9 convert_bitcast_fusion
  581.0 0.6 convert_bitcast_fusion.1
  581.5 4.6 copy.37
  586.2 5.8 reshape.266
  591.9 5.0 copy.38
  596.9 3.0 copy.52
  600.0 0.7 dynamic-slice.2
  600.6 0.6 constant_dynamic-slice_fusion
  601.2 0.7 fusion.24
  601.9 1.4 select_bitcast_fusion.1
  603.3 1.5 pad_maximum_fusion.3
  (129 shorter events, 3.9 us)
Async XLA Ops:
  0.7 4.5 copy-start.20
  0.7 4.6 copy-start.21
  0.7 4.8 copy-start.19
  0.7 5.1 copy-start.22
  0.7 5.3 copy-start.23
  0.7 5.5 copy-start.24
  0.7 5.7 copy-start.25
  0.7 5.9 copy-start.26
  0.7 6.1 %copy-start.27 = (bf16[256]{0:T(256)(128)(2,1)S(1)}, bf16[256]{0:T(256)(128)(2,1)}, u32[]{:S(2)}) copy-start(bf16[256]{0:T(256)(128)(2,1)} %param.30) | copy-start | bytes 1540
  0.7 6.3 %copy-start.28 = (bf16[256]{0:T(256)(128)(2,1)S(1)}, bf16[256]{0:T(256)(128)(2,1)}, u32[]{:S(2)}) copy-start(bf16[256]{0:T(256)(128)(2,1)} %param.31) | copy-start | bytes 1540
  2.1 202.8 %collective-permute-start = (bf16[256,1024]{1,0:T(8,128)(2,1)S(1)}, bf16[256,1024]{1,0:T(8,128)(2,1)S(1)}, u32[]{:S(2)}, u32[]{:S(2)}) collective-permute-start(bf16[256,1024]{1,0:T(8,128)(2,1)S(1)} %get-tuple-element.73), channel_id=1, source_target_pairs={{0,2},{1,3},{2,0},{3,1},{4,6},{5,7},{6,4},{7,5},{8,10},{9,11},{10,... | collective-permute-start | bytes 1572872 | tf_op jit(solution)/shard_map/ppermute | solution.py:553
  206.0 5.9 copy-start.7
  213.0 19.6 %collective-permute-start.1 = (bf16[512,1024]{1,0:T(8,128)(2,1)}, bf16[512,1024]{1,0:T(8,128)(2,1)}, u32[]{:S(2)}, u32[]{:S(2)}) collective-permute-start(bf16[512,1024]{1,0:T(8,128)(2,1)} %slice.253), channel_id=1, source_target_pairs={{0,1},{1,0},{2,3},{3,2},{4,5},{5,4},{6,7},{7,6},{8,9},{9,8},{10,11... | collective-permute-start | bytes 3145736 | tf_op jit(solution)/shard_map/ppermute | solution.py:572
  213.0 2.1 copy-start.15
  214.6 2.1 copy-start.30
  214.6 20.1 %collective-permute-start.2 = (bf16[512,1024]{1,0:T(8,128)(2,1)}, bf16[512,1024]{1,0:T(8,128)(2,1)}, u32[]{:S(2)}, u32[]{:S(2)}) collective-permute-start(bf16[512,1024]{1,0:T(8,128)(2,1)} %get-tuple-element.60), channel_id=1, source_target_pairs={{0,1},{1,0},{2,3},{3,2},{4,5},{5,4},{6,7},{7,6},{8,9},{9,8},{10,11... | collective-permute-start | bytes 3145736 | tf_op jit(solution)/shard_map/ppermute | solution.py:572
  216.2 14.0 %collective-permute-start.4 = (bf16[256,1024]{1,0:T(8,128)(2,1)}, bf16[256,1024]{1,0:T(8,128)(2,1)S(1)}, u32[]{:S(2)}, u32[]{:S(2)}) collective-permute-start(bf16[256,1024]{1,0:T(8,128)(2,1)} %get-tuple-element.71), channel_id=1, source_target_pairs={{0,2},{1,3},{2,0},{3,1},{4,6},{5,7},{6,4},{7,5},{8,10},{9,11},{10,... | collective-permute-start | bytes 1572872 | tf_op jit(solution)/shard_map/ppermute | solution.py:553
  230.2 0.8 copy-start.16
  232.6 37.5 %copy-start.6 = (bf16[512,1024]{1,0:T(8,128)(2,1)}, bf16[512,1024]{1,0:T(8,128)(2,1)S(1)}, u32[]{:S(2)}) copy-start(bf16[512,1024]{1,0:T(8,128)(2,1)S(1)} %get-tuple-element.51.refs_1_) | copy-start | bytes 3145732
  237.8 18.8 %copy-start.29 = (bf16[4,256,1024]{2,1,0:T(8,128)(2,1)S(1)}, bf16[4,256,1024]{2,1,0:T(8,128)(2,1)}, u32[]{:S(2)}) copy-start(bf16[4,256,1024]{2,1,0:T(8,128)(2,1)} %get-tuple-element.31) | copy-start | bytes 6291460
  256.6 2.7 copy-start
  260.1 10.0 %copy-start.8 = (bf16[512,1024]{1,0:T(8,128)(2,1)}, bf16[512,1024]{1,0:T(8,128)(2,1)S(1)}, u32[]{:S(2)}) copy-start(bf16[512,1024]{1,0:T(8,128)(2,1)S(1)} %add_convert_fusion.2.refs_2_) | copy-start | bytes 3145732
  270.1 23.4 %copy-start.9 = (bf16[512,4096]{1,0:T(8,128)(2,1)}, bf16[512,4096]{1,0:T(8,128)(2,1)S(1)}, u32[]{:S(2)}) copy-start(bf16[512,4096]{1,0:T(8,128)(2,1)S(1)} %get-tuple-element.93.refs_0_) | copy-start | bytes 12582916
  282.3 11.2 %copy-start.10 = (bf16[512,4096]{1,0:T(8,128)(2,1)}, bf16[512,4096]{1,0:T(8,128)(2,1)S(1)}, u32[]{:S(2)}) copy-start(bf16[512,4096]{1,0:T(8,128)(2,1)S(1)} %get-tuple-element.98.refs_3_) | copy-start | bytes 12582916
  282.4 11.2 %copy-start.13 = (bf16[256,1024]{1,0:T(8,128)(2,1)S(1)}, bf16[256,1024]{1,0:T(8,128)(2,1)}, u32[]{:S(2)}) copy-start(bf16[256,1024]{1,0:T(8,128)(2,1)} %get-tuple-element.70) | copy-start | bytes 1572868
  282.4 11.2 %copy-start.17 = (bf16[256,1024]{1,0:T(8,128)(2,1)S(1)}, bf16[256,1024]{1,0:T(8,128)(2,1)}, u32[]{:S(2)}) copy-start(bf16[256,1024]{1,0:T(8,128)(2,1)} %copy-done.16) | copy-start | bytes 1572868
  303.9 1.7 copy-start.3
  303.9 33.7 %copy-start.14 = (bf16[512,1024]{1,0:T(8,128)(2,1)}, bf16[512,1024]{1,0:T(8,128)(2,1)S(1)}, u32[]{:S(2)}) copy-start(bf16[512,1024]{1,0:T(8,128)(2,1)S(1)} %get-tuple-element.65) | copy-start | bytes 3145732
  304.2 1.3 copy-start.5
  337.6 17.8 %collective-permute-start.6 = (bf16[512,1024]{1,0:T(8,128)(2,1)}, bf16[512,1024]{1,0:T(8,128)(2,1)S(1)}, u32[]{:S(2)}, u32[]{:S(2)}) collective-permute-start(bf16[512,1024]{1,0:T(8,128)(2,1)} %slice.251), channel_id=1, source_target_pairs={{0,1},{1,0},{2,3},{3,2},{4,5},{5,4},{6,7},{7,6},{8,9},{9,8},{10,11... | collective-permute-start | bytes 3145736 | tf_op jit(solution)/shard_map/ppermute | solution.py:577
  338.5 14.7 %collective-permute-start.3 = (bf16[256,1024]{1,0:T(8,128)(2,1)}, bf16[256,1024]{1,0:T(8,128)(2,1)}, u32[]{:S(2)}, u32[]{:S(2)}) collective-permute-start(bf16[256,1024]{1,0:T(8,128)(2,1)} %slice.217), channel_id=1, source_target_pairs={{0,2},{1,3},{2,0},{3,1},{4,6},{5,7},{6,4},{7,5},{8,10},{9,11},{10,... | collective-permute-start | bytes 1572872 | tf_op jit(solution)/shard_map/ppermute | solution.py:557
  341.7 14.2 %collective-permute-start.5 = (bf16[512,1024]{1,0:T(8,128)(2,1)}, bf16[512,1024]{1,0:T(8,128)(2,1)}, u32[]{:S(2)}, u32[]{:S(2)}) collective-permute-start(bf16[512,1024]{1,0:T(8,128)(2,1)} %slice.252), channel_id=1, source_target_pairs={{0,1},{1,0},{2,3},{3,2},{4,5},{5,4},{6,7},{7,6},{8,9},{9,8},{10,11... | collective-permute-start | bytes 3145736 | tf_op jit(solution)/shard_map/ppermute | solution.py:577
  342.2 13.3 %copy-start.11 = (f32[1024,1024]{1,0:T(8,128)S(1)}, f32[1024,1024]{1,0:T(8,128)}, u32[]{:S(2)}) copy-start(f32[1024,1024]{1,0:T(8,128)} %get-tuple-element.37) | copy-start | bytes 12582916
  355.4 2.2 copy-start.12
  361.2 7.0 %copy-start.4 = (f32[512,1024]{1,0:T(8,128)S(1)}, f32[512,1024]{1,0:T(8,128)}, u32[]{:S(2)}) copy-start(f32[512,1024]{1,0:T(8,128)} %copy-done.3) | copy-start | bytes 6291460
  369.0 1.3 copy-start.1
  371.4 230.5 %collective-permute-start.7 = (f32[256,1024]{1,0:T(8,128)}, f32[256,1024]{1,0:T(8,128)}, u32[]{:S(2)}, u32[]{:S(2)}) collective-permute-start(f32[256,1024]{1,0:T(8,128)} %slice.221), channel_id=1, source_target_pairs={{0,2},{1,3},{2,0},{3,1},{4,6},{5,7},{6,4},{7,5},{8,10},{9,11},{10,... | collective-permute-start | bytes 3145736 | tf_op jit(solution)/shard_map/ppermute | solution.py:557
  569.9 3.1 copy-start.18
  596.9 5.0 copy-start.2

commit v2 on v1

v2 whole, which is shorter than its diff:
```python
import functools

import jax
import jax.numpy as jnp
from jax import lax
from jax.experimental import pallas as pl
from jax.experimental.pallas import tpu as pltpu
from jax.sharding import PartitionSpec as P

HEAD_DIM = 64
EPS = 1e-06
BF = jnp.bfloat16
F32 = jnp.float32
MESH = pl.DeviceIdType.MESH
MIB = 1024 * 1024
SLOTS = 4


def matmul(left, right, dims=((1,), (0,))):
    return lax.dot_general(left, right, (dims, ((), ())), preferred_element_type=F32)


def column_sum(values):
    return jnp.sum(values.astype(F32), axis=0)


def attend_forward(q_ref, k_ref, v_ref, out_ref, lse_ref):
    lane = lax.broadcasted_iota(jnp.int32, (1, 128), 1)
    query, key, value = q_ref[...], k_ref[...], v_ref[...]
    value_t = value.T
    parts = []
    for head in range(2):
        mine = (lane < HEAD_DIM) if head == 0 else (lane >= HEAD_DIM)
        own = jnp.where(mine, query * BF(HEAD_DIM**-0.5), BF(0))
        scores = matmul(key, own, ((1,), (1,)))
        highest = jnp.max(scores, axis=0, keepdims=True)
        expos = jnp.exp(scores - highest)
        denom = jnp.sum(expos, axis=0, keepdims=True)
        probs = (expos * (1.0 / denom)).astype(BF)
        lse_ref[0, head : head + 1, :] = highest + jnp.log(denom)
        rows = slice(head * HEAD_DIM, (head + 1) * HEAD_DIM)
        parts.append(matmul(value_t[rows, :], probs))
    out_ref[...] = jnp.concatenate(parts, axis=0).T.astype(BF)


def attention_forward(query, key, value):
    rows, width = query.shape
    keys = key.shape[0]
    pairs = width // 128
    part = lambda n: pl.BlockSpec((n, 128), lambda i: (0, i))
    return pl.pallas_call(
        attend_forward,
        grid=(pairs,),
        in_specs=[part(rows), part(keys), part(keys)],
        out_specs=[part(rows), pl.BlockSpec((1, 2, rows), lambda i: (i, 0, 0))],
        out_shape=[
            jax.ShapeDtypeStruct((rows, width), BF),
            jax.ShapeDtypeStruct((pairs, 2, rows), F32),
        ],
        compiler_params=pltpu.CompilerParams(vmem_limit_bytes=48 * MIB),
    )(query, key, value)


class Place:
    def __init__(self, replicas, shards):
        self.Z, self.Y = replicas // 2, shards // 2
        self.shards = shards
        replica, shard = lax.axis_index("replica"), lax.axis_index("shard")
        self.x, self.z = lax.rem(replica, 2), lax.div(replica, 2)
        self.c, self.y = lax.rem(shard, 2), lax.div(shard, 2)
        self.s = shard

    def part(self, y, c):
        return y * 2 + c

    def at(self, x=None, z=None, y=None, c=None):
        x = self.x if x is None else x
        z = self.z if z is None else z
        y = self.y if y is None else y
        c = self.c if c is None else c
        return (z * 2 + x, y * 2 + c)

    def ahead_z(self, k):
        return lax.rem(self.z + k, self.Z)

    def behind_z(self, k):
        return lax.rem(self.z + self.Z - k, self.Z)

    def ahead_y(self, k):
        return lax.rem(self.y + k, self.Y)

    def behind_y(self, k):
        return lax.rem(self.y + self.Y - k, self.Y)

    def greet(self, extra=()):
        others = [self.at(c=1 - self.c), self.at(x=1 - self.x)]
        others += [self.at(y=self.ahead_y(k)) for k in range(1, self.Y)]
        others += [self.at(z=self.ahead_z(k)) for k in range(1, self.Z)]
        others += list(extra)
        barrier = pltpu.get_barrier_semaphore()
        for other in others:
            pl.semaphore_signal(barrier, inc=1, device_id=other, device_id_type=MESH)
        pl.semaphore_wait(barrier, len(others))


def send(src, dst, send_sem, recv_sem, device):
    return pltpu.make_async_remote_copy(
        src_ref=src,
        dst_ref=dst,
        send_sem=send_sem,
        recv_sem=recv_sem,
        device_id=device,
        device_id_type=MESH,
    )


def gather_kernel(replicas, shards, count, *refs):
    ins, outs = refs[: count + 1], refs[count + 1 : 2 * count + 2]
    (local, small_s, small_r, ys, yr, zs, zr, xs, xr, cs, cr, os, orr) = refs[2 * count + 2 :]
    place = Place(replicas, shards)
    Y, Z = place.Y, place.Z
    s = place.s
    diagonal = [
        place.at(y=place.ahead_y(k), c=1 - place.c) for k in range(1, Y)
    ]
    place.greet(diagonal)

    keep = [pltpu.make_async_copy(ins[w], outs[w].at[s], local.at[w]) for w in range(count + 1)]
    for copy in keep:
        copy.start()
    small = []
    for k in range(1, shards):
        peer = lax.rem(s + k, shards)
        small.append(
            send(ins[count], outs[count].at[s], small_s.at[k - 1], small_r.at[k - 1],
                 (lax.axis_index("replica"), peer))
        )
        small[-1].start()

    def piece(w, z):
        rows, cols = ins[w].shape
        half, step = rows // 2, cols // Z
        return (pl.ds(pl.multiple_of(place.x * half, half), half),
                pl.ds(pl.multiple_of(z * step, 128), step))

    def y_copy(w, k):
        rows, cols = piece(w, place.z)
        return send(ins[w].at[rows, cols], outs[w].at[s, rows, cols], ys.at[w, k - 1], yr.at[w, k - 1],
                    place.at(y=place.ahead_y(k)))

    def z_copy(w, k, j):
        owner = place.part(place.behind_y(k), place.c)
        rows, cols = piece(w, place.z)
        block = outs[w].at[owner, rows, cols]
        return send(block, block, zs.at[w, k - 1, j - 1], zr.at[w, k - 1, j - 1],
                    place.at(z=place.ahead_z(j)))

    def x_copy(w, k):
        owner = place.part(place.behind_y(k), place.c)
        half = ins[w].shape[0] // 2
        block = outs[w].at[owner, pl.ds(pl.multiple_of(place.x * half, half), half)]
        return send(block, block, xs.at[w, k - 1], xr.at[w, k - 1], place.at(x=1 - place.x))

    def c_copy(w, k):
        owner = place.part(place.behind_y(k), place.c)
        block = outs[w].at[owner]
        return send(block, block, cs.at[w, k - 1], cr.at[w, k - 1], place.at(c=1 - place.c))

    def own_copy(w):
        return send(ins[w], outs[w].at[s], os.at[w], orr.at[w], place.at(c=1 - place.c))

    for w in range(count):
        for k in range(1, Y):
            y_copy(w, k).start()
    for w in range(count):
        own_copy(w).start()
    for t in range(count + 3):
        if t < count:
            for k in range(1, Y):
                y_copy(t, k).wait()
                for j in range(1, Z):
                    z_copy(t, k, j).start()
        if 0 <= t - 1 < count:
            for k in range(1, Y):
                for j in range(1, Z):
                    z_copy(t - 1, k, j).wait()
                x_copy(t - 1, k).start()
        if 0 <= t - 2 < count:
            for k in range(1, Y):
                x_copy(t - 2, k).wait()
                c_copy(t - 2, k).start()
        if 0 <= t - 3 < count:
            for k in range(1, Y):
                c_copy(t - 3, k).wait()
            own_copy(t - 3).wait()
    for copy in small + keep:
        copy.wait()


def gather_weights(replicas, shards, weights, small):
    count = len(weights)
    Y, Z = shards // 2, replicas // 2
    dma = pltpu.SemaphoreType.DMA
    arrays = list(weights) + [small]
    any_spec = pl.BlockSpec(memory_space=pl.ANY)
    return pl.pallas_call(
        functools.partial(gather_kernel, replicas, shards, count),
        in_specs=[any_spec] * (count + 1),
        out_specs=[any_spec] * (count + 1),
        out_shape=[jax.ShapeDtypeStruct((shards,) + a.shape, a.dtype) for a in arrays],
        scratch_shapes=[
            dma((count + 1,)),
            dma((shards - 1,)), dma((shards - 1,)),
            dma((count, Y - 1)), dma((count, Y - 1)),
            dma((count, Y - 1, Z - 1)), dma((count, Y - 1, Z - 1)),
            dma((count, Y - 1)), dma((count, Y - 1)),
            dma((count, Y - 1)), dma((count, Y - 1)),
            dma((count,)), dma((count,)),
        ],
        compiler_params=pltpu.CompilerParams(collective_id=0, has_side_effects=True),
    )(*arrays)


def norm_parts(values):
    centre = values - jnp.mean(values, axis=-1, keepdims=True)
    scale = lax.rsqrt(jnp.mean(centre * centre, axis=-1, keepdims=True) + EPS)
    return centre * scale, scale


def norm_back(grad, unit, scale, gain):
    inner = grad * gain
    return scale * (
        inner
        - jnp.mean(inner, axis=-1, keepdims=True)
        - unit * jnp.mean(inner * unit, axis=-1, keepdims=True)
    )


QV, PROJ_B, UP_B, DOWN_B, ATTN_GAIN, ATTN_SHIFT, MLP_GAIN, MLP_SHIFT, ATTN_SCALE, MLP_SCALE = (
    0, 2, 3, 7, 8, 9, 10, 11, 12, 13)
V_MLP_SCALE, V_MLP_GAIN, V_ATTN_SCALE, V_ATTN_GAIN, V_DOWN_B, V_LIVE = range(6)

HBM_INPUTS = ("act", "slope", "cot", "x", "branch", "second", "attended", "query", "key", "value",
              "first", "down", "up", "proj", "qkv")


def backward_kernel(replicas, shards, names, *refs):
    ref = dict(zip(names, refs))
    place = Place(replicas, shards)
    Y, Z = place.Y, place.Z
    half = shards // 2
    part, crecv, ysum, yrecv = ref["part"], ref["crecv"], ref["ysum"], ref["yrecv"]
    xsum, xrecv, zsum, zrecv = ref["xsum"], ref["xrecv"], ref["zsum"], ref["zrecv"]
    out, small, vec, lse = ref["out"], ref["small_buf"], ref["vec"], ref["lse"]
    CB, W = part.shape[3], part.shape[4]
    rows = ref["gfeed"].shape[0]
    R = rows // 2
    keys = half * rows
    FF = ref["slope_s"].shape[1]
    down_rows, other_rows = FF // shards, W // shards
    blocks_d, blocks = down_rows // CB, other_rows // CB
    n_down, n_up, n_proj, n_qkv = blocks_d, blocks * (FF // W), blocks, blocks * 3
    total = n_down + n_up + n_proj + n_qkv
    FB = FF // n_down
    mine = lax.div(place.s, half)
    j_half = lax.rem(place.s, half)
    replica = lax.axis_index("replica")

    def half_peer(k):
        return (replica, mine * half + lax.rem(j_half + k, half))

    swap_peer = (replica, lax.rem(place.s + half, shards))

    big, slope, cot, gfeed = ref["big"], ref["slope_s"], ref["cot_s"], ref["gfeed"]
    lsem = ref["lsem"]

    def load(src, dst, sem):
        return pltpu.make_async_copy(src, dst, sem)

    act_loads = [
        load(ref["act"].at[:, pl.ds(n * W, W)], big.at[pl.ds(n * rows, rows)], lsem.at[n])
        for n in range(FF // W)
    ]
    plain = {}
    for number, (name, target) in enumerate(
        [("cot", cot), ("slope", slope), ("x", ref["x_s"]), ("branch", ref["branch_s"]),
         ("second", ref["second_s"]), ("attended", ref["attended_s"]), ("query", ref["query_s"]),
         ("first", ref["first_s"]), ("proj", ref["proj_s"])]
    ):
        plain[name] = load(ref[name], target, lsem.at[8 + number])
    key_load = load(ref["key"], big.at[pl.ds(0, keys)], lsem.at[4])
    value_load = load(ref["value"], big.at[pl.ds(keys, keys)], lsem.at[5])

    def down_load(i):
        return load(ref["down"].at[pl.ds(pl.multiple_of(i * FB, FB), FB)], ref["wd"].at[lax.rem(i, 2)],
                    ref["wsem"].at[0, lax.rem(i, 2)])

    def up_load(i):
        return load(ref["up"].at[:, pl.ds(pl.multiple_of(i * FB, FB), FB)], ref["wu"].at[lax.rem(i, 2)],
                    ref["wsem"].at[1, lax.rem(i, 2)])

    def qkv_load(i):
        return load(ref["qkv"].at[:, pl.ds(pl.multiple_of(i * FB, FB), FB)], ref["wu"].at[lax.rem(i, 2)],
                    ref["wsem"].at[2, lax.rem(i, 2)])

    plain["cot"].start()
    for copy in act_loads:
        copy.start()
    plain["slope"].start()
    down_load(0).start()
    up_load(0).start()
    for name in ("second", "x", "branch", "proj", "attended", "query", "first"):
        plain[name].start()

    extra = [half_peer(k) for k in range(1, half)] if half > 2 else []
    place.greet(extra)

    def core_copy(i):
        a = lax.rem(i, SLOTS)
        return send(part.at[lax.rem(i, 2), 1 - place.c], crecv.at[a], ref["cs"].at[a], ref["cr"].at[a],
                    place.at(c=1 - place.c))

    def y_copy(i, k):
        a = lax.rem(i, SLOTS)
        return send(ysum.at[a, place.ahead_y(k)], yrecv.at[a, k - 1], ref["ys"].at[a, k - 1],
                    ref["yr"].at[a, k - 1], place.at(y=place.ahead_y(k)))

    def x_copy(i):
        a = lax.rem(i, SLOTS)
        return send(xsum.at[a, 1 - place.x], xrecv.at[a], ref["xs"].at[a], ref["xr"].at[a],
                    place.at(x=1 - place.x))

    def z_copy(i, k):
        a = lax.rem(i, SLOTS)
        return send(zsum.at[a, place.ahead_z(k)], zrecv.at[a, k - 1], ref["zs"].at[a, k - 1],
                    ref["zr"].at[a, k - 1], place.at(z=place.ahead_z(k)))

    HB, WZ = CB // 2, W // Z
    x_rows = pl.ds(pl.multiple_of(place.x * HB, HB), HB)
    z_cols = pl.ds(pl.multiple_of(place.z * WZ, WZ), WZ)

    def zg_copy(i, k):
        a = lax.rem(i, SLOTS)
        block = out.at[i, x_rows, z_cols]
        return send(block, block, ref["gs"].at[a, k - 1], ref["gr"].at[a, k - 1],
                    place.at(z=place.ahead_z(k)))

    def xg_copy(i):
        a = lax.rem(i, SLOTS)
        block = out.at[i, x_rows]
        return send(block, block, ref["hs"].at[a], ref["hr"].at[a], place.at(x=1 - place.x))

    def add(*terms):
        whole = terms[0].astype(F32)
        for term in terms[1:]:
            whole = whole + term.astype(F32)
        return whole.astype(BF)

    def tick(i):
        def stage(lag):
            j = i - lag
            return j, (j >= 0) & (j < total)

        j1, ok1 = stage(1)

        @pl.when(ok1)
        def _():
            core_copy(j1).wait()
            a = lax.rem(j1, SLOTS)
            for y in range(Y):
                ysum[a, y] = add(part[lax.rem(j1, 2), place.c, y], crecv[a, y])
            for k in range(1, Y):
                y_copy(j1, k).start()

        j2, ok2 = stage(2)

        @pl.when(ok2)
        def _():
            a = lax.rem(j2, SLOTS)
            for k in range(1, Y):
                y_copy(j2, k).wait()
            for h in range(2):
                piece = slice(h * HB, (h + 1) * HB)
                xsum[a, h] = add(ysum[a, place.y, piece], *[yrecv[a, k - 1, piece] for k in range(1, Y)])
            x_copy(j2).start()

        j3, ok3 = stage(3)

        @pl.when(ok3)
        def _():
            a = lax.rem(j3, SLOTS)
            x_copy(j3).wait()
            for z in range(Z):
                cols = slice(z * WZ, (z + 1) * WZ)
                zsum[a, z] = add(xsum[a, place.x, :, cols], xrecv[a, :, cols])
            for k in range(1, Z):
                z_copy(j3, k).start()

        j4, ok4 = stage(4)

        @pl.when(ok4)
        def _():
            a = lax.rem(j4, SLOTS)
            for k in range(1, Z):
                z_copy(j4, k).wait()
            out[j4, x_rows, z_cols] = add(zsum[a, place.z], *[zrecv[a, k - 1] for k in range(1, Z)])
            for k in range(1, Z):
                zg_copy(j4, k).start()

        j5, ok5 = stage(5)

        @pl.when(ok5)
        def _():
            for k in range(1, Z):
                zg_copy(j5, k).wait()
            xg_copy(j5).start()

        j6, ok6 = stage(6)

        @pl.when(ok6)
        def _():
            xg_copy(j6).wait()

    def produce(i, part_rows, left, b, cols):
        slot = lax.rem(i, 2)
        for turn in range(2):
            c = 1 - place.c if turn == 0 else place.c
            for y in range(Y):
                first = place.part(y, c) * part_rows + b * CB
                if CB % 128 == 0:
                    value = matmul(left(pl.multiple_of(first, 128), CB), cols, ((0,), (0,))).astype(BF)
                else:
                    start = pl.multiple_of(lax.div(first, 128) * 128, 128)
                    ref["tile"][...] = matmul(left(start, 128), cols, ((0,), (0,)))
                    value = ref["tile"][pl.ds(pl.multiple_of(first - start, CB), CB)].astype(BF)
                part[slot, c, y] = value
            if turn == 0:
                core_copy(i).start()

    def act_cols(first, size):
        n = lax.div(first, W)
        return big[pl.ds(pl.multiple_of(n * rows, rows), rows),
                   pl.ds(pl.multiple_of(lax.rem(first, W), 128), size)]

    def from_ref(array):
        return lambda first, size: array[:, pl.ds(first, size)]

    def vector(row):
        return vec[row : row + 1, :]

    def note(row, value):
        small[0, 0, row : row + 1, :] += value

    small[0, 0] = jnp.zeros_like(small[0, 0])
    plain["cot"].wait()
    TR = min(128, rows)

    def feed_tile(t, _):
        tile = pl.ds(pl.multiple_of(t * TR, TR), TR)
        value = (cot[tile, :].astype(F32) * vector(V_MLP_SCALE)).astype(BF)
        gfeed[tile, :] = value
        note(DOWN_B, jnp.sum(value.astype(F32), axis=0, keepdims=True))
        return 0

    lax.fori_loop(0, rows // TR, feed_tile, 0)
    for copy in act_loads:
        copy.wait()
    plain["slope"].wait()
    acc, gmid = ref["acc"], ref["gmid"]
    acc[...] = jnp.zeros_like(acc)
    gmid[...] = jnp.zeros_like(gmid)

    def down_step(i, _):
        slot = lax.rem(i, 2)
        produce(i, down_rows, act_cols, i, gfeed[...])
        tick(i)
        down_load(i).wait()
        up_load(i).wait()

        @pl.when(i + 1 < n_down)
        def _():
            down_load(i + 1).start()
            up_load(i + 1).start()

        cols = pl.ds(pl.multiple_of(i * FB, FB), FB)
        weight = ref["wd"][slot]
        grad = matmul(gfeed[...], weight, ((1,), (1,)))
        pre = (grad * slope[:, cols].astype(F32)).astype(BF)
        slope[:, cols] = pre
        row = UP_B + lax.div(i * FB, W)
        at = pl.ds(pl.multiple_of(lax.rem(i * FB, W), FB), FB)
        small[0, 0, pl.ds(row, 1), at] = jnp.sum(pre.astype(F32), axis=0, keepdims=True)
        acc[...] += matmul(act_cols(i * FB, FB), weight)
        gmid[...] += matmul(pre, ref["wu"][slot], ((1,), (1,)))
        return 0

    lax.fori_loop(0, n_down, down_step, 0)

    key_load.start()
    value_load.start()
    for name in ("x", "branch", "proj", "second", "attended", "query", "first"):
        plain[name].wait()
    x_s, branch, gbranch, gatt = ref["x_s"], ref["branch_s"], ref["gbranch"], ref["gatt"]
    tok_out, tok_send = ref["tok_out"], ref["tok_send"]

    def middle_tile(t, _):
        tile = pl.ds(pl.multiple_of(t * TR, TR), TR)
        low = branch[tile, :]
        middle = x_s[tile, :].astype(F32) + vector(V_ATTN_SCALE) * low
        feed = acc[tile, :] + vector(V_DOWN_B)
        result = ((middle + vector(V_MLP_SCALE) * feed) * vector(V_LIVE)).astype(BF)
        lower = pl.ds(pl.multiple_of(lax.rem(t * TR, R), TR), TR) if R >= TR else pl.ds(0, R)
        if R >= TR:
            @pl.when(t * TR < R)
            def _():
                tok_out[mine, lower, :] = result

            @pl.when(t * TR >= R)
            def _():
                tok_send[lower, :] = result
        else:
            tok_out[mine] = result[:R]
            tok_send[...] = result[R:]
        upstream = cot[tile, :].astype(F32)
        note(MLP_SCALE, jnp.sum(upstream * feed, axis=0, keepdims=True))
        unit, scale = norm_parts(middle)
        grad = gmid[tile, :]
        note(MLP_GAIN, jnp.sum(grad * unit, axis=0, keepdims=True))
        note(MLP_SHIFT, jnp.sum(grad, axis=0, keepdims=True))
        grad = upstream + norm_back(grad, unit, scale, vector(V_MLP_GAIN))
        gmid[tile, :] = grad
        note(ATTN_SCALE, jnp.sum(grad * low, axis=0, keepdims=True))
        grad = (grad * vector(V_ATTN_SCALE)).astype(BF)
        gbranch[tile, :] = grad
        note(PROJ_B, jnp.sum(grad.astype(F32), axis=0, keepdims=True))
        gatt[tile, :] = matmul(grad, ref["proj_s"][...], ((1,), (1,))).astype(BF)
        return 0

    lax.fori_loop(0, rows // TR, middle_tile, 0)
    tok_copy = send(tok_send, tok_out.at[mine], ref["ts"].at[0], ref["tr"].at[0], swap_peer)
    tok_copy.start()
    key_load.wait()
    value_load.wait()

    G, query = ref["G"], ref["query_s"]
    pown, psend, precv = ref["pown"], ref["psend"], ref["precv"]
    gk_acc, gv_acc = ref["gk_acc"], ref["gv_acc"]
    pairs = W // 128
    QT = min(256, rows)

    def pair_copy(p, k):
        a = lax.rem(p, SLOTS)
        return send(psend.at[a, k - 1], precv.at[a, k - 1], ref["ps"].at[a, k - 1], ref["pr"].at[a, k - 1],
                    half_peer(k))

    def pair_done(p):
        a = lax.rem(p, SLOTS)
        for k in range(1, half):
            pair_copy(p, k).wait()
        for which in range(2):
            whole = pown[a, which]
            for k in range(1, half):
                whole = whole + precv[a, k - 1, which].astype(F32)
            cols = pl.ds(pl.multiple_of((which + 1) * W + p * 128, 128), 128)
            G[:, cols] = whole.astype(BF)

    def pair_step(p):
        lane = lax.broadcasted_iota(jnp.int32, (1, 128), 1)
        cols = pl.ds(pl.multiple_of(p * 128, 128), 128)
        key = big[pl.ds(0, keys), cols]
        value = big[pl.ds(keys, keys), cols]
        key_t = key.T
        for t in range(rows // QT):
            tile = slice(t * QT, (t + 1) * QT)
            q_tile, g_tile = query[tile, cols], gatt[tile, cols]
            parts = []
            for head in range(2):
                owned = (lane < HEAD_DIM) if head == 0 else (lane >= HEAD_DIM)
                own = jnp.where(owned, q_tile * BF(HEAD_DIM**-0.5), BF(0))
                own_grad = jnp.where(owned, g_tile, BF(0))
                probs = jnp.exp(matmul(key, own, ((1,), (1,))) - lse[p, head : head + 1, tile])
                grad_probs = matmul(value, own_grad, ((1,), (1,)))
                centre = jnp.sum(grad_probs * probs, axis=0, keepdims=True)
                grad_scores = (probs * (grad_probs - centre)).astype(BF)
                gv = matmul(probs.astype(BF), own_grad)
                gk = matmul(grad_scores, own)
                if t == 0 and head == 0:
                    gv_acc[...], gk_acc[...] = gv, gk
                else:
                    gv_acc[...] += gv
                    gk_acc[...] += gk
                lanes = slice(head * HEAD_DIM, (head + 1) * HEAD_DIM)
                parts.append(matmul(key_t[lanes, :], grad_scores))
            whole = jnp.concatenate(parts, axis=0) * (HEAD_DIM**-0.5)
            G[tile, cols] = whole.T.astype(BF)
        a = lax.rem(p, SLOTS)
        pown[a, 0], pown[a, 1] = gk_acc[:rows], gv_acc[:rows]
        for k in range(1, half):
            psend[a, k - 1, 0] = gk_acc[k * rows : (k + 1) * rows].astype(BF)
            psend[a, k - 1, 1] = gv_acc[k * rows : (k + 1) * rows].astype(BF)
            pair_copy(p, k).start()

    per_tick = pairs // n_up

    def up_step(u, _):
        i = n_down + u
        b, n = lax.rem(u, blocks), lax.div(u, blocks)
        produce(i, other_rows, from_ref(ref["second_s"]), b,
                slope[:, pl.ds(pl.multiple_of(n * W, W), W)])
        tick(i)
        for m in range(per_tick):
            p = u * per_tick + m
            pair_step(p)

            @pl.when(p >= 1)
            def _():
                pair_done(p - 1)
        return 0

    lax.fori_loop(0, n_up, up_step, 0)

    qkv_load(0).start()

    def proj_step(u, _):
        i = n_down + n_up + u
        produce(i, other_rows, from_ref(ref["attended_s"]), u, gbranch[...])
        tick(i)

        @pl.when(u == 0)
        def _():
            pair_done(pairs - 1)
        return 0

    lax.fori_loop(0, n_proj, proj_step, 0)
    acc[...] = jnp.zeros_like(acc)

    def qkv_step(u, _):
        i = n_down + n_up + n_proj + u
        b, n = lax.rem(u, blocks), lax.div(u, blocks)
        produce(i, other_rows, from_ref(ref["first_s"]), b, G[:, pl.ds(pl.multiple_of(n * W, W), W)])
        tick(i)
        qkv_load(u).wait()

        @pl.when(u + 1 < n_qkv)
        def _():
            qkv_load(u + 1).start()

        acc[...] += matmul(G[:, pl.ds(pl.multiple_of(u * FB, FB), FB)], ref["wu"][lax.rem(u, 2)],
                           ((1,), (1,)))
        return 0

    lax.fori_loop(0, n_qkv, qkv_step, 0)

    gt_out, gt_send, gt_recv = ref["gt_out"], ref["gt_send"], ref["gt_recv"]

    def first_tile(t, _):
        tile = pl.ds(pl.multiple_of(t * TR, TR), TR)
        unit, scale = norm_parts(x_s[tile, :].astype(F32))
        grad = acc[tile, :]
        note(ATTN_GAIN, jnp.sum(grad * unit, axis=0, keepdims=True))
        note(ATTN_SHIFT, jnp.sum(grad, axis=0, keepdims=True))
        note(QV, jnp.sum(G[tile, :W].astype(F32), axis=0, keepdims=True))
        note(QV + 1, jnp.sum(G[tile, 2 * W :].astype(F32), axis=0, keepdims=True))
        whole = gmid[tile, :] + norm_back(grad, unit, scale, vector(V_ATTN_GAIN))
        if R >= TR:
            lower = pl.ds(pl.multiple_of(lax.rem(t * TR, R), TR), TR)

            @pl.when(t * TR < R)
            def _():
                gt_out[mine, lower, :] = whole

            @pl.when(t * TR >= R)
            def _():
                gt_send[lower, :] = whole.astype(BF)
        else:
            gt_out[mine] = whole[:R]
            gt_send[...] = whole[R:].astype(BF)
        return 0

    lax.fori_loop(0, rows // TR, first_tile, 0)

    small_steps = [
        [place.at(c=1 - place.c)],
        [place.at(y=place.ahead_y(k)) for k in range(1, Y)],
        [place.at(x=1 - place.x)],
        [place.at(z=place.ahead_z(k)) for k in range(1, Z)],
    ]

    def small_send(step):
        return [
            send(small.at[step, 0], small.at[step, k + 1], ref["ss"].at[step, k], ref["sr"].at[step, k], device)
            for k, device in enumerate(small_steps[step])
        ]

    for copy in small_send(0):
        copy.start()
    gt_copy = send(gt_send, gt_recv, ref["ts"].at[1], ref["tr"].at[1], swap_peer)
    for lag in range(6):
        tick(total + lag)
        if lag == 0:
            gt_copy.start()
        if lag < 4:
            for copy in small_send(lag):
                copy.wait()
            whole = small[lag, 0]
            for k in range(len(small_steps[lag])):
                whole = whole + small[lag, k + 1]
            if lag < 3:
                small[lag + 1, 0] = whole
                for copy in small_send(lag + 1):
                    copy.start()
            else:
                ref["small_out"][...] = whole
    tok_copy.wait()
    gt_copy.wait()
    gt_out[1 - mine] = gt_recv[...].astype(F32)


def backward(replicas, shards, hbm, vec, lse):
    Y, Z, half = shards // 2, replicas // 2, shards // 2
    W = hbm["cot"].shape[1]
    rows, FF = hbm["act"].shape
    R, keys = rows // 2, hbm["key"].shape[0]
    CB = min(128, W // shards)
    HB, WZ = CB // 2, W // Z
    counts = (FF // shards // CB, (W // shards // CB) * (FF // W), W // shards // CB, 3 * (W // shards // CB))
    total = sum(counts)
    FB = FF // counts[0]
    peers = max(Y, Z, 2)
    dma = pltpu.SemaphoreType.DMA
    vmem, anywhere = pl.BlockSpec(memory_space=pltpu.VMEM), pl.BlockSpec(memory_space=pl.ANY)
    scratch = {
        "part": pltpu.VMEM((2, 2, Y, CB, W), BF),
        "crecv": pltpu.VMEM((SLOTS, Y, CB, W), BF),
        "ysum": pltpu.VMEM((SLOTS, Y, CB, W), BF),
        "yrecv": pltpu.VMEM((SLOTS, Y - 1, CB, W), BF),
        "xsum": pltpu.VMEM((SLOTS, 2, HB, W), BF),
        "xrecv": pltpu.VMEM((SLOTS, HB, W), BF),
        "zsum": pltpu.VMEM((SLOTS, Z, HB, WZ), BF),
        "zrecv": pltpu.VMEM((SLOTS, Z - 1, HB, WZ), BF),
        "small_buf": pltpu.VMEM((4, peers, 16, W), F32),
        "big": pltpu.VMEM((max(rows * FF // W, 2 * keys), W), BF),
        "slope_s": pltpu.VMEM((rows, FF), BF),
        "cot_s": pltpu.VMEM((rows, W), BF),
        "gfeed": pltpu.VMEM((rows, W), BF),
        "x_s": pltpu.VMEM((rows, W), BF),
        "branch_s": pltpu.VMEM((rows, W), F32),
        "second_s": pltpu.VMEM((rows, W), BF),
        "attended_s": pltpu.VMEM((rows, W), BF),
        "query_s": pltpu.VMEM((rows, W), BF),
        "first_s": pltpu.VMEM((rows, W), BF),
        "proj_s": pltpu.VMEM((W, W), BF),
        "wd": pltpu.VMEM((2, FB, W), BF),
        "wu": pltpu.VMEM((2, W, FB), BF),
        "acc": pltpu.VMEM((rows, W), F32),
        "gmid": pltpu.VMEM((rows, W), F32),
        "gbranch": pltpu.VMEM((rows, W), BF),
        "gatt": pltpu.VMEM((rows, W), BF),
        "G": pltpu.VMEM((rows, 3 * W), BF),
        "pown": pltpu.VMEM((SLOTS, 2, rows, 128), F32),
        "psend": pltpu.VMEM((SLOTS, half - 1, 2, rows, 128), BF),
        "precv": pltpu.VMEM((SLOTS, half - 1, 2, rows, 128), BF),
        "gk_acc": pltpu.VMEM((keys, 128), F32),
        "gv_acc": pltpu.VMEM((keys, 128), F32),
        "tok_send": pltpu.VMEM((R, W), BF),
        "gt_send": pltpu.VMEM((R, W), BF),
        "gt_recv": pltpu.VMEM((R, W), BF),
        "lsem": dma((24,)), "wsem": dma((3, 2)),
        "cs": dma((SLOTS,)), "cr": dma((SLOTS,)),
        "ys": dma((SLOTS, Y - 1)), "yr": dma((SLOTS, Y - 1)),
        "xs": dma((SLOTS,)), "xr": dma((SLOTS,)),
        "zs": dma((SLOTS, Z - 1)), "zr": dma((SLOTS, Z - 1)),
        "gs": dma((SLOTS, Z - 1)), "gr": dma((SLOTS, Z - 1)),
        "hs": dma((SLOTS,)), "hr": dma((SLOTS,)),
        "ps": dma((SLOTS, half - 1)), "pr": dma((SLOTS, half - 1)),
        "ss": dma((4, peers - 1)), "sr": dma((4, peers - 1)),
        "ts": dma((2,)), "tr": dma((2,)),
    }
    if CB % 128:
        scratch["tile"] = pltpu.VMEM((128, W), F32)
    outs = {
        "out": jax.ShapeDtypeStruct((total, CB, W), BF),
        "small_out": jax.ShapeDtypeStruct((16, W), F32),
        "tok_out": jax.ShapeDtypeStruct((2, R, W), BF),
        "gt_out": jax.ShapeDtypeStruct((2, R, W), F32),
    }
    names = HBM_INPUTS + ("vec", "lse") + tuple(outs) + tuple(scratch)
    out, small_out, tok_out, gt_out = pl.pallas_call(
        functools.partial(backward_kernel, replicas, shards, names),
        in_specs=[anywhere] * len(HBM_INPUTS) + [vmem, vmem],
        out_specs=[vmem] * len(outs),
        out_shape=list(outs.values()),
        scratch_shapes=list(scratch.values()),
        compiler_params=pltpu.CompilerParams(
            collective_id=1, has_side_effects=True, vmem_limit_bytes=63 * MIB
        ),
    )(*[hbm[name] for name in HBM_INPUTS], vec, lse)
    grads, base = [], 0
    for chunks, n_cols in zip(counts, (1, FF // W, 1, 3)):
        block = out[base : base + chunks].reshape(n_cols, -1, W).swapaxes(0, 1)
        grads.append(block.reshape(-1, n_cols * W).astype(F32))
        base += chunks
    return grads, small_out, tok_out, gt_out


def on_device(replicas, shards, tokens, qkv_weight, qv_bias, proj_weight, proj_bias, up_weight, up_bias,
              down_weight, down_bias, attn_gain, attn_shift, mlp_gain, mlp_shift, attn_scale, mlp_scale,
              cotangent, image_count):
    vectors = (qv_bias, proj_bias, up_bias, down_bias, attn_gain, attn_shift, mlp_gain, mlp_shift,
               attn_scale, mlp_scale)
    lengths = [v.shape[0] for v in vectors]
    n_small = sum(lengths)
    padded = -(-n_small // 2048) * 2048
    packed = jnp.pad(jnp.concatenate(vectors), (0, padded - n_small)).reshape(16, padded // 16)
    qkv_all, proj_all, up_all, down_all, small_all = gather_weights(
        replicas, shards, (qkv_weight, proj_weight, up_weight, down_weight), packed
    )
    width = tokens.shape[2]
    qkv_full, proj_full = qkv_all.reshape(width, -1), proj_all.reshape(width, -1)
    up_full, down_full = up_all.reshape(width, -1), down_all.reshape(-1, width)
    small_flat = small_all.reshape(shards, padded)
    full, place = [], 0
    for n in lengths:
        full.append(small_flat[:, place : place + n].reshape(-1).astype(F32))
        place += n
    (qv_shift, proj_shift, up_shift, down_shift, gain_first, shift_first, gain_second, shift_second,
     scale_first, scale_second) = full

    half = shards // 2
    shard = lax.axis_index("shard")
    mine = lax.div(shard, half)
    swap = [(i, (i + half) % shards) for i in range(shards)]

    def join(array):
        keep = lax.dynamic_index_in_dim(array, mine, 0, keepdims=False)
        give = lax.dynamic_index_in_dim(array, 1 - mine, 0, keepdims=False)
        return jnp.concatenate([keep, lax.ppermute(give, "shard", swap)], axis=0)

    joined = join(tokens)
    inputs = joined.astype(F32)
    live = mine < image_count[lax.axis_index("replica")]
    upstream = jnp.where(live, join(cotangent), BF(0))
    groups = [list(range(half)), list(range(half, shards))]
    other = [(i, i ^ 1) for i in range(shards)]

    def all_rows(array):
        if half == 2:
            return jnp.concatenate([array, lax.ppermute(array, "shard", other)], axis=0)
        whole = lax.all_gather(array, "shard", axis=0, tiled=True, axis_index_groups=groups)
        return jnp.roll(whole, -lax.rem(shard, half) * array.shape[0], axis=0)

    unit_first, _ = norm_parts(inputs)
    normed_low = (unit_first * gain_first + shift_first).astype(BF)
    projected = matmul(normed_low, qkv_full)
    queries = (projected[:, :width] + qv_shift[:width]).astype(BF)
    keys = projected[:, width : 2 * width].astype(BF)
    values = (projected[:, 2 * width :] + qv_shift[width:]).astype(BF)
    keys_all, values_all = all_rows(keys), all_rows(values)
    attended, lse = attention_forward(queries, keys_all, values_all)
    branch = matmul(attended, proj_full) + proj_shift
    middle = inputs + scale_first * branch
    unit_second, _ = norm_parts(middle)
    second_low = (unit_second * gain_second + shift_second).astype(BF)
    hidden = matmul(second_low, up_full) + up_shift
    gate = 0.5 * (1.0 + lax.erf(hidden * (0.5**0.5)))
    act = (hidden * gate).astype(BF)
    slope = (gate + hidden * (jnp.exp(-0.5 * hidden * hidden) * 0.3989422804014327)).astype(BF)

    vec = jnp.stack([scale_second, gain_second, scale_first, gain_first, down_shift,
                     jnp.broadcast_to(live.astype(F32), (width,))])
    vec = jnp.concatenate([vec, jnp.zeros((2, width), F32)])
    hbm = dict(act=act, slope=slope, cot=upstream, x=joined, branch=branch, second=second_low,
               attended=attended, query=queries, key=keys_all, value=values_all, first=normed_low,
               down=down_full, up=up_full, proj=proj_full, qkv=qkv_full)
    grads, small, output, grad_tokens = backward(replicas, shards, hbm, vec, lse)
    grad_down, grad_up, grad_proj, grad_qkv = grads

    def own(row, count=1):
        whole = small[row : row + count].reshape(-1)
        size = whole.shape[0] // shards
        return lax.dynamic_slice_in_dim(whole, shard * size, size)

    return (output, grad_tokens, grad_qkv, own(QV, 2), grad_proj, own(PROJ_B), grad_up,
            own(UP_B, up_bias.shape[0] * shards // width), grad_down, own(DOWN_B), own(ATTN_GAIN),
            own(ATTN_SHIFT), own(MLP_GAIN), own(MLP_SHIFT), own(ATTN_SCALE), own(MLP_SCALE))


def solution(mesh):
    rows, vector = P("shard", None), P("shard")
    image = P("replica", "shard", None)
    in_specs = (image, rows, vector, rows, vector, rows, vector, rows, vector, vector, vector, vector,
                vector, vector, vector, image, P())
    out_specs = (image, image, rows, vector, rows, vector, rows, vector, rows, vector, vector, vector,
                 vector, vector, vector, vector)
    return jax.shard_map(
        functools.partial(on_device, mesh.shape["replica"], mesh.shape["shard"]),
        mesh=mesh, in_specs=in_specs, out_specs=out_specs, check_vma=False,
    )
```

time: 614 us -> 502 us (0.82); the launches traced: 605 us -> 502 us
  matrix products: 60.6 us -> 18.8 us
  local copies, waits for them, and re-layouts: 49.8 us -> 30.2 us
  Pallas kernels: 435 us -> 421 us
  waiting for transfers between devices: 23.1 us -> 9.82 us
  other arithmetic: 28.6 us -> 16 us
    dot_general x8 -> x3, matrix products: 60.6 us -> 18.8 us  [matmul(): lax.dot_general(left, right, (dims, ((), ())), preferred_element_type=F32)]
    convert_element_type x6 -> x2, local copies, waits for them, and re-layouts: 22.4 us -> 4.69 us  [backward(): grads.append(block.reshape(-1, n_cols * W).astype(F32))]
    pallas_call x2 -> x1, Pallas kernels: 220 us -> 205 us  [backward(): pl.pallas_call(functools.partial(backward_kernel, replicas, shards, names...]
    ppermute x4 -> x0, waiting for transfers between devices: 10.9 us -> none  [the longest x2 10.9 us: split(): got = lax.ppermute(array[rows:], 'shard', swap)]
  transfers between devices with their start and end apart: 8 -> 4, of which waited for: 2 -> 1; matrix products, arithmetic and copies ran while one was open for 9% -> 2% of each run, Pallas kernels for 64% -> 39%
where the time goes in v2:
time: 502 us
  Pallas kernels  421 us (84%)
  local copies, waits for them, and re-layouts  30.2 us (6%)
  matrix products  18.8 us (4%)
  other arithmetic  16 us (3%)
  waiting for transfers between devices  9.82 us (2%)
    pallas_call x1, Pallas kernels, backward(): pl.pallas_call(functools.partial(backward_kernel, replicas, shards, names...  205 us
    pallas_call x1, Pallas kernels, gather_weights(): pl.pallas_call(functools.partial(gather_kernel, replicas, shards, count),...  196 us
    pallas_call x1, Pallas kernels, attention_forward(): pl.pallas_call(attend_forward, grid=(pairs,), in_specs=[part(rows), part(...  19.5 us
    dot_general x3, matrix products, matmul(): lax.dot_general(left, right, (dims, ((), ())), preferred_element_type=F32)  18.8 us
  transfers between devices with their start and end apart: 4, of which 1 were waited for; matrix products, arithmetic and copies ran while one was open for 2% of the time, Pallas kernels for 39%

profile of v2, /device:TPU:0, one launch (start us, length us, event | category | flops | bytes accessed | tf_op | source)
XLA Modules:
  0.0 501.6 jit_solution(10675459049077723348)
XLA Ops:
  0.8 1.3 dynamic-slice_bitcast_fusion.3
  2.1 3.0 collective-permute-start
  5.1 0.2 dynamic-update-slice
  5.3 0.2 dynamic-update-slice.1
  5.5 0.2 dynamic-update-slice.2
  5.7 0.2 dynamic-update-slice.3
  6.0 0.2 dynamic-update-slice.4
  6.2 0.2 dynamic-update-slice.5
  6.4 0.2 dynamic-update-slice.6
  6.6 0.2 dynamic-update-slice.7
  6.8 0.2 dynamic-update-slice.8
  7.0 0.2 dynamic-update-slice.9
  7.2 0.6 reshape.224.refs_4_
  7.9 196.1 %shard_map.288 = (bf16[4,256,3072]{2,1,0:T(8,128)(2,1)}, bf16[4,256,1024]{2,1,0:T(8,128)(2,1)}, bf16[4,256,4096]{2,1,0:T(8,128)(2,1)}, bf16[4,1024,1024]{2,1,0:T(8,128)(2,1)}, bf16[4,16,256]{2,1,0:T(8,128)(2,1)}) custom-call(bf16[256,3072]{1,0:T(8,128)(2,1)} %refs_0_.1, bf16[256,1024]{1,0:T(8,128)(2,1)} %refs_1_.1, bf16[256,4096]{1,0:T(8,128)(2,1)} %refs_2_.1, ...), custom_call_target="tpu_custom_call" | custom-call | tf_op jit(solution)/shard_map/pallas_call | solution.py:206
  204.0 0.8 copy.39
  204.9 0.0 collective-permute-done
  204.9 0.2 convert_reduce_fusion
  205.1 0.4 fusion.7
  205.5 0.5 fusion.10.refs_10_
  206.0 5.9 %fusion.16 = f32[512,3072]{1,0:T(8,128)S(1)} fusion(bf16[512,1024]{1,0:T(8,128)(2,1)S(1)} %fusion.10.refs_10_, bf16[1024,3072]{1,0:T(8,128)(2,1)} %bitcast.117), kind=kOutput, calls=%fused_computation.72 | convolution fusion | flops 3221225472 | bytes 13631488 | tf_op jit(solution)/shard_map/dot_general | solution.py:20
  211.9 1.6 fusion.11
  213.5 0.0 collective-permute-start.2
  213.5 0.2 slice.164
  213.7 0.6 collective-permute-start.1
  214.3 0.9 copy-done.12
  215.1 1.0 dynamic-slice_bitcast_fusion.1
  216.2 0.5 collective-permute-start.3
  216.7 0.6 dynamic_slice.64
  218.1 0.7 concatenate.23.refs_15_
  218.7 1.0 pad_maximum_fusion.2.refs_3_
  219.8 9.8 %collective-permute-done.3 = bf16[256,1024]{1,0:T(8,128)(2,1)} collective-permute-done((bf16[256,1024]{1,0:T(8,128)(2,1)}, bf16[256,1024]{1,0:T(8,128)(2,1)}, u32[]{:S(2)}, u32[]{:S(2)}) %collective-permute-start.3) | collective-permute-done | bytes 524320 | tf_op jit(solution)/shard_map/ppermute | solution.py:837
  229.6 2.2 maximum_select_fusion.refs_2_
  231.8 0.0 collective-permute-done.2
  231.8 3.0 pad_maximum_fusion.1.v_ref.refs_9_
  234.8 0.0 collective-permute-done.1
  234.8 1.4 pad_maximum_fusion.k_ref.refs_8_
  236.3 0.0 slice-start
  236.3 19.5 %shard_map.289 = (bf16[512,1024]{1,0:T(8,128)(2,1)S(1)}, f32[8,2,512]{2,1,0:T(2,128)S(1)}) custom-call(bf16[512,1024]{1,0:T(8,128)(2,1)S(1)} %get-tuple-element.59.q_ref.refs_7_, bf16[1024,1024]{1,0:T(8,128)(2,1)S(1)} %pad_maximum_fusion.k_ref.refs_8_, bf16[1024,1024]{1,0:T(8,128)(2,1)} %pad_maximum_fusion.1.v_ref.refs_9_), custom_call_target="tpu_custom_call" | custom-call | tf_op jit(solution)/shard_map/pallas_call | solution.py:51
  255.8 0.0 slice-start.1
  255.8 3.4 fusion.13
  259.2 0.0 copy-start.4
  259.2 0.5 multiply_reduce_fusion
  259.7 0.5 add_convert_fusion.refs_5_
  260.3 0.2 copy-done.4
  260.5 9.5 %fusion.4 = (bf16[512,4096]{1,0:T(8,128)(2,1)}, bf16[512,4096]{1,0:T(8,128)(2,1)}) fusion(f32[4096]{0:T(1024)S(1)} %bitcast.139, bf16[512,1024]{1,0:T(8,128)(2,1)S(1)} %add_convert_fusion.refs_5_, bf16[1024,4096]{1,0:T(8,128)(2,1)S(1)} %bitcast.114), kind=kOutput, calls=%fused_computation.5 | convolution fusion | flops 4320133120 | bytes 17842176 | tf_op jit(solution)/shard_map/dot_general | solution.py:20
  270.0 205.3 %shard_map.290 = (bf16[24,128,1024]{2,1,0:T(8,128)(2,1)}, f32[16,1024]{1,0:T(8,128)}, bf16[2,256,1024]{2,1,0:T(8,128)(2,1)}, f32[2,256,1024]{2,1,0:T(8,128)}) custom-call(bf16[512,4096]{1,0:T(8,128)(2,1)} %get-tuple-element.55.refs_0_, bf16[512,4096]{1,0:T(8,128)(2,1)} %get-tuple-element.54.refs_1_, bf16[512,1024]{1,0:T(8,128)(2,1)} %maximum_select_fusion.refs_2_, ...), custom_call_target="tpu_custom_call" | custom-call | tf_op jit(solution)/shard_map/pallas_call | solution.py:788
  475.3 4.0 fusion.14
  479.3 1.6 slice.111
  480.9 1.9 slice.113
  482.8 0.4 convert_bitcast_fusion
  483.3 2.3 copy.38
  485.6 0.4 bitcast_convert_fusion.1
  486.0 2.4 copy.35
  488.4 3.7 copy.37
  492.1 2.6 bitcast_convert_fusion
  494.7 1.1 bitcast_convert_fusion.2
  495.8 0.6 constant_dynamic-slice_fusion
  496.4 0.6 constant_dynamic-slice_fusion.2
  496.9 0.6 constant_dynamic-slice_fusion.4
  497.5 0.6 constant_dynamic-slice_fusion.6
  498.1 0.6 dynamic_slice.70
  498.7 0.7 dynamic_slice.67
  499.3 1.0 copy.74
  500.3 1.3 copy.75
  (81 shorter events, 0.3 us)
Async XLA Ops:
  0.7 4.5 copy-start.15
  0.7 4.6 copy-start.16
  0.7 4.8 copy-start.14
  0.7 5.1 %copy-start.17 = (bf16[256]{0:T(256)(128)(2,1)S(1)}, bf16[256]{0:T(256)(128)(2,1)}, u32[]{:S(2)}) copy-start(bf16[256]{0:T(256)(128)(2,1)} %param.25) | copy-start | bytes 1540
  0.7 5.3 %copy-start.18 = (bf16[256]{0:T(256)(128)(2,1)S(1)}, bf16[256]{0:T(256)(128)(2,1)}, u32[]{:S(2)}) copy-start(bf16[256]{0:T(256)(128)(2,1)} %param.26) | copy-start | bytes 1540
  0.7 5.5 %copy-start.19 = (bf16[256]{0:T(256)(128)(2,1)S(1)}, bf16[256]{0:T(256)(128)(2,1)}, u32[]{:S(2)}) copy-start(bf16[256]{0:T(256)(128)(2,1)} %param.27) | copy-start | bytes 1540
  0.7 5.7 %copy-start.20 = (bf16[256]{0:T(256)(128)(2,1)S(1)}, bf16[256]{0:T(256)(128)(2,1)}, u32[]{:S(2)}) copy-start(bf16[256]{0:T(256)(128)(2,1)} %param.28) | copy-start | bytes 1540
  0.7 5.9 %copy-start.21 = (bf16[256]{0:T(256)(128)(2,1)S(1)}, bf16[256]{0:T(256)(128)(2,1)}, u32[]{:S(2)}) copy-start(bf16[256]{0:T(256)(128)(2,1)} %param.29) | copy-start | bytes 1540
  0.7 6.1 %copy-start.22 = (bf16[256]{0:T(256)(128)(2,1)S(1)}, bf16[256]{0:T(256)(128)(2,1)}, u32[]{:S(2)}) copy-start(bf16[256]{0:T(256)(128)(2,1)} %param.30) | copy-start | bytes 1540
  0.7 6.3 %copy-start.23 = (bf16[256]{0:T(256)(128)(2,1)S(1)}, bf16[256]{0:T(256)(128)(2,1)}, u32[]{:S(2)}) copy-start(bf16[256]{0:T(256)(128)(2,1)} %param.31) | copy-start | bytes 1540
  2.1 202.8 %collective-permute-start = (bf16[256,1024]{1,0:T(8,128)(2,1)S(1)}, bf16[256,1024]{1,0:T(8,128)(2,1)S(1)}, u32[]{:S(2)}, u32[]{:S(2)}) collective-permute-start(bf16[256,1024]{1,0:T(8,128)(2,1)S(1)} %get-tuple-element.63), channel_id=1, source_target_pairs={{0,2},{1,3},{2,0},{3,1},{4,6},{5,7},{6,4},{7,5},{8,10},{9,11},{10,... | collective-permute-start | bytes 1572872 | tf_op jit(solution)/shard_map/ppermute | solution.py:837
  206.0 5.9 %copy-start.6 = (bf16[512,1024]{1,0:T(8,128)(2,1)}, bf16[512,1024]{1,0:T(8,128)(2,1)S(1)}, u32[]{:S(2)}) copy-start(bf16[512,1024]{1,0:T(8,128)(2,1)S(1)} %fusion.10.refs_10_) | copy-start | bytes 3145732
  213.5 22.7 %copy-start.1 = (bf16[512,1024]{1,0:T(8,128)(2,1)}, bf16[512,1024]{1,0:T(8,128)(2,1)S(1)}, u32[]{:S(2)}) copy-start(bf16[512,1024]{1,0:T(8,128)(2,1)S(1)} %get-tuple-element.59.q_ref.refs_7_) | copy-start | bytes 3145732
  213.5 1.6 copy-start.12
  213.5 3.2 copy-start.24
  213.5 18.3 %collective-permute-start.2 = (bf16[512,1024]{1,0:T(8,128)(2,1)}, bf16[512,1024]{1,0:T(8,128)(2,1)}, u32[]{:S(2)}, u32[]{:S(2)}) collective-permute-start(bf16[512,1024]{1,0:T(8,128)(2,1)} %get-tuple-element.58), channel_id=1, source_target_pairs={{0,1},{1,0},{2,3},{3,2},{4,5},{5,4},{6,7},{7,6},{8,9},{9,8},{10,11... | collective-permute-start | bytes 3145736 | tf_op jit(solution)/shard_map/ppermute | solution.py:848
  213.7 21.2 %collective-permute-start.1 = (bf16[512,1024]{1,0:T(8,128)(2,1)S(1)}, bf16[512,1024]{1,0:T(8,128)(2,1)}, u32[]{:S(2)}, u32[]{:S(2)}) collective-permute-start(bf16[512,1024]{1,0:T(8,128)(2,1)S(1)} %slice.164), channel_id=1, source_target_pairs={{0,1},{1,0},{2,3},{3,2},{4,5},{5,4},{6,7},{7,6},{8,9},{9,8},{10,11... | collective-permute-start | bytes 3145736 | tf_op jit(solution)/shard_map/ppermute | solution.py:848
  216.2 13.4 %collective-permute-start.3 = (bf16[256,1024]{1,0:T(8,128)(2,1)}, bf16[256,1024]{1,0:T(8,128)(2,1)}, u32[]{:S(2)}, u32[]{:S(2)}) collective-permute-start(bf16[256,1024]{1,0:T(8,128)(2,1)} %get-tuple-element.61), channel_id=1, source_target_pairs={{0,2},{1,3},{2,0},{3,1},{4,6},{5,7},{6,4},{7,5},{8,10},{9,11},{10,... | collective-permute-start | bytes 1572872 | tf_op jit(solution)/shard_map/ppermute | solution.py:837
  218.7 10.9 %copy-start.10 = (bf16[256,1024]{1,0:T(8,128)(2,1)S(1)}, bf16[256,1024]{1,0:T(8,128)(2,1)}, u32[]{:S(2)}) copy-start(bf16[256,1024]{1,0:T(8,128)(2,1)} %get-tuple-element.60) | copy-start | bytes 1572868
  236.2 19.5 %copy-start = (bf16[1024,1024]{1,0:T(8,128)(2,1)}, bf16[1024,1024]{1,0:T(8,128)(2,1)S(1)}, u32[]{:S(2)}) copy-start(bf16[1024,1024]{1,0:T(8,128)(2,1)S(1)} %pad_maximum_fusion.k_ref.refs_8_) | copy-start | bytes 6291460
  236.3 24.3 %slice-start = ((s8[8388608]{0:T(1024)(128)(4,1)}), s8[4194304]{0:T(1024)(128)(4,1)S(1)}, s32[]{:S(2)}) async-start(s8[8388608]{0:T(1024)(128)(4,1)} %bitcast.112), calls=%async_computation | async-start | bytes 8388608
  255.7 3.4 copy-start.2
  255.8 3.4 copy-start.3
  255.8 4.8 slice-start.1
  259.2 1.3 copy-start.4
  260.5 9.5 %copy-start.7 = (bf16[512,1024]{1,0:T(8,128)(2,1)}, bf16[512,1024]{1,0:T(8,128)(2,1)S(1)}, u32[]{:S(2)}) copy-start(bf16[512,1024]{1,0:T(8,128)(2,1)S(1)} %add_convert_fusion.refs_5_) | copy-start | bytes 3145732
  479.3 3.4 copy-start.13
  488.4 3.7 copy-start.5
  492.1 2.6 copy-start.8
  492.1 7.3 %copy-start.11 = (bf16[2,256,1024]{2,1,0:T(8,128)(2,1)S(1)}, bf16[2,256,1024]{2,1,0:T(8,128)(2,1)}, u32[]{:S(2)}) copy-start(bf16[2,256,1024]{2,1,0:T(8,128)(2,1)} %get-tuple-element.111) | copy-start | bytes 3145732
  494.7 5.6 %copy-start.9 = (f32[2,256,1024]{2,1,0:T(8,128)S(1)}, f32[2,256,1024]{2,1,0:T(8,128)}, u32[]{:S(2)}) copy-start(f32[2,256,1024]{2,1,0:T(8,128)} %get-tuple-element.112) | copy-start | bytes 6291460

commit v3 on v2

--- a/solution.py
+++ b/solution.py
@@ -18,47 +18,6 @@
 
 def matmul(left, right, dims=((1,), (0,))):
     return lax.dot_general(left, right, (dims, ((), ())), preferred_element_type=F32)
-
-
-def column_sum(values):
-    return jnp.sum(values.astype(F32), axis=0)
-
-
-def attend_forward(q_ref, k_ref, v_ref, out_ref, lse_ref):
-    lane = lax.broadcasted_iota(jnp.int32, (1, 128), 1)
-    query, key, value = q_ref[...], k_ref[...], v_ref[...]
-    value_t = value.T
-    parts = []
-    for head in range(2):
-        mine = (lane < HEAD_DIM) if head == 0 else (lane >= HEAD_DIM)
-        own = jnp.where(mine, query * BF(HEAD_DIM**-0.5), BF(0))
-        scores = matmul(key, own, ((1,), (1,)))
-        highest = jnp.max(scores, axis=0, keepdims=True)
-        expos = jnp.exp(scores - highest)
-        denom = jnp.sum(expos, axis=0, keepdims=True)
-        probs = (expos * (1.0 / denom)).astype(BF)
-        lse_ref[0, head : head + 1, :] = highest + jnp.log(denom)
-        rows = slice(head * HEAD_DIM, (head + 1) * HEAD_DIM)
-        parts.append(matmul(value_t[rows, :], probs))
-    out_ref[...] = jnp.concatenate(parts, axis=0).T.astype(BF)
-
-
-def attention_forward(query, key, value):
-    rows, width = query.shape
-    keys = key.shape[0]
-    pairs = width // 128
-    part = lambda n: pl.BlockSpec((n, 128), lambda i: (0, i))
-    return pl.pallas_call(
-        attend_forward,
-        grid=(pairs,),
-        in_specs=[part(rows), part(keys), part(keys)],
-        out_specs=[part(rows), pl.BlockSpec((1, 2, rows), lambda i: (i, 0, 0))],
-        out_shape=[
-            jax.ShapeDtypeStruct((rows, width), BF),
-            jax.ShapeDtypeStruct((pairs, 2, rows), F32),
-        ],
-        compiler_params=pltpu.CompilerParams(vmem_limit_bytes=48 * MIB),
-    )(query, key, value)
 
 
 class Place:
@@ -114,111 +73,9 @@
     )
 
 
-def gather_kernel(replicas, shards, count, *refs):
-    ins, outs = refs[: count + 1], refs[count + 1 : 2 * count + 2]
-    (local, small_s, small_r, ys, yr, zs, zr, xs, xr, cs, cr, os, orr) = refs[2 * count + 2 :]
-    place = Place(replicas, shards)
-    Y, Z = place.Y, place.Z
-    s = place.s
-    diagonal = [
-        place.at(y=place.ahead_y(k), c=1 - place.c) for k in range(1, Y)
-    ]
-    place.greet(diagonal)
-
-    keep = [pltpu.make_async_copy(ins[w], outs[w].at[s], local.at[w]) for w in range(count + 1)]
-    for copy in keep:
-        copy.start()
-    small = []
-    for k in range(1, shards):
-        peer = lax.rem(s + k, shards)
-        small.append(
-            send(ins[count], outs[count].at[s], small_s.at[k - 1], small_r.at[k - 1],
-                 (lax.axis_index("replica"), peer))
-        )
-        small[-1].start()
-
-    def piece(w, z):
-        rows, cols = ins[w].shape
-        half, step = rows // 2, cols // Z
-        return (pl.ds(pl.multiple_of(place.x * half, half), half),
-                pl.ds(pl.multiple_of(z * step, 128), step))
-
-    def y_copy(w, k):
-        rows, cols = piece(w, place.z)
-        return send(ins[w].at[rows, cols], outs[w].at[s, rows, cols], ys.at[w, k - 1], yr.at[w, k - 1],
-                    place.at(y=place.ahead_y(k)))
-
-    def z_copy(w, k, j):
-        owner = place.part(place.behind_y(k), place.c)
-        rows, cols = piece(w, place.z)
-        block = outs[w].at[owner, rows, cols]
-        return send(block, block, zs.at[w, k - 1, j - 1], zr.at[w, k - 1, j - 1],
-                    place.at(z=place.ahead_z(j)))
-
-    def x_copy(w, k):
-        owner = place.part(place.behind_y(k), place.c)
-        half = ins[w].shape[0] // 2
-        block = outs[w].at[owner, pl.ds(pl.multiple_of(place.x * half, half), half)]
-        return send(block, block, xs.at[w, k - 1], xr.at[w, k - 1], place.at(x=1 - place.x))
-
-    def c_copy(w, k):
-        owner = place.part(place.behind_y(k), place.c)
-        block = outs[w].at[owner]
-        return send(block, block, cs.at[w, k - 1], cr.at[w, k - 1], place.at(c=1 - place.c))
-
-    def own_copy(w):
-        return send(ins[w], outs[w].at[s], os.at[w], orr.at[w], place.at(c=1 - place.c))
-
-    for w in range(count):
-        for k in range(1, Y):
-            y_copy(w, k).start()
-    for w in range(count):
-        own_copy(w).start()
-    for t in range(count + 3):
-        if t < count:
-            for k in range(1, Y):
-                y_copy(t, k).wait()
-                for j in range(1, Z):
-                    z_copy(t, k, j).start()
-        if 0 <= t - 1 < count:
-            for k in range(1, Y):
-                for j in range(1, Z):
-                    z_copy(t - 1, k, j).wait()
-                x_copy(t - 1, k).start()
-        if 0 <= t - 2 < count:
-            for k in range(1, Y):
-                x_copy(t - 2, k).wait()
-                c_copy(t - 2, k).start()
-        if 0 <= t - 3 < count:
-            for k in range(1, Y):
-                c_copy(t - 3, k).wait()
-            own_copy(t - 3).wait()
-    for copy in small + keep:
-        copy.wait()
-
-
-def gather_weights(replicas, shards, weights, small):
-    count = len(weights)
-    Y, Z = shards // 2, replicas // 2
-    dma = pltpu.SemaphoreType.DMA
-    arrays = list(weights) + [small]
-    any_spec = pl.BlockSpec(memory_space=pl.ANY)
-    return pl.pallas_call(
-        functools.partial(gather_kernel, replicas, shards, count),
-        in_specs=[any_spec] * (count + 1),
-        out_specs=[any_spec] * (count + 1),
-        out_shape=[jax.ShapeDtypeStruct((shards,) + a.shape, a.dtype) for a in arrays],
-        scratch_shapes=[
-            dma((count + 1,)),
-            dma((shards - 1,)), dma((shards - 1,)),
-            dma((count, Y - 1)), dma((count, Y - 1)),
-            dma((count, Y - 1, Z - 1)), dma((count, Y - 1, Z - 1)),
-            dma((count, Y - 1)), dma((count, Y - 1)),
-            dma((count, Y - 1)), dma((count, Y - 1)),
-            dma((count,)), dma((count,)),
-        ],
-        compiler_params=pltpu.CompilerParams(collective_id=0, has_side_effects=True),
-    )(*arrays)
+QV, PROJ_B, UP_B, DOWN_B, ATTN_GAIN, ATTN_SHIFT, MLP_GAIN, MLP_SHIFT, ATTN_SCALE, MLP_SCALE, LIVE = (
+    0, 2, 3, 7, 8, 9, 10, 11, 12, 13, 14)
+WEIGHTS = ("qkv", "proj", "up", "down")
 
 
 def norm_parts(values):
@@ -236,9 +93,408 @@
     )
 
 
-QV, PROJ_B, UP_B, DOWN_B, ATTN_GAIN, ATTN_SHIFT, MLP_GAIN, MLP_SHIFT, ATTN_SCALE, MLP_SCALE = (
-    0, 2, 3, 7, 8, 9, 10, 11, 12, 13)
-V_MLP_SCALE, V_MLP_GAIN, V_ATTN_SCALE, V_ATTN_GAIN, V_DOWN_B, V_LIVE = range(6)
+def forward_kernel(replicas, shards, items, multiples, names, *refs):
+    ref = dict(zip(names, refs))
+    place = Place(replicas, shards)
+    Y, Z, s = place.Y, place.Z, place.s
+    half = shards // 2
+    mine, j_half = lax.div(s, half), lax.rem(s, half)
+    replica = lax.axis_index("replica")
+    x_s, cot_s, first, query = ref["x_s"], ref["cot_s"], ref["first_s"], ref["query_s"]
+    key, value, attended = ref["key_s"], ref["value_s"], ref["attended_s"]
+    vec, lse = ref["vec"], ref["lse"]
+    rows, W = x_s.shape
+    R, keys = rows // 2, key.shape[0]
+    weights = {name: ref["w_" + name] for name in WEIGHTS}
+    shard_rows = {name: ref[name].shape[0] for name in WEIGHTS}
+    FF = weights["up"].shape[1]
+
+    def half_peer(k):
+        return (replica, mine * half + lax.rem(j_half + k, half))
+
+    swap_peer = (replica, lax.rem(s + half, shards))
+
+    def own_rows(name):
+        size = shard_rows[name]
+        return weights[name].at[pl.ds(pl.multiple_of(s * size, size), size)]
+
+    x_load = pltpu.make_async_copy(ref["tokens"].at[mine], x_s.at[pl.ds(0, R)], ref["lsem"].at[0])
+    cot_load = pltpu.make_async_copy(ref["cotangent"].at[mine], cot_s.at[pl.ds(0, R)], ref["lsem"].at[1])
+    own_loads = {
+        name: pltpu.make_async_copy(ref[name], own_rows(name), ref["lsem"].at[2 + n])
+        for n, name in enumerate(WEIGHTS)
+    }
+    small_load = pltpu.make_async_copy(ref["packed"], ref["small_s"].at[s], ref["lsem"].at[6])
+    x_load.start()
+    small_load.start()
+    for name in WEIGHTS:
+        own_loads[name].start()
+    cot_load.start()
+    extra = [(replica, lax.rem(s + k, shards)) for k in range(1, shards)]
+    place.greet(extra)
+
+    x_swap = send(ref["tokens"].at[1 - mine], x_s.at[pl.ds(R, R)], ref["ts"].at[0], ref["tr"].at[0], swap_peer)
+    cot_swap = send(ref["cotangent"].at[1 - mine], cot_s.at[pl.ds(R, R)], ref["ts"].at[1], ref["tr"].at[1],
+                    swap_peer)
+    small_sends = [
+        send(ref["packed"], ref["small_s"].at[s], ref["ss"].at[k - 1], ref["sr"].at[k - 1],
+             (replica, lax.rem(s + k, shards)))
+        for k in range(1, shards)
+    ]
+    own_sends = {
+        name: send(ref[name], own_rows(name), ref["os"].at[n], ref["or"].at[n], place.at(c=1 - place.c))
+        for n, name in enumerate(WEIGHTS)
+    }
+
+    def piece(m, owner, whole_rows=False, whole_cols=False):
+        name, start, size, _ = items[m]
+        at = owner * shard_rows[name] + start
+        step = ref[name].shape[1] // Z
+        if not whole_rows:
+            at, size = at + place.x * (size // 2), size // 2
+        at = pl.ds(pl.multiple_of(at, 16), size)
+        if whole_cols:
+            return at, slice(None)
+        return at, pl.ds(pl.multiple_of(place.z * step, 128), step)
+
+    def y_copy(m, k):
+        name, _, _, direct = items[m]
+        src = ref[name].at[piece(m, 0, direct, direct)]
+        dst = weights[name].at[piece(m, s, direct, direct)]
+        return send(src, dst, ref["ys"].at[m, k - 1], ref["yr"].at[m, k - 1], place.at(y=place.ahead_y(k)))
+
+    def block(m, k, whole_rows, whole_cols):
+        owner = place.part(place.behind_y(k), place.c)
+        return weights[items[m][0]].at[piece(m, owner, whole_rows, whole_cols)]
+
+    def z_copy(m, k, j):
+        b = block(m, k, False, False)
+        return send(b, b, ref["zs"].at[m, k - 1, j - 1], ref["zr"].at[m, k - 1, j - 1],
+                    place.at(z=place.ahead_z(j)))
+
+    def x_copy(m, k):
+        b = block(m, k, False, True)
+        return send(b, b, ref["xs"].at[m, k - 1], ref["xr"].at[m, k - 1], place.at(x=1 - place.x))
+
+    def c_copy(m, k):
+        b = block(m, k, True, True)
+        return send(b, b, ref["cs"].at[m, k - 1], ref["cr"].at[m, k - 1], place.at(c=1 - place.c))
+
+    def y_start(m):
+        for k in range(1, Y):
+            y_copy(m, k).start()
+
+    def y_step(m):
+        for k in range(1, Y):
+            y_copy(m, k).wait()
+            if items[m][3]:
+                c_copy(m, k).start()
+            else:
+                for j in range(1, Z):
+                    z_copy(m, k, j).start()
+
+    def z_step(m):
+        for k in range(1, Y):
+            for j in range(1, Z):
+                z_copy(m, k, j).wait()
+            x_copy(m, k).start()
+
+    def x_step(m):
+        for k in range(1, Y):
+            x_copy(m, k).wait()
+            c_copy(m, k).start()
+
+    def c_step(m):
+        for k in range(1, Y):
+            c_copy(m, k).wait()
+
+    QKV_A, QKV_B, PROJ, UP_A, UP_B2, DOWN_A, DOWN_B2 = range(7)
+    stores = []
+
+    def store(src, dst):
+        copy = pltpu.make_async_copy(src, dst, ref["osem"].at[len(stores)])
+        stores.append(copy)
+        copy.start()
+
+    y_start(QKV_A)
+    x_swap.start()
+    for copy in small_sends:
+        copy.start()
+    y_start(QKV_B)
+    for name in WEIGHTS:
+        own_sends[name].start()
+
+    small_load.wait()
+    for copy in small_sends:
+        copy.wait()
+    vec[...] = jnp.zeros_like(vec)
+    row = 0
+    for count in multiples:
+        pieces = [ref["small_s"][part, row + r : row + r + 1, :].astype(F32)
+                  for part in range(shards) for r in range(count)]
+        for r in range(count):
+            vec[row + r : row + r + 1, :] = jnp.concatenate(pieces[r * shards : (r + 1) * shards], axis=1)
+        row += count
+    vec[LIVE : LIVE + 1, :] = ref["live"][0:1, :]
+
+    def vector(at):
+        return vec[at : at + 1, :]
+
+    TR = min(128, R)
+
+    def first_tile(t, _):
+        tile = pl.ds(pl.multiple_of(t * TR, TR), TR)
+        unit, _ = norm_parts(x_s[tile, :].astype(F32))
+        first[tile, :] = (unit * vector(ATTN_GAIN) + vector(ATTN_SHIFT)).astype(BF)
+        return 0
+
+    x_load.wait()
+    lax.fori_loop(0, R // TR, first_tile, 0)
+    y_step(QKV_A)
+    y_start(PROJ)
+    y_start(UP_A)
+    y_start(UP_B2)
+    x_swap.wait()
+    cot_swap.start()
+    lax.fori_loop(R // TR, rows // TR, first_tile, 0)
+    store(first, ref["o_first"])
+    store(x_s, ref["o_x"])
+    own_loads["qkv"].wait()
+    own_sends["qkv"].wait()
+    y_step(PROJ)
+    y_step(UP_A)
+
+    acc = ref["acc"]
+    CT = min(512, W)
+    chunk = 2 * shard_rows["qkv"]
+
+    def project(y, cols):
+        at = pl.ds(pl.multiple_of(y * chunk, chunk), chunk)
+        return matmul(first[:, at], weights["qkv"][at, cols])
+
+    def near_tile(n, _):
+        cols = pl.ds(pl.multiple_of(n * CT, CT), CT)
+        acc[:, cols] = project(place.y, cols)
+        return 0
+
+    lax.fori_loop(0, 3 * W // CT, near_tile, 0)
+    z_step(QKV_A)
+    y_start(DOWN_A)
+    y_start(DOWN_B2)
+    x_step(QKV_A)
+    y_step(QKV_B)
+    z_step(PROJ)
+    c_step(QKV_A)
+    c_step(QKV_B)
+
+    def full_tile(n):
+        cols = slice(n * CT, (n + 1) * CT)
+        whole = acc[:, cols]
+        for k in range(1, Y):
+            whole = whole + project(place.ahead_y(k), cols)
+        return whole
+
+    per = W // CT
+
+    def kv_copy(which, n, k):
+        array = (key, value)[which]
+        cols = pl.ds(n * CT, CT)
+        return send(array.at[pl.ds(0, rows), cols], array.at[pl.ds((half - k) * rows, rows), cols],
+                    ref["ks"].at[which, n, k - 1], ref["kr"].at[which, n, k - 1], half_peer(k))
+
+    for n in range(per):
+        here = slice(n * CT, (n + 1) * CT)
+        key[:rows, here] = full_tile(per + n).astype(BF)
+        for k in range(1, half):
+            kv_copy(0, n, k).start()
+        value[:rows, here] = (full_tile(2 * per + n) + vector(QV + 1)[:, here]).astype(BF)
+        for k in range(1, half):
+            kv_copy(1, n, k).start()
+    for n in range(per):
+        here = slice(n * CT, (n + 1) * CT)
+        query[:, here] = (full_tile(n) + vector(QV)[:, here]).astype(BF)
+    store(weights["qkv"], ref["o_qkv"])
+    store(query, ref["o_query"])
+
+    pairs = W // 128
+    QT = min(256, rows)
+    x_step(PROJ)
+    y_step(UP_B2)
+
+    def attend(p, _):
+        for n in range(per):
+            @pl.when(p == n * (pairs // per))
+            def _():
+                for k in range(1, half):
+                    kv_copy(0, n, k).wait()
+                    kv_copy(1, n, k).wait()
+
+        for at, steps in (
+            (1, ((z_step, UP_A), (c_step, PROJ), (y_step, DOWN_A))),
+            (4, ((z_step, UP_B2), (x_step, UP_A))),
+            (6, ((z_step, DOWN_A),)),
+            (7, ((x_step, UP_B2), (c_step, UP_A))),
+        ):
+            @pl.when(p == at)
+            def _():
+                for step, m in steps:
+                    step(m)
+
+        lane = lax.broadcasted_iota(jnp.int32, (1, 128), 1)
+        cols = pl.ds(pl.multiple_of(p * 128, 128), 128)
+        key_p, value_p = key[:, cols], value[:, cols]
+        value_t = value_p.T
+        for t in range(rows // QT):
+            tile = slice(t * QT, (t + 1) * QT)
+            q_tile = query[tile, cols] * BF(HEAD_DIM**-0.5)
+            parts = []
+            for head in range(2):
+                owned = (lane < HEAD_DIM) if head == 0 else (lane >= HEAD_DIM)
+                scores = matmul(key_p, jnp.where(owned, q_tile, BF(0)), ((1,), (1,)))
+                highest = jnp.max(scores, axis=0, keepdims=True)
+                expos = jnp.exp(scores - highest)
+                denom = jnp.sum(expos, axis=0, keepdims=True)
+                probs = (expos * (1.0 / denom)).astype(BF)
+                lse[p, head : head + 1, tile] = highest + jnp.log(denom)
+                lanes = slice(head * HEAD_DIM, (head + 1) * HEAD_DIM)
+                parts.append(matmul(value_t[lanes, :], probs))
+            attended[tile, cols] = jnp.concatenate(parts, axis=0).T.astype(BF)
+        return 0
+
+    lax.fori_loop(0, pairs, attend, 0)
+    store(key, ref["o_key"])
+    store(value, ref["o_value"])
+    store(attended, ref["o_attended"])
+    own_loads["proj"].wait()
+    own_sends["proj"].wait()
+    store(weights["proj"], ref["o_proj"])
+
+    branch, second = ref["branch_s"], ref["second_s"]
+    MT = min(256, rows)
+
+    def branch_tile(t, _):
+        tile = pl.ds(pl.multiple_of(t * MT, MT), MT)
+        low = matmul(attended[tile, :], weights["proj"][...]) + vector(PROJ_B)
+        branch[tile, :] = low
+        unit, _ = norm_parts(x_s[tile, :].astype(F32) + vector(ATTN_SCALE) * low)
+        second[tile, :] = (unit * vector(MLP_GAIN) + vector(MLP_SHIFT)).astype(BF)
+        return 0
+
+    lax.fori_loop(0, rows // MT, branch_tile, 0)
+    store(branch, ref["o_branch"])
+    store(second, ref["o_second"])
+    cot_load.wait()
+    cot_swap.wait()
+    store(cot_s, ref["o_cot"])
+    x_step(DOWN_A)
+    y_step(DOWN_B2)
+    own_loads["up"].wait()
+    own_sends["up"].wait()
+    c_step(UP_B2)
+    store(weights["up"], ref["o_up"])
+
+    FT = ref["act_s"].shape[2]
+
+    def act_store(i, which):
+        name = ("act", "slope")[which]
+        return pltpu.make_async_copy(
+            ref[name + "_s"].at[lax.rem(i, 2)],
+            ref["o_" + name].at[:, pl.ds(pl.multiple_of(i * FT, FT), FT)],
+            ref["asem"].at[which, lax.rem(i, 2)],
+        )
+
+    steps = FF // FT
+
+    def up_tile(i, _):
+        @pl.when(i >= 2)
+        def _():
+            act_store(i - 2, 0).wait()
+            act_store(i - 2, 1).wait()
+
+        cols = pl.ds(pl.multiple_of(i * FT, FT), FT)
+        bias = vec[pl.ds(UP_B + lax.div(i * FT, W), 1), pl.ds(pl.multiple_of(lax.rem(i * FT, W), FT), FT)]
+        for t in range(rows // MT):
+            tile = slice(t * MT, (t + 1) * MT)
+            hidden = matmul(second[tile, :], weights["up"][:, cols]) + bias
+            gate = 0.5 * (1.0 + lax.erf(hidden * (0.5**0.5)))
+            ref["act_s"][lax.rem(i, 2), tile, :] = (hidden * gate).astype(BF)
+            bell = jnp.exp(-0.5 * hidden * hidden) * 0.3989422804014327
+            ref["slope_s"][lax.rem(i, 2), tile, :] = (gate + hidden * bell).astype(BF)
+        act_store(i, 0).start()
+        act_store(i, 1).start()
+        return 0
+
+    lax.fori_loop(0, steps, up_tile, 0)
+    c_step(DOWN_A)
+    c_step(DOWN_B2)
+    own_loads["down"].wait()
+    own_sends["down"].wait()
+    store(weights["down"], ref["o_down"])
+    for i in range(steps - 2, steps):
+        act_store(i, 0).wait()
+        act_store(i, 1).wait()
+    for copy in stores:
+        copy.wait()
+
+
+def forward(replicas, shards, tokens, cotangent, shards_of, packed, live, multiples):
+    Y, Z, half = shards // 2, replicas // 2, shards // 2
+    _, R, W = tokens.shape
+    rows, keys = 2 * R, half * 2 * R
+    FF = shards_of["up"].shape[1]
+    size = {name: shards_of[name].shape[0] for name in WEIGHTS}
+    q, p, u, d = (size[name] for name in WEIGHTS)
+    items = (
+        ("qkv", 0, q // 2, False), ("qkv", q // 2, q // 2, True), ("proj", 0, p, False),
+        ("up", 0, u // 2, False), ("up", u // 2, u // 2, False),
+        ("down", 0, d // 2, False), ("down", d // 2, d // 2, True),
+    )
+    FT = min(512, FF)
+    dma = pltpu.SemaphoreType.DMA
+    vmem, anywhere = pl.BlockSpec(memory_space=pltpu.VMEM), pl.BlockSpec(memory_space=pl.ANY)
+    inputs = dict(tokens=tokens, cotangent=cotangent, packed=packed, live=live, **shards_of)
+    outs = {
+        "o_qkv": ((W, 3 * W), BF), "o_proj": ((W, W), BF), "o_up": ((W, FF), BF), "o_down": ((FF, W), BF),
+        "o_act": ((rows, FF), BF), "o_slope": ((rows, FF), BF), "o_cot": ((rows, W), BF),
+        "o_x": ((rows, W), BF), "o_branch": ((rows, W), F32), "o_second": ((rows, W), BF),
+        "o_attended": ((rows, W), BF), "o_query": ((rows, W), BF), "o_key": ((keys, W), BF),
+        "o_value": ((keys, W), BF), "o_first": ((rows, W), BF),
+        "vec": ((16, W), F32), "lse": ((W // 128, 2, rows), F32),
+    }
+    m, per = len(items), W // min(512, W)
+    scratch = {
+        "w_qkv": pltpu.VMEM((W, 3 * W), BF), "w_proj": pltpu.VMEM((W, W), BF),
+        "w_up": pltpu.VMEM((W, FF), BF), "w_down": pltpu.VMEM((FF, W), BF),
+        "x_s": pltpu.VMEM((rows, W), BF), "cot_s": pltpu.VMEM((rows, W), BF),
+        "first_s": pltpu.VMEM((rows, W), BF), "acc": pltpu.VMEM((rows, 3 * W), F32),
+        "query_s": pltpu.VMEM((rows, W), BF), "key_s": pltpu.VMEM((keys, W), BF),
+        "value_s": pltpu.VMEM((keys, W), BF), "attended_s": pltpu.VMEM((rows, W), BF),
+        "branch_s": pltpu.VMEM((rows, W), F32), "second_s": pltpu.VMEM((rows, W), BF),
+        "act_s": pltpu.VMEM((2, rows, FT), BF), "slope_s": pltpu.VMEM((2, rows, FT), BF),
+        "small_s": pltpu.VMEM((shards,) + packed.shape, BF),
+        "lsem": dma((8,)), "osem": dma((16,)), "asem": dma((2, 2)),
+        "ts": dma((2,)), "tr": dma((2,)),
+        "ss": dma((shards - 1,)), "sr": dma((shards - 1,)),
+        "os": dma((4,)), "or": dma((4,)),
+        "ys": dma((m, Y - 1)), "yr": dma((m, Y - 1)),
+        "zs": dma((m, Y - 1, Z - 1)), "zr": dma((m, Y - 1, Z - 1)),
+        "xs": dma((m, Y - 1)), "xr": dma((m, Y - 1)),
+        "cs": dma((m, Y - 1)), "cr": dma((m, Y - 1)),
+        "ks": dma((2, per, half - 1)), "kr": dma((2, per, half - 1)),
+    }
+    names = tuple(inputs) + tuple(outs) + tuple(scratch)
+    results = pl.pallas_call(
+        functools.partial(forward_kernel, replicas, shards, items, multiples, names),
+        in_specs=[vmem if name == "live" else anywhere for name in inputs],
+        out_specs=[vmem if name in ("vec", "lse") else anywhere for name in outs],
+        out_shape=[jax.ShapeDtypeStruct(*shape) for shape in outs.values()],
+        scratch_shapes=list(scratch.values()),
+        compiler_params=pltpu.CompilerParams(
+            collective_id=0, has_side_effects=True, vmem_limit_bytes=63 * MIB
+        ),
+    )(*inputs.values())
+    return dict(zip((name.removeprefix("o_") for name in outs), results))
+
 
 HBM_INPUTS = ("act", "slope", "cot", "x", "branch", "second", "attended", "query", "key", "value",
               "first", "down", "up", "proj", "qkv")
@@ -457,7 +713,7 @@
 
     def feed_tile(t, _):
         tile = pl.ds(pl.multiple_of(t * TR, TR), TR)
-        value = (cot[tile, :].astype(F32) * vector(V_MLP_SCALE)).astype(BF)
+        value = (cot[tile, :].astype(F32) * vector(LIVE) * vector(MLP_SCALE)).astype(BF)
         gfeed[tile, :] = value
         note(DOWN_B, jnp.sum(value.astype(F32), axis=0, keepdims=True))
         return 0
@@ -506,9 +762,9 @@
     def middle_tile(t, _):
         tile = pl.ds(pl.multiple_of(t * TR, TR), TR)
         low = branch[tile, :]
-        middle = x_s[tile, :].astype(F32) + vector(V_ATTN_SCALE) * low
-        feed = acc[tile, :] + vector(V_DOWN_B)
-        result = ((middle + vector(V_MLP_SCALE) * feed) * vector(V_LIVE)).astype(BF)
+        middle = x_s[tile, :].astype(F32) + vector(ATTN_SCALE) * low
+        feed = acc[tile, :] + vector(DOWN_B)
+        result = ((middle + vector(MLP_SCALE) * feed) * vector(LIVE)).astype(BF)
         lower = pl.ds(pl.multiple_of(lax.rem(t * TR, R), TR), TR) if R >= TR else pl.ds(0, R)
         if R >= TR:
             @pl.when(t * TR < R)
@@ -521,16 +777,16 @@
         else:
             tok_out[mine] = result[:R]
             tok_send[...] = result[R:]
-        upstream = cot[tile, :].astype(F32)
+        upstream = cot[tile, :].astype(F32) * vector(LIVE)
         note(MLP_SCALE, jnp.sum(upstream * feed, axis=0, keepdims=True))
         unit, scale = norm_parts(middle)
         grad = gmid[tile, :]
         note(MLP_GAIN, jnp.sum(grad * unit, axis=0, keepdims=True))
         note(MLP_SHIFT, jnp.sum(grad, axis=0, keepdims=True))
-        grad = upstream + norm_back(grad, unit, scale, vector(V_MLP_GAIN))
+        grad = upstream + norm_back(grad, unit, scale, vector(MLP_GAIN))
         gmid[tile, :] = grad
         note(ATTN_SCALE, jnp.sum(grad * low, axis=0, keepdims=True))
-        grad = (grad * vector(V_ATTN_SCALE)).astype(BF)
+        grad = (grad * vector(ATTN_SCALE)).astype(BF)
         gbranch[tile, :] = grad
         note(PROJ_B, jnp.sum(grad.astype(F32), axis=0, keepdims=True))
         gatt[tile, :] = matmul(grad, ref["proj_s"][...], ((1,), (1,))).astype(BF)
@@ -661,7 +917,7 @@
         note(ATTN_SHIFT, jnp.sum(grad, axis=0, keepdims=True))
         note(QV, jnp.sum(G[tile, :W].astype(F32), axis=0, keepdims=True))
         note(QV + 1, jnp.sum(G[tile, 2 * W :].astype(F32), axis=0, keepdims=True))
-        whole = gmid[tile, :] + norm_back(grad, unit, scale, vector(V_ATTN_GAIN))
+        whole = gmid[tile, :] + norm_back(grad, unit, scale, vector(ATTN_GAIN))
         if R >= TR:
             lower = pl.ds(pl.multiple_of(lax.rem(t * TR, R), TR), TR)
 
@@ -808,71 +1064,17 @@
               cotangent, image_count):
     vectors = (qv_bias, proj_bias, up_bias, down_bias, attn_gain, attn_shift, mlp_gain, mlp_shift,
                attn_scale, mlp_scale)
-    lengths = [v.shape[0] for v in vectors]
-    n_small = sum(lengths)
-    padded = -(-n_small // 2048) * 2048
-    packed = jnp.pad(jnp.concatenate(vectors), (0, padded - n_small)).reshape(16, padded // 16)
-    qkv_all, proj_all, up_all, down_all, small_all = gather_weights(
-        replicas, shards, (qkv_weight, proj_weight, up_weight, down_weight), packed
-    )
     width = tokens.shape[2]
-    qkv_full, proj_full = qkv_all.reshape(width, -1), proj_all.reshape(width, -1)
-    up_full, down_full = up_all.reshape(width, -1), down_all.reshape(-1, width)
-    small_flat = small_all.reshape(shards, padded)
-    full, place = [], 0
-    for n in lengths:
-        full.append(small_flat[:, place : place + n].reshape(-1).astype(F32))
-        place += n
-    (qv_shift, proj_shift, up_shift, down_shift, gain_first, shift_first, gain_second, shift_second,
-     scale_first, scale_second) = full
-
-    half = shards // 2
+    piece = width // shards
+    multiples = tuple(v.shape[0] // piece for v in vectors)
+    packed = jnp.pad(jnp.concatenate(vectors).reshape(-1, piece), ((0, 16 - sum(multiples)), (0, 0)))
     shard = lax.axis_index("shard")
-    mine = lax.div(shard, half)
-    swap = [(i, (i + half) % shards) for i in range(shards)]
-
-    def join(array):
-        keep = lax.dynamic_index_in_dim(array, mine, 0, keepdims=False)
-        give = lax.dynamic_index_in_dim(array, 1 - mine, 0, keepdims=False)
-        return jnp.concatenate([keep, lax.ppermute(give, "shard", swap)], axis=0)
-
-    joined = join(tokens)
-    inputs = joined.astype(F32)
-    live = mine < image_count[lax.axis_index("replica")]
-    upstream = jnp.where(live, join(cotangent), BF(0))
-    groups = [list(range(half)), list(range(half, shards))]
-    other = [(i, i ^ 1) for i in range(shards)]
-
-    def all_rows(array):
-        if half == 2:
-            return jnp.concatenate([array, lax.ppermute(array, "shard", other)], axis=0)
-        whole = lax.all_gather(array, "shard", axis=0, tiled=True, axis_index_groups=groups)
-        return jnp.roll(whole, -lax.rem(shard, half) * array.shape[0], axis=0)
-
-    unit_first, _ = norm_parts(inputs)
-    normed_low = (unit_first * gain_first + shift_first).astype(BF)
-    projected = matmul(normed_low, qkv_full)
-    queries = (projected[:, :width] + qv_shift[:width]).astype(BF)
-    keys = projected[:, width : 2 * width].astype(BF)
-    values = (projected[:, 2 * width :] + qv_shift[width:]).astype(BF)
-    keys_all, values_all = all_rows(keys), all_rows(values)
-    attended, lse = attention_forward(queries, keys_all, values_all)
-    branch = matmul(attended, proj_full) + proj_shift
-    middle = inputs + scale_first * branch
-    unit_second, _ = norm_parts(middle)
-    second_low = (unit_second * gain_second + shift_second).astype(BF)
-    hidden = matmul(second_low, up_full) + up_shift
-    gate = 0.5 * (1.0 + lax.erf(hidden * (0.5**0.5)))
-    act = (hidden * gate).astype(BF)
-    slope = (gate + hidden * (jnp.exp(-0.5 * hidden * hidden) * 0.3989422804014327)).astype(BF)
-
-    vec = jnp.stack([scale_second, gain_second, scale_first, gain_first, down_shift,
-                     jnp.broadcast_to(live.astype(F32), (width,))])
-    vec = jnp.concatenate([vec, jnp.zeros((2, width), F32)])
-    hbm = dict(act=act, slope=slope, cot=upstream, x=joined, branch=branch, second=second_low,
-               attended=attended, query=queries, key=keys_all, value=values_all, first=normed_low,
-               down=down_full, up=up_full, proj=proj_full, qkv=qkv_full)
-    grads, small, output, grad_tokens = backward(replicas, shards, hbm, vec, lse)
+    live = lax.div(shard, shards // 2) < image_count[lax.axis_index("replica")]
+    live = jnp.broadcast_to(live.astype(F32), (8, width))
+    shards_of = dict(qkv=qkv_weight, proj=proj_weight, up=up_weight, down=down_weight)
+    kept = forward(replicas, shards, tokens, cotangent, shards_of, packed, live, multiples)
+    hbm = {name: kept[name] for name in HBM_INPUTS}
+    grads, small, output, grad_tokens = backward(replicas, shards, hbm, kept["vec"], kept["lse"])
     grad_down, grad_up, grad_proj, grad_qkv = grads
 
     def own(row, count=1):
@@ -881,8 +1083,8 @@
         return lax.dynamic_slice_in_dim(whole, shard * size, size)
 
     return (output, grad_tokens, grad_qkv, own(QV, 2), grad_proj, own(PROJ_B), grad_up,
-            own(UP_B, up_bias.shape[0] * shards // width), grad_down, own(DOWN_B), own(ATTN_GAIN),
-            own(ATTN_SHIFT), own(MLP_GAIN), own(MLP_SHIFT), own(ATTN_SCALE), own(MLP_SCALE))
+            own(UP_B, DOWN_B - UP_B), grad_down, own(DOWN_B), own(ATTN_GAIN), own(ATTN_SHIFT), own(MLP_GAIN),
+            own(MLP_SHIFT), own(ATTN_SCALE), own(MLP_SCALE))
 
 
 def solution(mesh):

time: 502 us -> 365 us (0.73)
  Pallas kernels: 421 us -> 324 us
  matrix products: 18.8 us -> 0 us
  other arithmetic: 16 us -> 4.56 us
  waiting for transfers between devices: 9.82 us -> 0 us
    pallas_call x2 -> x1, Pallas kernels: 216 us -> 116 us  [forward(): pl.pallas_call(functools.partial(forward_kernel, replicas, shards, items,...]
    dot_general x3 -> x0, matrix products: 18.8 us -> none  [matmul(): lax.dot_general(left, right, (dims, ((), ())), preferred_element_type=F32)]
    ppermute x4 -> x0, waiting for transfers between devices: 9.82 us -> none  [the longest x2 9.82 us: join(): return jnp.concatenate([keep, lax.ppermute(give, 'shard', swap)], axis=0)]
    concatenate x3 -> x0, other arithmetic: 5.47 us -> none  [the longest x2 4.43 us: all_rows(): return jnp.concatenate([array, lax.ppermute(array, 'shard', other)], axis=0)]
    unnamed x86 -> x22, local copies, waits for them, and re-layouts: 9.95 us -> 15.1 us
  transfers between devices with their start and end apart: 4 -> 0, of which waited for: 1 -> 0; matrix products, arithmetic and copies ran while one was open for 2% -> 0% of each run, Pallas kernels for 39% -> 0%
where the time goes in v3:
time: 365 us; the launch traced here: 364 us
  Pallas kernels  324 us (89%)
  local copies, waits for them, and re-layouts  34.3 us (9%)
  other arithmetic  4.56 us (1%)
    pallas_call x1, Pallas kernels, backward(): pl.pallas_call(functools.partial(backward_kernel, replicas, shards, names...  208 us
    pallas_call x1, Pallas kernels, forward(): pl.pallas_call(functools.partial(forward_kernel, replicas, shards, items,...  116 us
    unnamed x22, local copies, waits for them, and re-layouts  15.1 us

profile of v3, /device:TPU:0, one launch (start us, length us, event | category | flops | bytes accessed | tf_op | source)
XLA Modules:
  0.0 364.3 jit_solution(7006504810123494165)
XLA Ops:
  0.7 1.2 dynamic_slice.49
  2.5 0.6 broadcast_in_dim.3.refs_3_
  3.2 0.9 dynamic-update-slice
  4.0 0.8 dynamic-update-slice.1
  4.9 0.8 dynamic-update-slice.2
  5.7 0.8 dynamic-update-slice.3
  6.5 0.8 dynamic-update-slice.4
  7.4 0.8 dynamic-update-slice.5
  8.2 0.8 dynamic-update-slice.6
  9.0 0.8 dynamic-update-slice.7
  9.9 0.8 dynamic-update-slice.8
  10.7 0.8 dynamic-update-slice.9
  11.5 0.6 pad.4.refs_2_
  12.2 115.8 %shard_map.288 = (bf16[1024,3072]{1,0:T(8,128)(2,1)}, bf16[1024,1024]{1,0:T(8,128)(2,1)}, bf16[1024,4096]{1,0:T(8,128)(2,1)}, bf16[4096,1024]{1,0:T(8,128)(2,1)}...) custom-call(bf16[2,256,1024]{2,1,0:T(8,128)(2,1)} %refs_0_.1, ...), custom_call_target="tpu_custom_call" | custom-call | tf_op jit(solution)/shard_map/pallas_call | solution.py:486
  127.9 208.2 %shard_map.289 = (bf16[24,128,1024]{2,1,0:T(8,128)(2,1)}, f32[16,1024]{1,0:T(8,128)}, bf16[2,256,1024]{2,1,0:T(8,128)(2,1)}, f32[2,256,1024]{2,1,0:T(8,128)}) custom-call(bf16[512,4096]{1,0:T(8,128)(2,1)} %get-tuple-element.37.refs_0_, bf16[512,4096]{1,0:T(8,128)(2,1)} %get-tuple-element.38.refs_1_, bf16[512,1024]{1,0:T(8,128)(2,1)} %get-tuple-element.39.refs_2_, ...), custom_call_target="tpu_custom_call" | custom-call | tf_op jit(solution)/shard_map/pallas_call | solution.py:1044
  336.2 1.0 fusion.1
  337.2 0.6 constant_dynamic-slice_fusion
  337.8 0.6 constant_dynamic-slice_fusion.2
  338.4 0.6 constant_dynamic-slice_fusion.4
  338.9 0.6 constant_dynamic-slice_fusion.6
  339.5 4.0 %fusion = (bf16[8,128,1024]{2,1,0:T(8,128)(2,1)}, bf16[8,128,1024]{2,1,0:T(8,128)(2,1)S(1)}) fusion(bf16[24,128,1024]{2,1,0:T(8,128)(2,1)} %get-tuple-element.56), kind=kLoop, calls=%fused_computation.16 | loop fusion | bytes 8388608 | tf_op jit(solution)/shard_map/slice | solution.py:1056
  343.5 0.4 convert_bitcast_fusion
  344.0 2.3 copy.38
  346.3 1.6 slice.42
  347.9 0.4 bitcast_convert_fusion.1
  348.2 2.4 copy.35
  350.6 0.0 copy-start
  350.6 3.7 %copy.37 = f32[256,3072]{1,0:T(8,128)} copy(f32[256,3072]{0,1:T(8,128)} %bitcast.40) | data formatting | bytes 6291456
  354.3 0.0 copy-done
  354.3 2.6 bitcast_convert_fusion
  356.9 0.0 copy-start.2
  356.9 1.2 slice.44
  358.1 0.0 copy-start.1
  358.1 1.1 bitcast_convert_fusion.2
  359.2 0.8 slice_bitcast_fusion
  360.0 0.6 dynamic_slice.53
  360.6 0.8 slice_bitcast_fusion.1
  361.3 0.7 dynamic_slice.50
  362.0 0.0 copy-done.2
  362.0 1.0 copy.57
  363.0 0.0 copy-done.1
  363.0 1.3 copy.58
  (4 shorter events, 0.0 us)
Async XLA Ops:
  350.6 3.7 %copy-start = (bf16[8,128,1024]{2,1,0:T(8,128)(2,1)S(1)}, bf16[8,128,1024]{2,1,0:T(8,128)(2,1)}, u32[]{:S(2)}) copy-start(bf16[8,128,1024]{2,1,0:T(8,128)(2,1)} %get-tuple-element.74) | copy-start | bytes 6291460
  356.9 5.1 %copy-start.2 = (bf16[2,256,1024]{2,1,0:T(8,128)(2,1)S(1)}, bf16[2,256,1024]{2,1,0:T(8,128)(2,1)}, u32[]{:S(2)}) copy-start(bf16[2,256,1024]{2,1,0:T(8,128)(2,1)} %get-tuple-element.108) | copy-start | bytes 3145732
  358.1 4.9 %copy-start.1 = (f32[2,256,1024]{2,1,0:T(8,128)S(1)}, f32[2,256,1024]{2,1,0:T(8,128)}, u32[]{:S(2)}) copy-start(f32[2,256,1024]{2,1,0:T(8,128)} %get-tuple-element.109) | copy-start | bytes 6291460

commit v4 on v2

v4 whole, which is shorter than its diff:
```python
import functools
import types

import jax
import jax.numpy as jnp
from jax import lax
from jax.experimental import pallas as pl
from jax.experimental.pallas import tpu as pltpu
from jax.sharding import PartitionSpec as P

HEAD_DIM = 64
EPS = 1e-06
BF = jnp.bfloat16
F32 = jnp.float32
MESH = pl.DeviceIdType.MESH
MIB = 1024 * 1024
SLOTS = 6
PAIR_SLOTS = 4
CORE_SLOTS = 4
LAG = 2
GLAG = 2


def matmul(left, right, dims=((1,), (0,))):
    return lax.dot_general(left, right, (dims, ((), ())), preferred_element_type=F32)


class Place:
    def __init__(self, replicas, shards):
        self.Z, self.Y = replicas // 2, shards // 2
        self.shards = shards
        replica, shard = lax.axis_index("replica"), lax.axis_index("shard")
        self.x, self.z = lax.rem(replica, 2), lax.div(replica, 2)
        self.c, self.y = lax.rem(shard, 2), lax.div(shard, 2)
        self.s = shard

    def part(self, y, c):
        return y * 2 + c

    def at(self, x=None, z=None, y=None, c=None):
        x = self.x if x is None else x
        z = self.z if z is None else z
        y = self.y if y is None else y
        c = self.c if c is None else c
        return (z * 2 + x, y * 2 + c)

    def ahead_z(self, k):
        return lax.rem(self.z + k, self.Z)

    def behind_z(self, k):
        return lax.rem(self.z + self.Z - k, self.Z)

    def ahead_y(self, k):
        return lax.rem(self.y + k, self.Y)

    def behind_y(self, k):
        return lax.rem(self.y + self.Y - k, self.Y)

    def greet(self, extra=()):
        others = [self.at(c=1 - self.c), self.at(x=1 - self.x)]
        others += [self.at(y=self.ahead_y(k)) for k in range(1, self.Y)]
        others += [self.at(z=self.ahead_z(k)) for k in range(1, self.Z)]
        others += list(extra)
        barrier = pltpu.get_barrier_semaphore()
        for other in others:
            pl.semaphore_signal(barrier, inc=1, device_id=other, device_id_type=MESH)
        pl.semaphore_wait(barrier, len(others))


def send(src, dst, send_sem, recv_sem, device):
    return pltpu.make_async_remote_copy(
        src_ref=src,
        dst_ref=dst,
        send_sem=send_sem,
        recv_sem=recv_sem,
        device_id=device,
        device_id_type=MESH,
    )


QV, PROJ_B, UP_B, DOWN_B, ATTN_GAIN, ATTN_SHIFT, MLP_GAIN, MLP_SHIFT, ATTN_SCALE, MLP_SCALE, LIVE = (
    0, 2, 3, 7, 8, 9, 10, 11, 12, 13, 14)
QKV, PROJ, UP, DOWN = range(4)


def norm_parts(values):
    centre = values - jnp.mean(values, axis=-1, keepdims=True)
    scale = lax.rsqrt(jnp.mean(centre * centre, axis=-1, keepdims=True) + EPS)
    return centre * scale, scale


def norm_back(grad, unit, scale, gain):
    inner = grad * gain
    return scale * (
        inner
        - jnp.mean(inner, axis=-1, keepdims=True)
        - unit * jnp.mean(inner * unit, axis=-1, keepdims=True)
    )


BW = 128


def gather_items(replicas, shards, width, hidden):
    Z = replicas // 2
    step = max(512, 128 * Z)
    size, down = width // shards, hidden // shards
    staged = [(QKV, 0, size, (1 + n) * width + h * step, step) for h in range(width // step) for n in range(2)]
    direct = [(QKV, 0, size, h * step, step) for h in range(width // step)]
    staged += [(PROJ, 0, size, h * step, step) for h in range(width // step)]
    need, known = [], set()
    for b in range(down // BW):
        for p in range(shards):
            c = (p * down + b * BW) // step
            if c not in known:
                known.add(c)
                staged.append((UP, 0, size, c * step, step))
        staged.append((DOWN, b * BW, BW, 0, width))
        need.append(len(staged))
    return staged, direct, need


def layer_kernel(replicas, shards, multiples, names, *refs):
    vector_refs, refs = refs[: len(multiples)], refs[len(multiples) :]
    ref = types.SimpleNamespace(**dict(zip(names, refs)))
    place = Place(replicas, shards)
    Y, Z, s = place.Y, place.Z, place.s
    half = shards // 2
    part, crecv, ysum, yrecv = ref.part, ref.crecv, ref.ysum, ref.yrecv
    xsum, xrecv, zsum, zrecv = ref.xsum, ref.xrecv, ref.zsum, ref.zrecv
    out, small, vec, lse = ref.out, ref.small_buf, ref.vec, ref.lse
    CB, CW = part.shape[3], part.shape[4]
    rows, W = ref.gfeed.shape
    R = rows // 2
    keys = half * rows
    FF = ref.gpre.shape[1]
    down_rows, other_rows = FF // shards, W // shards
    n_blocks, blocks = down_rows // BW, other_rows // CB
    per_block = (BW // CB) * (W // CW)
    n_down, n_up = n_blocks * per_block, blocks * (FF // CW)
    n_proj, n_qkv = blocks * (W // CW), blocks * (3 * W // CW)
    total = n_down + n_up + n_proj + n_qkv
    mine = lax.div(s, half)
    j_half = lax.rem(s, half)
    replica = lax.axis_index("replica")
    kv, gpre, cot, gfeed, G = ref.kv, ref.gpre, ref.cot_s, ref.gfeed, ref.G
    second, first, query, x_s = ref.second_s, ref.first_s, ref.query_s, ref.x_s
    attended, branch, gbranch, gatt = ref.attended_s, ref.branch_s, ref.gbranch, ref.gatt
    TR, MT, QT = min(128, R), min(256, rows), min(256, rows)
    pairs, tiles = W // 128, rows // QT

    def half_peer(k):
        return (replica, mine * half + lax.rem(j_half + k, half))

    swap_peer = (replica, lax.rem(s + half, shards))

    def load(src, dst, sem):
        return pltpu.make_async_copy(src, dst, sem)

    sources = (ref.qkv, ref.proj, ref.up, ref.down)
    weights = (ref.g_qkv, ref.g_proj, ref.g_up, ref.g_down)
    sizes = [source.shape[0] for source in sources]
    bounce = (G, gbranch, gpre, ref.proj_s)

    def own_rows(w):
        return weights[w].at[pl.ds(pl.multiple_of(s * sizes[w], sizes[w]), sizes[w])]

    own_loads = [load(sources[w], bounce[w].at[pl.ds(0, sizes[w])], ref.lsem.at[w]) for w in range(4)]
    own_stores = [load(bounce[w].at[pl.ds(0, sizes[w])], own_rows(w), ref.lsem.at[4 + w]) for w in range(4)]
    x_load = load(ref.tokens.at[mine], x_s.at[pl.ds(0, R)], ref.lsem.at[8])
    cot_load = load(ref.cotangent.at[mine], cot.at[pl.ds(0, R)], ref.lsem.at[9])
    x_load.start()
    for copy in own_loads:
        copy.start()
    cot_load.start()
    row = 0
    for vector_ref, count in zip(vector_refs, multiples):
        values = vector_ref[...].astype(F32).reshape(count, ref.small_s.shape[2])
        ref.small_s[s, row : row + count, :] = values
        row += count
    place.greet([(replica, lax.rem(s + k, shards)) for k in range(1, shards)])

    staged, direct, need = gather_items(replicas, shards, W, FF)
    items = staged + direct
    n_staged = len(staged)

    def piece(m, owner, whole_rows, whole_cols):
        w, row, size, col, width = items[m]
        at = owner * sizes[w] + row
        if not whole_rows:
            at, size = at + place.x * (size // 2), size // 2
        at = pl.ds(pl.multiple_of(at, 16), size)
        if whole_cols:
            return at, pl.ds(col, width)
        return at, pl.ds(pl.multiple_of(col + place.z * (width // Z), 128), width // Z)

    def gy_copy(m, k):
        w, whole = items[m][0], m >= n_staged
        return send(sources[w].at[piece(m, 0, whole, whole)], weights[w].at[piece(m, s, whole, whole)],
                    ref.gys.at[m, k - 1], ref.gyr.at[m, k - 1], place.at(y=place.ahead_y(k)))

    def gathered(m, k, whole_rows, whole_cols):
        owner = place.part(place.behind_y(k), place.c)
        return weights[items[m][0]].at[piece(m, owner, whole_rows, whole_cols)]

    def gz_copy(m, k, j):
        b = gathered(m, k, False, False)
        return send(b, b, ref.gzs.at[m, k - 1, j - 1], ref.gzr.at[m, k - 1, j - 1],
                    place.at(z=place.ahead_z(j)))

    def gx_copy(m, k):
        b = gathered(m, k, False, True)
        return send(b, b, ref.gxs.at[m, k - 1], ref.gxr.at[m, k - 1], place.at(x=1 - place.x))

    def gc_copy(m, k):
        b = gathered(m, k, True, True)
        return send(b, b, ref.gcs.at[m, k - 1], ref.gcr.at[m, k - 1], place.at(c=1 - place.c))

    def gy_start(m):
        for k in range(1, Y):
            gy_copy(m, k).start()

    def direct_arrived(h):
        for k in range(1, Y):
            gy_copy(n_staged + h, k).wait()
            gc_copy(n_staged + h, k).start()

    def arrived(m):
        for k in range(1, Y):
            gc_copy(m, k).wait()

    early = 2 * (W // CW)
    ahead = early + 2

    def gather_tick(t):
        if early <= t + ahead < n_staged:
            gy_start(t + ahead)
        if t < n_staged:
            for k in range(1, Y):
                gy_copy(t, k).wait()
                for j in range(1, Z):
                    gz_copy(t, k, j).start()
        m = t - GLAG
        if 0 <= m < n_staged:
            for k in range(1, Y):
                for j in range(1, Z):
                    gz_copy(m, k, j).wait()
                gx_copy(m, k).start()
        m = t - 2 * GLAG
        if 0 <= m < n_staged:
            for k in range(1, Y):
                gx_copy(m, k).wait()
                gc_copy(m, k).start()
        m = t - 3 * GLAG
        if 0 <= m < n_staged:
            arrived(m)

    ticked = [0]

    def gather_until(t):
        while ticked[0] < min(t + 3 * GLAG, n_staged + 3 * GLAG):
            gather_tick(ticked[0])
            ticked[0] += 1

    def gather_ticks(count):
        gather_until(ticked[0] + count - 3 * GLAG)

    x_swap = send(ref.tokens.at[1 - mine], x_s.at[pl.ds(R, R)], ref.ts.at[2], ref.tr.at[2], swap_peer)
    cot_swap = send(ref.cotangent.at[1 - mine], cot.at[pl.ds(R, R)], ref.ts.at[3], ref.tr.at[3], swap_peer)
    small_sends = [
        send(ref.small_s.at[s], ref.small_s.at[s], ref.vs.at[k - 1], ref.vr.at[k - 1],
             (replica, lax.rem(s + k, shards)))
        for k in range(1, shards)
    ]
    own_sends = [send(sources[w], own_rows(w), ref.os.at[w], ref.orr.at[w], place.at(c=1 - place.c))
                 for w in range(4)]
    for copy in small_sends:
        copy.start()
    for m in range(early):
        gy_start(m)
    x_swap.start()
    for h in range(W // CW):
        gy_start(n_staged + h)
    for m in range(early, early + 2):
        gy_start(m)
    for copy in own_sends:
        copy.start()

    for copy in small_sends:
        copy.wait()
    vec[...] = jnp.zeros_like(vec)
    row = 0
    for count in multiples:
        pieces = [ref.small_s[p, row + r : row + r + 1, :] for p in range(shards) for r in range(count)]
        for r in range(count):
            vec[row + r : row + r + 1, :] = jnp.concatenate(pieces[r * shards : (r + 1) * shards], axis=1)
        row += count
    live = (mine < ref.count[replica]).astype(F32)
    vec[LIVE : LIVE + 1, :] = jnp.full((1, W), live, F32)

    def vector(row):
        return vec[row : row + 1, :]

    def note(row, value):
        small[0, 0, row : row + 1, :] += value

    def norm_tile(t, _):
        tile = pl.ds(pl.multiple_of(t * TR, TR), TR)
        unit, _ = norm_parts(x_s[tile, :].astype(F32))
        first[tile, :] = (unit * vector(ATTN_GAIN) + vector(ATTN_SHIFT)).astype(BF)
        return 0

    x_load.wait()
    lax.fori_loop(0, R // TR, norm_tile, 0)
    for w in range(4):
        own_loads[w].wait()
        own_stores[w].start()
    gather_ticks(2)
    x_swap.wait()
    cot_swap.start()
    lax.fori_loop(R // TR, rows // TR, norm_tile, 0)
    gather_ticks(2)
    direct_arrived(0)
    gather_until(2)
    for w in (QKV, DOWN):
        own_stores[w].wait()
    own_sends[QKV].wait()

    def kv_copy(which, h, k):
        cols = pl.ds(h * CW, CW)
        return send(kv.at[which, pl.ds(0, rows), cols], kv.at[which, pl.ds((half - k) * rows, rows), cols],
                    ref.ks.at[which, h, k - 1], ref.kr.at[which, h, k - 1], half_peer(k))

    def qkv_tile(n, h, slot):
        return load(ref.g_qkv.at[:, pl.ds(n * W + h * CW, CW)], ref.wu.at[slot, :, pl.ds(0, CW)],
                    ref.qsem.at[slot])

    def project(h):
        here = slice(h * CW, (h + 1) * CW)
        tile_loads = [qkv_tile(1, h, 0), qkv_tile(2, h, 1), qkv_tile(0, h, 0)]
        tile_loads[0].start()
        tile_loads[1].start()
        for n in range(3):
            tile_loads[n].wait()
            for t in range(rows // MT):
                tile = slice(t * MT, (t + 1) * MT)
                value = matmul(first[tile, :], ref.wu[n % 2, :, :CW])
                if n == 0:
                    kv[0, tile, here] = value.astype(BF)
                elif n == 1:
                    kv[1, tile, here] = (value + vector(QV + 1)[:, here]).astype(BF)
                else:
                    query[tile, here] = (value + vector(QV)[:, here]).astype(BF)
            if n < 2:
                for k in range(1, half):
                    kv_copy(n, h, k).start()
            if n == 0:
                tile_loads[2].start()

    def exchanged(h):
        for which in range(2):
            for k in range(1, half):
                kv_copy(which, h, k).wait()

    for k in range(1, Y):
        gc_copy(n_staged, k).wait()
    project(0)

    halves = W // CW
    plan = {}

    def at_pair(p, act):
        plan.setdefault(p, []).append(act)

    if halves > 1:
        def second_half():
            direct_arrived(1)
            gather_until(early)
            arrived(n_staged + 1)
            project(1)

        at_pair(2, second_half)
        at_pair(4, lambda: exchanged(1))
    stop = 2 * halves + halves + 2
    at_pair(5, lambda: gather_until(early + 1))
    at_pair(6, lambda: gather_until(early + 2))
    at_pair(7, lambda: gather_until(stop))
    exchanged(0)

    def attend(p, _):
        for at in sorted(plan):
            @pl.when(p == at)
            def _(at=at):
                for act in plan[at]:
                    act()

        lane = lax.broadcasted_iota(jnp.int32, (1, 128), 1)
        cols = pl.ds(pl.multiple_of(p * 128, 128), 128)
        key, value_t = kv[0, :, cols], kv[1, :, cols].T
        for t in range(tiles):
            tile = slice(t * QT, (t + 1) * QT)
            q_tile = query[tile, cols] * BF(HEAD_DIM**-0.5)
            parts = []
            for head in range(2):
                owned = (lane < HEAD_DIM) if head == 0 else (lane >= HEAD_DIM)
                scores = matmul(key, jnp.where(owned, q_tile, BF(0)), ((1,), (1,)))
                highest = jnp.max(scores, axis=0, keepdims=True)
                expos = jnp.exp(scores - highest)
                denom = jnp.sum(expos, axis=0, keepdims=True)
                probs = (expos * (1.0 / denom)).astype(BF)
                lse[p, head : head + 1, tile] = highest + jnp.log(denom)
                lanes = slice(head * HEAD_DIM, (head + 1) * HEAD_DIM)
                parts.append(matmul(value_t[lanes, :], probs))
            attended[tile, cols] = jnp.concatenate(parts, axis=0).T.astype(BF)
        return 0

    lax.fori_loop(0, pairs, attend, 0)

    gather_until(3 * halves)
    own_stores[PROJ].wait()
    own_sends[PROJ].wait()
    proj_load = load(ref.g_proj, ref.proj_s, ref.lsem.at[10])
    proj_load.start()
    cot_load.wait()
    cot_swap.wait()
    small[0, 0] = jnp.zeros_like(small[0, 0])

    def feed_tile(t, _):
        tile = pl.ds(pl.multiple_of(t * TR, TR), TR)
        value = (cot[tile, :].astype(F32) * vector(LIVE) * vector(MLP_SCALE)).astype(BF)
        gfeed[tile, :] = value
        note(DOWN_B, jnp.sum(value.astype(F32), axis=0, keepdims=True))
        return 0

    lax.fori_loop(0, rows // TR, feed_tile, 0)
    proj_load.wait()

    def branch_tile(t, _):
        tile = pl.ds(pl.multiple_of(t * MT, MT), MT)
        low = matmul(attended[tile, :], ref.proj_s[...]) + vector(PROJ_B)
        branch[tile, :] = low
        unit, _ = norm_parts(x_s[tile, :].astype(F32) + vector(ATTN_SCALE) * low)
        second[tile, :] = (unit * vector(MLP_GAIN) + vector(MLP_SHIFT)).astype(BF)
        return 0

    lax.fori_loop(0, rows // MT, branch_tile, 0)
    for w in (UP, DOWN):
        own_sends[w].wait()
    own_stores[UP].wait()

    def block_loads(b):
        slot = lax.rem(b, 2)
        copies = []
        for p in range(shards):
            at = pl.ds(pl.multiple_of(p * down_rows + b * BW, BW), BW)
            to = pl.ds(p * BW, BW)
            copies.append(load(ref.g_up.at[:, at], ref.wu.at[slot, :, to], ref.wsem.at[0, slot, p]))
            copies.append(load(ref.g_down.at[at], ref.wd.at[slot, to], ref.wsem.at[1, slot, p]))
        return copies

    gather_until(need[0])
    for copy in block_loads(0):
        copy.start()

    def core_copy(i):
        a = lax.rem(i, CORE_SLOTS)
        return send(part.at[lax.rem(i, 2), 1 - place.c], crecv.at[a], ref.cs.at[a], ref.cr.at[a],
                    place.at(c=1 - place.c))

    def y_copy(i, k):
        a = lax.rem(i, SLOTS)
        return send(ysum.at[a, place.ahead_y(k)], yrecv.at[a, k - 1], ref.ys.at[a, k - 1],
                    ref.yr.at[a, k - 1], place.at(y=place.ahead_y(k)))

    def x_copy(i):
        a = lax.rem(i, SLOTS)
        return send(xsum.at[a, 1 - place.x], xrecv.at[a], ref.xs.at[a], ref.xr.at[a],
                    place.at(x=1 - place.x))

    def z_copy(i, k):
        a = lax.rem(i, SLOTS)
        return send(zsum.at[a, place.ahead_z(k)], zrecv.at[a, k - 1], ref.zs.at[a, k - 1],
                    ref.zr.at[a, k - 1], place.at(z=place.ahead_z(k)))

    HB, WZ = CB // 2, CW // Z
    x_rows = pl.ds(pl.multiple_of(place.x * HB, HB), HB)
    z_cols = pl.ds(pl.multiple_of(place.z * WZ, WZ), WZ)

    def zg_copy(i, k):
        a = lax.rem(i, SLOTS)
        block = out.at[i, x_rows, z_cols]
        return send(block, block, ref.gs.at[a, k - 1], ref.gr.at[a, k - 1],
                    place.at(z=place.ahead_z(k)))

    def xg_copy(i):
        a = lax.rem(i, SLOTS)
        block = out.at[i, x_rows]
        return send(block, block, ref.hs.at[a], ref.hr.at[a], place.at(x=1 - place.x))

    def for_store(i, act):
        a = lax.rem(i, SLOTS)
        base = 0
        plan = ((ref.o_down, n_down, False), (ref.o_up, n_up, True), (ref.o_proj, n_proj, False),
                (ref.o_qkv, n_qkv, True))
        for target, count, rows_first in plan:
            u = i - base
            if rows_first:
                r, c = lax.rem(u, blocks), lax.div(u, blocks)
            else:
                r, c = lax.div(u, W // CW), lax.rem(u, W // CW)
            at = (pl.ds(pl.multiple_of(r * CB, CB), CB), pl.ds(pl.multiple_of(c * CW, CW), CW))

            @pl.when((u >= 0) & (u < count))
            def _(target=target, at=at):
                act(load(out.at[i], target.at[at], ref.osem.at[a]))

            base += count

    def add(*terms):
        whole = terms[0].astype(F32)
        for term in terms[1:]:
            whole = whole + term.astype(F32)
        return whole.astype(BF)

    def tick(i):
        def stage(lag):
            j = i - lag
            return j, (j >= 0) & (j < total)

        j1, ok1 = stage(1)

        @pl.when(ok1)
        def _():
            core_copy(j1).wait()
            a = lax.rem(j1, SLOTS)
            for y in range(Y):
                ysum[a, y] = add(part[lax.rem(j1, 2), place.c, y], crecv[lax.rem(j1, CORE_SLOTS), y])
            for k in range(1, Y):
                y_copy(j1, k).start()

        j2, ok2 = stage(1 + LAG)

        @pl.when(ok2)
        def _():
            a = lax.rem(j2, SLOTS)
            for k in range(1, Y):
                y_copy(j2, k).wait()
            for h in range(2):
                piece = slice(h * HB, (h + 1) * HB)
                xsum[a, h] = add(ysum[a, place.y, piece], *[yrecv[a, k - 1, piece] for k in range(1, Y)])
            x_copy(j2).start()

        j3, ok3 = stage(1 + 2 * LAG)

        @pl.when(ok3)
        def _():
            a = lax.rem(j3, SLOTS)
            x_copy(j3).wait()
            for z in range(Z):
                cols = slice(z * WZ, (z + 1) * WZ)
                zsum[a, z] = add(xsum[a, place.x, :, cols], xrecv[a, :, cols])
            for k in range(1, Z):
                z_copy(j3, k).start()

        j4, ok4 = stage(1 + 3 * LAG)

        @pl.when(ok4)
        def _():
            a = lax.rem(j4, SLOTS)
            for k in range(1, Z):
                z_copy(j4, k).wait()
            out[j4, x_rows, z_cols] = add(zsum[a, place.z], *[zrecv[a, k - 1] for k in range(1, Z)])
            for k in range(1, Z):
                zg_copy(j4, k).start()

        j5, ok5 = stage(1 + 4 * LAG)

        @pl.when(ok5)
        def _():
            for k in range(1, Z):
                zg_copy(j5, k).wait()
            xg_copy(j5).start()

        j6, ok6 = stage(1 + 5 * LAG)

        @pl.when(ok6)
        def _():
            xg_copy(j6).wait()
            for_store(j6, lambda copy: copy.start())

        j7, ok7 = stage(2 + 5 * LAG)

        @pl.when(ok7)
        def _():
            for_store(j7, lambda copy: copy.wait())

    def produce(i, left, offset, cols):
        slot = lax.rem(i, 2)
        for turn in range(2):
            c = 1 - place.c if turn == 0 else place.c
            for y in range(Y):
                first = offset(place.part(y, c))
                if CB % 128 == 0:
                    first = pl.multiple_of(first, 128)
                    value = matmul(left[:, pl.ds(first, CB)], cols, ((0,), (0,))).astype(BF)
                else:
                    start = pl.multiple_of(lax.div(first, 128) * 128, 128)
                    ref.tile[...] = matmul(left[:, pl.ds(start, 128)], cols, ((0,), (0,)))
                    value = ref.tile[pl.ds(pl.multiple_of(first - start, CB), CB)].astype(BF)
                part[slot, c, y] = value
            if turn == 0:
                core_copy(i).start()

    def columns(array, n):
        return array[:, pl.ds(pl.multiple_of(n * CW, CW), CW)]

    acc, gmid, act, slope = ref.acc, ref.gmid, ref.act_s, ref.slope_s
    spread = []
    for b in range(n_blocks):
        goal = need[min(b + 1, n_blocks - 1)] + 3 * GLAG
        start = spread[-1][1] if spread else ticked[0]
        left = n_staged + 3 * GLAG - start
        stop = min(max(goal, start + -(-left // max(1, n_blocks - 1 - b))), n_staged + 3 * GLAG)
        spread.append((start, stop))

    def block_step(b, _):
        slot = lax.rem(b, 2)
        for copy in block_loads(b):
            copy.wait()

        for at, (start, stop) in enumerate(spread):
            @pl.when(b == at)
            def _(start=start, stop=stop):
                for t in range(start, stop):
                    gather_tick(t)

        @pl.when(b + 1 < n_blocks)
        def _():
            for copy in block_loads(b + 1):
                copy.start()

        spots = []
        for p in range(shards):
            row, col = UP_B + p * down_rows // W, p * down_rows % W
            spots.append((slice(row, row + 1), pl.ds(pl.multiple_of(col + b * BW, BW), BW)))
        bias = jnp.concatenate([vec[spot] for spot in spots], axis=1)
        for t in range(rows // MT):
            tile = slice(t * MT, (t + 1) * MT)
            hidden = matmul(second[tile, :], ref.wu[slot]) + bias
            gate = 0.5 * (1.0 + lax.erf(hidden * (0.5**0.5)))
            act[tile, :] = (hidden * gate).astype(BF)
            bell = jnp.exp(-0.5 * hidden * hidden) * 0.3989422804014327
            slope[tile, :] = gate + hidden * bell

        def chunk(n):
            r, c = n // (W // CW), n % (W // CW)
            produce(b * per_block + n, act, lambda p: p * BW + r * CB, columns(gfeed, c))
            tick(b * per_block + n)

        chunk(0)
        sums = [0.0] * shards
        for t in range(rows // MT):
            tile = slice(t * MT, (t + 1) * MT)
            pre = (matmul(gfeed[tile, :], ref.wd[slot], ((1,), (1,))) * slope[tile, :]).astype(BF)
            for p in range(shards):
                mid = pre[:, p * BW : (p + 1) * BW]
                gpre[tile, pl.ds(pl.multiple_of(p * down_rows + b * BW, BW), BW)] = mid
                sums[p] = sums[p] + jnp.sum(mid.astype(F32), axis=0, keepdims=True)
            more = matmul(pre, ref.wu[slot], ((1,), (1,)))
            feed = matmul(act[tile, :], ref.wd[slot])

            @pl.when(b == 0)
            def _():
                gmid[tile, :] = more
                acc[tile, :] = feed

            @pl.when(b > 0)
            def _():
                gmid[tile, :] += more
                acc[tile, :] += feed

            if t == 0:
                for n in range(1, per_block):
                    chunk(n)
        for p in range(shards):
            row, cols = spots[p]
            small[0, 0, row, cols] = sums[p]
        return 0

    lax.fori_loop(0, n_blocks, block_step, 0)

    tok_out, tok_send = ref.tok_out, ref.tok_send

    def to_owner(t, value, kept, given):
        if R >= TR:
            lower = pl.ds(pl.multiple_of(lax.rem(t * TR, R), TR), TR)

            @pl.when(t * TR < R)
            def _():
                kept[mine, lower, :] = value.astype(kept.dtype)

            @pl.when(t * TR >= R)
            def _():
                given[lower, :] = value.astype(BF)
        else:
            kept[mine] = value[:R].astype(kept.dtype)
            given[...] = value[R:].astype(BF)

    def middle_tile(t, _):
        tile = pl.ds(pl.multiple_of(t * TR, TR), TR)
        low = branch[tile, :]
        middle = x_s[tile, :].astype(F32) + vector(ATTN_SCALE) * low
        feed = acc[tile, :] + vector(DOWN_B)
        to_owner(t, (middle + vector(MLP_SCALE) * feed) * vector(LIVE), tok_out, tok_send)
        upstream = cot[tile, :].astype(F32) * vector(LIVE)
        note(MLP_SCALE, jnp.sum(upstream * feed, axis=0, keepdims=True))
        unit, scale = norm_parts(middle)
        grad = gmid[tile, :]
        note(MLP_GAIN, jnp.sum(grad * unit, axis=0, keepdims=True))
        note(MLP_SHIFT, jnp.sum(grad, axis=0, keepdims=True))
        grad = upstream + norm_back(grad, unit, scale, vector(MLP_GAIN))
        gmid[tile, :] = grad
        note(ATTN_SCALE, jnp.sum(grad * low, axis=0, keepdims=True))
        grad = (grad * vector(ATTN_SCALE)).astype(BF)
        gbranch[tile, :] = grad
        note(PROJ_B, jnp.sum(grad.astype(F32), axis=0, keepdims=True))
        gatt[tile, :] = matmul(grad, ref.proj_s[...], ((1,), (1,))).astype(BF)
        return 0

    lax.fori_loop(0, rows // TR, middle_tile, 0)
    tok_copy = send(tok_send, tok_out.at[mine], ref.ts.at[0], ref.tr.at[0], swap_peer)
    tok_copy.start()

    def qkv_load(n):
        slot = lax.rem(n, 2)
        return load(ref.g_qkv.at[:, pl.ds(pl.multiple_of(n * CW, CW), CW)], ref.wu.at[slot, :, pl.ds(0, CW)],
                    ref.qsem.at[slot])

    pown, psend, precv = ref.pown, ref.psend, ref.precv
    gk_acc, gv_acc = ref.gk_acc, ref.gv_acc

    def pair_copy(p, k):
        a = lax.rem(p, PAIR_SLOTS)
        return send(psend.at[a, k - 1], precv.at[a, k - 1], ref.ps.at[a, k - 1], ref.pr.at[a, k - 1],
                    half_peer(k))

    def pair_done(p):
        a = lax.rem(p, PAIR_SLOTS)
        for k in range(1, half):
            pair_copy(p, k).wait()
        for which in range(2):
            whole = pown[a, which]
            for k in range(1, half):
                whole = whole + precv[a, k - 1, which].astype(F32)
            cols = pl.ds(pl.multiple_of((which + 1) * W + p * 128, 128), 128)
            G[:, cols] = whole.astype(BF)

    def up_chunk(u):
        i = n_down + u
        b, n = lax.rem(u, blocks), lax.div(u, blocks)
        produce(i, second, lambda p: p * other_rows + b * CB, columns(gpre, n))
        tick(i)

    per_pair = n_up // pairs

    def pair_step(p, _):
        if per_pair:
            for m in range(max(1, per_pair - tiles + 1)):
                up_chunk(p * per_pair + m)
        else:
            @pl.when(lax.rem(p, pairs // n_up) == 0)
            def _():
                up_chunk(lax.div(p, pairs // n_up))

        lane = lax.broadcasted_iota(jnp.int32, (1, 128), 1)
        cols = pl.ds(pl.multiple_of(p * 128, 128), 128)
        key, value = kv[0, :, cols], kv[1, :, cols]
        key_t = key.T
        for t in range(tiles):
            tile = slice(t * QT, (t + 1) * QT)
            q_tile, g_tile = query[tile, cols], gatt[tile, cols]
            parts = []
            for head in range(2):
                owned = (lane < HEAD_DIM) if head == 0 else (lane >= HEAD_DIM)
                own = jnp.where(owned, q_tile * BF(HEAD_DIM**-0.5), BF(0))
                own_grad = jnp.where(owned, g_tile, BF(0))
                probs = jnp.exp(matmul(key, own, ((1,), (1,))) - lse[p, head : head + 1, tile])
                grad_probs = matmul(value, own_grad, ((1,), (1,)))
                centre = jnp.sum(grad_probs * probs, axis=0, keepdims=True)
                grad_scores = (probs * (grad_probs - centre)).astype(BF)
                gv = matmul(probs.astype(BF), own_grad)
                gk = matmul(grad_scores, own)
                if t == 0 and head == 0:
                    gv_acc[...], gk_acc[...] = gv, gk
                else:
                    gv_acc[...] += gv
                    gk_acc[...] += gk
                lanes = slice(head * HEAD_DIM, (head + 1) * HEAD_DIM)
                parts.append(matmul(key_t[lanes, :], grad_scores))
            whole = jnp.concatenate(parts, axis=0) * (HEAD_DIM**-0.5)
            G[tile, cols] = whole.T.astype(BF)
            if per_pair and t < tiles - 1:
                up_chunk(p * per_pair + max(1, per_pair - tiles + 1) + t)
        a = lax.rem(p, PAIR_SLOTS)
        pown[a, 0], pown[a, 1] = gk_acc[:rows], gv_acc[:rows]
        for k in range(1, half):
            psend[a, k - 1, 0] = gk_acc[k * rows : (k + 1) * rows].astype(BF)
            psend[a, k - 1, 1] = gv_acc[k * rows : (k + 1) * rows].astype(BF)
            pair_copy(p, k).start()

        @pl.when(p >= 1)
        def _():
            pair_done(p - 1)
        return 0

    lax.fori_loop(0, pairs, pair_step, 0)

    qkv_load(0).start()

    def proj_step(u, _):
        i = n_down + n_up + u
        r, c = lax.div(u, W // CW), lax.rem(u, W // CW)
        produce(i, attended, lambda p: p * other_rows + r * CB, columns(gbranch, c))
        tick(i)

        @pl.when(u == 0)
        def _():
            pair_done(pairs - 1)
        return 0

    lax.fori_loop(0, n_proj, proj_step, 0)

    def qkv_step(n, _):
        cols = columns(G, n)
        for b in range(blocks):
            i = n_down + n_up + n_proj + n * blocks + b
            produce(i, first, lambda p: p * other_rows + b * CB, cols)
            tick(i)
            if b == 0:
                qkv_load(n).wait()

                @pl.when(n + 1 < 3 * W // CW)
                def _():
                    qkv_load(n + 1).start()

                for t in range(rows // MT):
                    tile = slice(t * MT, (t + 1) * MT)
                    term = matmul(cols[tile, :], ref.wu[lax.rem(n, 2), :, :CW], ((1,), (1,)))

                    @pl.when(n == 0)
                    def _():
                        acc[tile, :] = term

                    @pl.when(n > 0)
                    def _():
                        acc[tile, :] += term
        return 0

    lax.fori_loop(0, 3 * W // CW, qkv_step, 0)

    gt_out, gt_send, gt_recv = ref.gt_out, ref.gt_send, ref.gt_recv

    def first_tile(t, _):
        tile = pl.ds(pl.multiple_of(t * TR, TR), TR)
        unit, scale = norm_parts(x_s[tile, :].astype(F32))
        grad = acc[tile, :]
        note(ATTN_GAIN, jnp.sum(grad * unit, axis=0, keepdims=True))
        note(ATTN_SHIFT, jnp.sum(grad, axis=0, keepdims=True))
        note(QV, jnp.sum(G[tile, :W].astype(F32), axis=0, keepdims=True))
        note(QV + 1, jnp.sum(G[tile, 2 * W :].astype(F32), axis=0, keepdims=True))
        to_owner(t, gmid[tile, :] + norm_back(grad, unit, scale, vector(ATTN_GAIN)), gt_out, gt_send)
        return 0

    lax.fori_loop(0, rows // TR, first_tile, 0)

    small_steps = [
        [place.at(c=1 - place.c)],
        [place.at(y=place.ahead_y(k)) for k in range(1, Y)],
        [place.at(x=1 - place.x)],
        [place.at(z=place.ahead_z(k)) for k in range(1, Z)],
    ]

    def small_send(step):
        return [
            send(small.at[step, 0], small.at[step, k + 1], ref.ss.at[step, k], ref.sr.at[step, k], device)
            for k, device in enumerate(small_steps[step])
        ]

    def small_step(step):
        for copy in small_send(step):
            copy.wait()
        whole = small[step, 0]
        for k in range(len(small_steps[step])):
            whole = whole + small[step, k + 1]
        if step < 3:
            small[step + 1, 0] = whole
            for copy in small_send(step + 1):
                copy.start()
        else:
            ref.small_out[...] = whole

    for copy in small_send(0):
        copy.start()
    gt_copy = send(gt_send, gt_recv, ref.ts.at[1], ref.tr.at[1], swap_peer)
    depth = 3 + 5 * LAG
    for lag in range(depth):
        tick(total + lag)
        if lag == 1:
            gt_copy.start()
        if lag % 2 == 1 and lag < 8:
            small_step(lag // 2)
    tok_copy.wait()
    gt_copy.wait()
    gt_out[1 - mine] = gt_recv[...].astype(F32)


def layer(replicas, shards, vectors, count, tokens, cotangent, weights):
    Y, Z, half = shards // 2, replicas // 2, shards // 2
    _, R, W = tokens.shape
    rows, keys = 2 * R, half * 2 * R
    FF = weights[UP].shape[1]
    CB, CW = min(128, W // shards), max(512, 128 * Z)
    HB, WZ = CB // 2, CW // Z
    total = (FF // shards // CB) * (W // CW) + (W // shards // CB) * ((FF + 4 * W) // CW)
    peers = max(Y, Z, 2)
    staged, direct, _ = gather_items(replicas, shards, W, FF)
    m = len(staged) + len(direct)
    multiples = tuple(v.shape[0] // (W // shards) for v in vectors)
    if (W // shards) % 128:
        vectors = [v.reshape(n, W // shards) for v, n in zip(vectors, multiples)]
    dma = pltpu.SemaphoreType.DMA
    vmem, anywhere = pl.BlockSpec(memory_space=pltpu.VMEM), pl.BlockSpec(memory_space=pl.ANY)
    inputs = dict(count=count, tokens=tokens, cotangent=cotangent, qkv=weights[QKV], proj=weights[PROJ],
                  up=weights[UP], down=weights[DOWN])
    scratch = dict(
        part=pltpu.VMEM((2, 2, Y, CB, CW), BF),
        crecv=pltpu.VMEM((CORE_SLOTS, Y, CB, CW), BF),
        ysum=pltpu.VMEM((SLOTS, Y, CB, CW), BF),
        yrecv=pltpu.VMEM((SLOTS, Y - 1, CB, CW), BF),
        xsum=pltpu.VMEM((SLOTS, 2, HB, CW), BF),
        xrecv=pltpu.VMEM((SLOTS, HB, CW), BF),
        zsum=pltpu.VMEM((SLOTS, Z, HB, WZ), BF),
        zrecv=pltpu.VMEM((SLOTS, Z - 1, HB, WZ), BF),
        out=pltpu.VMEM((total, CB, CW), BF),
        small_buf=pltpu.VMEM((4, peers, 16, W), F32),
        kv=pltpu.VMEM((2, keys, W), BF),
        gpre=pltpu.VMEM((rows, FF), BF),
        act_s=pltpu.VMEM((rows, shards * BW), BF),
        slope_s=pltpu.VMEM((rows, shards * BW), F32),
        cot_s=pltpu.VMEM((rows, W), BF),
        gfeed=pltpu.VMEM((rows, W), BF),
        x_s=pltpu.VMEM((rows, W), BF),
        branch_s=pltpu.VMEM((rows, W), F32),
        second_s=pltpu.VMEM((rows, W), BF),
        attended_s=pltpu.VMEM((rows, W), BF),
        query_s=pltpu.VMEM((rows, W), BF),
        first_s=pltpu.VMEM((rows, W), BF),
        proj_s=pltpu.VMEM((W, W), BF),
        wd=pltpu.VMEM((2, shards * BW, W), BF),
        wu=pltpu.VMEM((2, W, shards * BW), BF),
        acc=pltpu.VMEM((rows, W), F32),
        gmid=pltpu.VMEM((rows, W), F32),
        gbranch=pltpu.VMEM((rows, W), BF),
        gatt=pltpu.VMEM((rows, W), BF),
        G=pltpu.VMEM((rows, 3 * W), BF),
        pown=pltpu.VMEM((PAIR_SLOTS, 2, rows, 128), F32),
        psend=pltpu.VMEM((PAIR_SLOTS, half - 1, 2, rows, 128), BF),
        precv=pltpu.VMEM((PAIR_SLOTS, half - 1, 2, rows, 128), BF),
        gk_acc=pltpu.VMEM((keys, 128), F32),
        gv_acc=pltpu.VMEM((keys, 128), F32),
        tok_send=pltpu.VMEM((R, W), BF),
        gt_send=pltpu.VMEM((R, W), BF),
        gt_recv=pltpu.VMEM((R, W), BF),
        small_s=pltpu.VMEM((shards, 16, W // shards), F32),
        vec=pltpu.VMEM((16, W), F32),
        lse=pltpu.VMEM((W // 128, 2, rows), F32),
        lsem=dma((12,)), wsem=dma((2, 2, shards)), qsem=dma((2,)), osem=dma((SLOTS,)),
        gys=dma((m, Y - 1)), gyr=dma((m, Y - 1)),
        gzs=dma((m, Y - 1, Z - 1)), gzr=dma((m, Y - 1, Z - 1)),
        gxs=dma((m, Y - 1)), gxr=dma((m, Y - 1)),
        gcs=dma((m, Y - 1)), gcr=dma((m, Y - 1)),
        os=dma((4,)), orr=dma((4,)),
        vs=dma((shards - 1,)), vr=dma((shards - 1,)),
        ks=dma((2, W // CW, half - 1)), kr=dma((2, W // CW, half - 1)),
        cs=dma((CORE_SLOTS,)), cr=dma((CORE_SLOTS,)),
        ys=dma((SLOTS, Y - 1)), yr=dma((SLOTS, Y - 1)),
        xs=dma((SLOTS,)), xr=dma((SLOTS,)),
        zs=dma((SLOTS, Z - 1)), zr=dma((SLOTS, Z - 1)),
        gs=dma((SLOTS, Z - 1)), gr=dma((SLOTS, Z - 1)),
        hs=dma((SLOTS,)), hr=dma((SLOTS,)),
        ps=dma((PAIR_SLOTS, half - 1)), pr=dma((PAIR_SLOTS, half - 1)),
        ss=dma((4, peers - 1)), sr=dma((4, peers - 1)),
        ts=dma((4,)), tr=dma((4,)),
    )
    if CB % 128:
        scratch["tile"] = pltpu.VMEM((128, CW), F32)
    outs = dict(
        o_down=jax.ShapeDtypeStruct((FF // shards, W), BF),
        o_up=jax.ShapeDtypeStruct((W // shards, FF), BF),
        o_proj=jax.ShapeDtypeStruct((W // shards, W), BF),
        o_qkv=jax.ShapeDtypeStruct((W // shards, 3 * W), BF),
        small_out=jax.ShapeDtypeStruct((16, W), F32),
        tok_out=jax.ShapeDtypeStruct((2, R, W), BF),
        gt_out=jax.ShapeDtypeStruct((2, R, W), F32),
        g_qkv=jax.ShapeDtypeStruct((W, 3 * W), BF),
        g_proj=jax.ShapeDtypeStruct((W, W), BF),
        g_up=jax.ShapeDtypeStruct((W, FF), BF),
        g_down=jax.ShapeDtypeStruct((FF, W), BF),
    )
    names = tuple(inputs) + tuple(outs) + tuple(scratch)
    results = pl.pallas_call(
        functools.partial(layer_kernel, replicas, shards, multiples, names),
        in_specs=[vmem] * len(vectors) + [pl.BlockSpec(memory_space=pltpu.SMEM)] + [anywhere] * 6,
        out_specs=[anywhere] * 4 + [vmem] * 3 + [anywhere] * 4,
        out_shape=list(outs.values()),
        scratch_shapes=list(scratch.values()),
        compiler_params=pltpu.CompilerParams(
            collective_id=0, has_side_effects=True, vmem_limit_bytes=63 * MIB
        ),
    )(*vectors, *inputs.values())
    return results[:7]


def on_device(replicas, shards, tokens, qkv_weight, qv_bias, proj_weight, proj_bias, up_weight, up_bias,
              down_weight, down_bias, attn_gain, attn_shift, mlp_gain, mlp_shift, attn_scale, mlp_scale,
              cotangent, image_count):
    vectors = (qv_bias, proj_bias, up_bias, down_bias, attn_gain, attn_shift, mlp_gain, mlp_shift,
               attn_scale, mlp_scale)
    shard = lax.axis_index("shard")
    *grads, small, output, grad_tokens = layer(
        replicas, shards, vectors, image_count, tokens, cotangent,
        (qkv_weight, proj_weight, up_weight, down_weight),
    )
    grad_down, grad_up, grad_proj, grad_qkv = [grad.astype(F32) for grad in grads]

    def own(row, count=1):
        whole = small[row : row + count].reshape(-1)
        size = whole.shape[0] // shards
        return lax.dynamic_slice_in_dim(whole, shard * size, size)

    return (output, grad_tokens, grad_qkv, own(QV, 2), grad_proj, own(PROJ_B), grad_up,
            own(UP_B, DOWN_B - UP_B), grad_down, own(DOWN_B), own(ATTN_GAIN), own(ATTN_SHIFT), own(MLP_GAIN),
            own(MLP_SHIFT), own(ATTN_SCALE), own(MLP_SCALE))


def solution(mesh):
    rows, vector = P("shard", None), P("shard")
    image = P("replica", "shard", None)
    in_specs = (image, rows, vector, rows, vector, rows, vector, rows, vector, vector, vector, vector,
                vector, vector, vector, image, P())
    out_specs = (image, image, rows, vector, rows, vector, rows, vector, rows, vector, vector, vector,
                 vector, vector, vector, vector)
    return jax.shard_map(
        functools.partial(on_device, mesh.shape["replica"], mesh.shape["shard"]),
        mesh=mesh, in_specs=in_specs, out_specs=out_specs, check_vma=False,
    )
```

time: 502 us -> 316 us (0.63)
  Pallas kernels: 421 us -> 296 us
  local copies, waits for them, and re-layouts: 30.2 us -> 8.5 us
  matrix products: 18.8 us -> 0 us
  waiting for transfers between devices: 9.82 us -> 0 us
  other arithmetic: 16 us -> 9.83 us
    pallas_call x3 -> x1, Pallas kernels: 421 us -> 296 us  [layer(): pl.pallas_call(functools.partial(layer_kernel, replicas, shards, multiple...]
    dot_general x3 -> x0, matrix products: 18.8 us -> none  [matmul(): lax.dot_general(left, right, (dims, ((), ())), preferred_element_type=F32)]
    ppermute x4 -> x0, waiting for transfers between devices: 9.82 us -> none  [the longest x2 9.82 us: join(): return jnp.concatenate([keep, lax.ppermute(give, 'shard', swap)], axis=0)]
    slice x4 -> x0, local copies, waits for them, and re-layouts: 7.6 us -> none  [the longest x3 7.45 us: backward(): block = out[base:base + chunks].reshape(n_cols, -1, W).swapaxes(0, 1)]
    unnamed x86 -> x16, local copies, waits for them, and re-layouts: 9.95 us -> 3.84 us
    concatenate x3 -> x0, other arithmetic: 5.47 us -> none  [the longest x2 4.43 us: all_rows(): return jnp.concatenate([array, lax.ppermute(array, 'shard', other)], axis=0)]
  transfers between devices with their start and end apart: 4 -> 0, of which waited for: 1 -> 0; matrix products, arithmetic and copies ran while one was open for 2% -> 0% of each run, Pallas kernels for 39% -> 0%
where the time goes in v4:
time: 316 us; the launch traced here: 315 us
  Pallas kernels  296 us (94%)
  other arithmetic  9.83 us (3%)
  local copies, waits for them, and re-layouts  8.5 us (3%)
    pallas_call x1, Pallas kernels, layer(): pl.pallas_call(functools.partial(layer_kernel, replicas, shards, multiple...  296 us
    convert_element_type x4, other arithmetic, on_device(): grad.astype(F32)  9.83 us

profile of v4, /device:TPU:0, one launch (start us, length us, event | category | flops | bytes accessed | tf_op | source)
XLA Modules:
  0.0 315.0 jit_solution(15830070994448447037)
XLA Ops:
  0.7 296.0 %shard_map.288 = (bf16[1024,1024]{1,0:T(8,128)(2,1)}, bf16[256,4096]{1,0:T(8,128)(2,1)}, bf16[256,1024]{1,0:T(8,128)(2,1)}, bf16[256,3072]{1,0:T(8,128)(2,1)}, f...) custom-call(bf16[512]{0:T(512)(128)(2,1)} %refs_0_.1, ...), custom_call_target="tpu_custom_call" | custom-call | tf_op jit(solution)/shard_map/pallas_call | solution.py:1011
  296.7 1.1 fusion
  297.8 0.6 constant_dynamic-slice_fusion
  298.4 0.6 constant_dynamic-slice_fusion.2
  299.0 0.6 constant_dynamic-slice_fusion.4
  299.5 0.6 constant_dynamic-slice_fusion.6
  300.1 0.8 slice_bitcast_fusion
  300.9 0.6 dynamic_slice.49
  301.5 0.8 slice_bitcast_fusion.1
  302.2 0.7 dynamic_slice.46
  302.9 0.0 copy-start
  302.9 4.2 %convert_element_type.14 = f32[256,4096]{1,0:T(8,128)} convert(bf16[256,4096]{1,0:T(8,128)(2,1)} %get-tuple-element.28) | non-fusion elementwise | flops 1048576 | bytes 6291456 | tf_op jit(solution)/shard_map/convert_element_type | solution.py:1034
  307.1 0.0 copy-done
  307.1 0.0 copy-start.2
  307.1 2.5 convert_element_type.15
  309.6 0.0 copy-done.2
  309.6 0.0 copy-start.4
  309.6 0.0 copy-start.3
  309.6 2.0 convert_element_type.12
  311.7 0.0 copy-start.1
  311.7 0.0 copy-done.4
  311.7 1.1 convert_element_type.13
  312.7 0.0 copy-done.3
  312.7 1.0 copy.41
  313.7 0.0 copy-done.1
  313.7 1.3 copy.42
  (2 shorter events, 0.0 us)
Async XLA Ops:
  302.9 4.3 %copy-start = (bf16[1024,1024]{1,0:T(8,128)(2,1)S(1)}, bf16[1024,1024]{1,0:T(8,128)(2,1)}, u32[]{:S(2)}) copy-start(bf16[1024,1024]{1,0:T(8,128)(2,1)} %get-tuple-element.29) | copy-start | bytes 6291460
  307.1 2.5 copy-start.2
  309.6 2.0 copy-start.4
  309.6 3.1 copy-start.3
  311.7 2.1 copy-start.1

commit v5 on v4

--- a/solution.py
+++ b/solution.py
@@ -18,7 +18,6 @@
 PAIR_SLOTS = 4
 CORE_SLOTS = 4
 LAG = 2
-GLAG = 2
 
 
 def matmul(left, right, dims=((1,), (0,))):
@@ -44,11 +43,16 @@
         c = self.c if c is None else c
         return (z * 2 + x, y * 2 + c)
 
-    def ahead_z(self, k):
-        return lax.rem(self.z + k, self.Z)
-
-    def behind_z(self, k):
-        return lax.rem(self.z + self.Z - k, self.Z)
+    def near_z(self, k):
+        z, bit = self.z, 1
+        while bit < self.Z:
+            if k & bit:
+                z = z + bit - 2 * bit * lax.rem(lax.div(z, bit), 2)
+            bit *= 2
+        return z
+
+    def z_order(self):
+        return sorted(range(1, self.Z), key=lambda k: (-(k.bit_length()), k))
 
     def ahead_y(self, k):
         return lax.rem(self.y + k, self.Y)
@@ -59,7 +63,7 @@
     def greet(self, extra=()):
         others = [self.at(c=1 - self.c), self.at(x=1 - self.x)]
         others += [self.at(y=self.ahead_y(k)) for k in range(1, self.Y)]
-        others += [self.at(z=self.ahead_z(k)) for k in range(1, self.Z)]
+        others += [self.at(z=self.near_z(k)) for k in range(1, self.Z)]
         others += list(extra)
         barrier = pltpu.get_barrier_semaphore()
         for other in others:
@@ -80,6 +84,8 @@
 
 QV, PROJ_B, UP_B, DOWN_B, ATTN_GAIN, ATTN_SHIFT, MLP_GAIN, MLP_SHIFT, ATTN_SCALE, MLP_SCALE, LIVE = (
     0, 2, 3, 7, 8, 9, 10, 11, 12, 13, 14)
+SMALL_ROWS = ((QV, 2), (PROJ_B, 1), (UP_B, 4), (DOWN_B, 1), (ATTN_GAIN, 1), (ATTN_SHIFT, 1), (MLP_GAIN, 1),
+              (MLP_SHIFT, 1), (ATTN_SCALE, 1), (MLP_SCALE, 1))
 QKV, PROJ, UP, DOWN = range(4)
 
 
@@ -101,22 +107,33 @@
 BW = 128
 
 
+FIRST = 6
+TAIL = 4
+
+
 def gather_items(replicas, shards, width, hidden):
     Z = replicas // 2
     step = max(512, 128 * Z)
     size, down = width // shards, hidden // shards
-    staged = [(QKV, 0, size, (1 + n) * width + h * step, step) for h in range(width // step) for n in range(2)]
-    direct = [(QKV, 0, size, h * step, step) for h in range(width // step)]
-    staged += [(PROJ, 0, size, h * step, step) for h in range(width // step)]
-    need, known = [], set()
+    halves = width // step
+    items = [(QKV, 0, size, n * width + h * step, step) for h in range(halves) for n in (1, 2, 0)]
+    items += [(PROJ, 0, size, h * step, step) for h in range(halves)]
+    upto, known = [], set()
     for b in range(down // BW):
         for p in range(shards):
             c = (p * down + b * BW) // step
             if c not in known:
                 known.add(c)
-                staged.append((UP, 0, size, c * step, step))
-        staged.append((DOWN, b * BW, BW, 0, width))
-        need.append(len(staged))
+                items.append((UP, 0, size, c * step, step))
+        items.append((DOWN, b * BW, BW, 0, width))
+        upto.append(len(items))
+    straight = set(range(len(items) - TAIL, len(items)))
+    staged = [item for n, item in enumerate(items) if n not in straight]
+    direct = [item for n, item in enumerate(items) if n in straight]
+    need = []
+    for n in upto:
+        over = len([m for m in straight if m < n])
+        need.append((n - over, over))
     return staged, direct, need
 
 
@@ -146,7 +163,7 @@
     kv, gpre, cot, gfeed, G = ref.kv, ref.gpre, ref.cot_s, ref.gfeed, ref.G
     second, first, query, x_s = ref.second_s, ref.first_s, ref.query_s, ref.x_s
     attended, branch, gbranch, gatt = ref.attended_s, ref.branch_s, ref.gbranch, ref.gatt
-    TR, MT, QT = min(128, R), min(256, rows), min(256, rows)
+    TR, MT, QT, TM = min(128, R), min(256, rows), min(256, rows), min(256, R)
     pairs, tiles = W // 128, rows // QT
 
     def half_peer(k):
@@ -186,13 +203,17 @@
 
     def piece(m, owner, whole_rows, whole_cols):
         w, row, size, col, width = items[m]
-        at = owner * sizes[w] + row
+        at, cols = owner * sizes[w] + row, pl.ds(col, width)
         if not whole_rows:
-            at, size = at + place.x * (size // 2), size // 2
-        at = pl.ds(pl.multiple_of(at, 16), size)
-        if whole_cols:
-            return at, pl.ds(col, width)
-        return at, pl.ds(pl.multiple_of(col + place.z * (width // Z), 128), width // Z)
+            size //= 2
+            at = at + place.x * size
+        if not whole_cols:
+            if size % (16 * Z):
+                cols = pl.ds(pl.multiple_of(col + place.z * (width // Z), 128), width // Z)
+            else:
+                size //= Z
+                at = at + place.z * size
+        return pl.ds(pl.multiple_of(at, 16), size), cols
 
     def gy_copy(m, k):
         w, whole = items[m][0], m >= n_staged
@@ -206,7 +227,7 @@
     def gz_copy(m, k, j):
         b = gathered(m, k, False, False)
         return send(b, b, ref.gzs.at[m, k - 1, j - 1], ref.gzr.at[m, k - 1, j - 1],
-                    place.at(z=place.ahead_z(j)))
+                    place.at(z=place.near_z(j)))
 
     def gx_copy(m, k):
         b = gathered(m, k, False, True)
@@ -229,41 +250,60 @@
         for k in range(1, Y):
             gc_copy(m, k).wait()
 
-    early = 2 * (W // CW)
-    ahead = early + 2
-
-    def gather_tick(t):
-        if early <= t + ahead < n_staged:
-            gy_start(t + ahead)
-        if t < n_staged:
+    halves = W // CW
+    early = 3 * halves
+
+    def gather_y_step(m):
+        for k in range(1, Y):
+            gy_copy(m, k).wait()
+            for j in place.z_order():
+                gz_copy(m, k, j).start()
+
+    def gather_x_step(m):
+        if 0 <= m - 2 < n_staged:
             for k in range(1, Y):
-                gy_copy(t, k).wait()
-                for j in range(1, Z):
-                    gz_copy(t, k, j).start()
-        m = t - GLAG
-        if 0 <= m < n_staged:
+                gx_copy(m - 2, k).wait()
+                gc_copy(m - 2, k).start()
+        if m < n_staged:
             for k in range(1, Y):
                 for j in range(1, Z):
                     gz_copy(m, k, j).wait()
                 gx_copy(m, k).start()
-        m = t - 2 * GLAG
-        if 0 <= m < n_staged:
-            for k in range(1, Y):
-                gx_copy(m, k).wait()
-                gc_copy(m, k).start()
-        m = t - 3 * GLAG
-        if 0 <= m < n_staged:
-            arrived(m)
-
-    ticked = [0]
-
-    def gather_until(t):
-        while ticked[0] < min(t + 3 * GLAG, n_staged + 3 * GLAG):
-            gather_tick(ticked[0])
-            ticked[0] += 1
-
-    def gather_ticks(count):
-        gather_until(ticked[0] + count - 3 * GLAG)
+        if 0 <= m - 4 < n_staged and m - 4 >= done[2]:
+            gather_c_step(m - 4)
+
+    def gather_c_step(m):
+        for k in range(1, Y):
+            gc_copy(m, k).wait()
+        done[2] = m + 1
+
+    last_step = n_staged + 4
+    done = [0, 0, 0]
+
+    def gather_y(n):
+        while done[0] < min(n, n_staged):
+            gather_y_step(done[0])
+            done[0] += 1
+
+    def gather_x(n, window=3):
+        while done[1] < min(n, last_step):
+            gather_y(done[1] + window)
+            gather_x_step(done[1])
+            done[1] += 1
+
+    def gather_until(m):
+        gather_x(m + 2)
+        while done[2] < min(m, n_staged):
+            gather_c_step(done[2])
+
+    def direct_step(h):
+        for k in range(1, Y):
+            gy_copy(n_staged + h, k).wait()
+            gc_copy(n_staged + h, k).start()
+
+    def direct_arrived(h):
+        for k in range(1, Y):
+            gc_copy(n_staged + h, k).wait()
 
     x_swap = send(ref.tokens.at[1 - mine], x_s.at[pl.ds(R, R)], ref.ts.at[2], ref.tr.at[2], swap_peer)
     cot_swap = send(ref.cotangent.at[1 - mine], cot.at[pl.ds(R, R)], ref.ts.at[3], ref.tr.at[3], swap_peer)
@@ -276,12 +316,10 @@
                  for w in range(4)]
     for copy in small_sends:
         copy.start()
-    for m in range(early):
+    for m in range(min(FIRST, n_staged)):
         gy_start(m)
     x_swap.start()
-    for h in range(W // CW):
-        gy_start(n_staged + h)
-    for m in range(early, early + 2):
+    for m in range(FIRST, n_staged):
         gy_start(m)
     for copy in own_sends:
         copy.start()
@@ -302,7 +340,7 @@
         return vec[row : row + 1, :]
 
     def note(row, value):
-        small[0, 0, row : row + 1, :] += value
+        small[row : row + 1, :] += value
 
     def norm_tile(t, _):
         tile = pl.ds(pl.multiple_of(t * TR, TR), TR)
@@ -315,15 +353,11 @@
     for w in range(4):
         own_loads[w].wait()
         own_stores[w].start()
-    gather_ticks(2)
+    gather_x(3)
     x_swap.wait()
-    cot_swap.start()
     lax.fori_loop(R // TR, rows // TR, norm_tile, 0)
-    gather_ticks(2)
-    direct_arrived(0)
     gather_until(2)
-    for w in (QKV, DOWN):
-        own_stores[w].wait()
+    own_stores[QKV].wait()
     own_sends[QKV].wait()
 
     def kv_copy(which, h, k):
@@ -331,20 +365,29 @@
         return send(kv.at[which, pl.ds(0, rows), cols], kv.at[which, pl.ds((half - k) * rows, rows), cols],
                     ref.ks.at[which, h, k - 1], ref.kr.at[which, h, k - 1], half_peer(k))
 
+    def qkv_slot(slot):
+        if slot < 2:
+            return ref.wu[slot, :, :CW]
+        return ref.wq[...]
+
     def qkv_tile(n, h, slot):
-        return load(ref.g_qkv.at[:, pl.ds(n * W + h * CW, CW)], ref.wu.at[slot, :, pl.ds(0, CW)],
-                    ref.qsem.at[slot])
-
-    def project(h):
+        target = ref.wu.at[slot, :, pl.ds(0, CW)] if slot < 2 else ref.wq
+        return load(ref.g_qkv.at[:, pl.ds(n * W + h * CW, CW)], target, ref.qsem.at[slot])
+
+    def project(h, ready=None):
         here = slice(h * CW, (h + 1) * CW)
-        tile_loads = [qkv_tile(1, h, 0), qkv_tile(2, h, 1), qkv_tile(0, h, 0)]
+        tile_loads = [qkv_tile(1, h, 0), qkv_tile(2, h, 1), qkv_tile(0, h, 2)]
         tile_loads[0].start()
         tile_loads[1].start()
         for n in range(3):
+            if n == 2:
+                if ready:
+                    ready()
+                tile_loads[2].start()
             tile_loads[n].wait()
             for t in range(rows // MT):
                 tile = slice(t * MT, (t + 1) * MT)
-                value = matmul(first[tile, :], ref.wu[n % 2, :, :CW])
+                value = matmul(first[tile, :], qkv_slot(n))
                 if n == 0:
                     kv[0, tile, here] = value.astype(BF)
                 elif n == 1:
@@ -354,38 +397,41 @@
             if n < 2:
                 for k in range(1, half):
                     kv_copy(n, h, k).start()
-            if n == 0:
-                tile_loads[2].start()
 
     def exchanged(h):
         for which in range(2):
             for k in range(1, half):
                 kv_copy(which, h, k).wait()
 
-    for k in range(1, Y):
-        gc_copy(n_staged, k).wait()
-    project(0)
-
-    halves = W // CW
+    project(0, lambda: gather_until(3))
+    cot_swap.start()
+    for h in range(len(direct)):
+        gy_start(n_staged + h)
+
     plan = {}
 
     def at_pair(p, act):
         plan.setdefault(p, []).append(act)
 
+    pace = (6, 7, 8, 9, 11, 12, 13, 14)
+    for p in range(1, pairs):
+        at_pair(p, lambda p=p: gather_x(pace[p], 5))
     if halves > 1:
         def second_half():
-            direct_arrived(1)
             gather_until(early)
-            arrived(n_staged + 1)
             project(1)
 
-        at_pair(2, second_half)
-        at_pair(4, lambda: exchanged(1))
-    stop = 2 * halves + halves + 2
-    at_pair(5, lambda: gather_until(early + 1))
-    at_pair(6, lambda: gather_until(early + 2))
-    at_pair(7, lambda: gather_until(stop))
+        at_pair(pairs // 2 - 1, second_half)
+        at_pair(pairs // 2, lambda: exchanged(1))
+    gather_x(pace[0], 5)
     exchanged(0)
+
+    def both_heads(array, lane):
+        return jnp.concatenate([jnp.where(lane < HEAD_DIM, array, BF(0)), jnp.where(lane >= HEAD_DIM, array, BF(0))])
+
+    def own_heads(array):
+        n = array.shape[1] // 2
+        return jnp.concatenate([array[:HEAD_DIM, :n], array[HEAD_DIM:, n:]])
 
     def attend(p, _):
         for at in sorted(plan):
@@ -397,33 +443,26 @@
         lane = lax.broadcasted_iota(jnp.int32, (1, 128), 1)
         cols = pl.ds(pl.multiple_of(p * 128, 128), 128)
         key, value_t = kv[0, :, cols], kv[1, :, cols].T
-        for t in range(tiles):
-            tile = slice(t * QT, (t + 1) * QT)
-            q_tile = query[tile, cols] * BF(HEAD_DIM**-0.5)
-            parts = []
-            for head in range(2):
-                owned = (lane < HEAD_DIM) if head == 0 else (lane >= HEAD_DIM)
-                scores = matmul(key, jnp.where(owned, q_tile, BF(0)), ((1,), (1,)))
-                highest = jnp.max(scores, axis=0, keepdims=True)
-                expos = jnp.exp(scores - highest)
-                denom = jnp.sum(expos, axis=0, keepdims=True)
-                probs = (expos * (1.0 / denom)).astype(BF)
-                lse[p, head : head + 1, tile] = highest + jnp.log(denom)
-                lanes = slice(head * HEAD_DIM, (head + 1) * HEAD_DIM)
-                parts.append(matmul(value_t[lanes, :], probs))
-            attended[tile, cols] = jnp.concatenate(parts, axis=0).T.astype(BF)
+        scores = matmul(key, both_heads(query[:, cols] * BF(HEAD_DIM**-0.5), lane), ((1,), (1,)))
+        highest = jnp.max(scores, axis=0, keepdims=True)
+        expos = jnp.exp(scores - highest)
+        denom = jnp.sum(expos, axis=0, keepdims=True)
+        probs = (expos * (1.0 / denom)).astype(BF)
+        lse[p] = highest + jnp.log(denom)
+        attended[:, cols] = own_heads(matmul(value_t, probs)).T.astype(BF)
         return 0
 
     lax.fori_loop(0, pairs, attend, 0)
 
-    gather_until(3 * halves)
+    gather_until(early + halves)
     own_stores[PROJ].wait()
+    own_stores[DOWN].wait()
     own_sends[PROJ].wait()
     proj_load = load(ref.g_proj, ref.proj_s, ref.lsem.at[10])
     proj_load.start()
     cot_load.wait()
     cot_swap.wait()
-    small[0, 0] = jnp.zeros_like(small[0, 0])
+    small[...] = jnp.zeros_like(small)
 
     def feed_tile(t, _):
         tile = pl.ds(pl.multiple_of(t * TR, TR), TR)
@@ -444,6 +483,7 @@
         return 0
 
     lax.fori_loop(0, rows // MT, branch_tile, 0)
+    gather_x(pace[-1] + 2, 5)
     for w in (UP, DOWN):
         own_sends[w].wait()
     own_stores[UP].wait()
@@ -458,7 +498,10 @@
             copies.append(load(ref.g_down.at[at], ref.wd.at[slot, to], ref.wsem.at[1, slot, p]))
         return copies
 
-    gather_until(need[0])
+    gather_until(need[0][0])
+    for h in range(need[0][1]):
+        direct_step(h)
+        direct_arrived(h)
     for copy in block_loads(0):
         copy.start()
 
@@ -479,8 +522,8 @@
 
     def z_copy(i, k):
         a = lax.rem(i, SLOTS)
-        return send(zsum.at[a, place.ahead_z(k)], zrecv.at[a, k - 1], ref.zs.at[a, k - 1],
-                    ref.zr.at[a, k - 1], place.at(z=place.ahead_z(k)))
+        return send(zsum.at[a, place.near_z(k)], zrecv.at[a, k - 1], ref.zs.at[a, k - 1],
+                    ref.zr.at[a, k - 1], place.at(z=place.near_z(k)))
 
     HB, WZ = CB // 2, CW // Z
     x_rows = pl.ds(pl.multiple_of(place.x * HB, HB), HB)
@@ -490,7 +533,7 @@
         a = lax.rem(i, SLOTS)
         block = out.at[i, x_rows, z_cols]
         return send(block, block, ref.gs.at[a, k - 1], ref.gr.at[a, k - 1],
-                    place.at(z=place.ahead_z(k)))
+                    place.at(z=place.near_z(k)))
 
     def xg_copy(i):
         a = lax.rem(i, SLOTS)
@@ -517,6 +560,8 @@
             base += count
 
     def add(*terms):
+        if len(terms) == 2:
+            return terms[0] + terms[1]
         whole = terms[0].astype(F32)
         for term in terms[1:]:
             whole = whole + term.astype(F32)
@@ -559,7 +604,7 @@
             for z in range(Z):
                 cols = slice(z * WZ, (z + 1) * WZ)
                 zsum[a, z] = add(xsum[a, place.x, :, cols], xrecv[a, :, cols])
-            for k in range(1, Z):
+            for k in place.z_order():
                 z_copy(j3, k).start()
 
         j4, ok4 = stage(1 + 3 * LAG)
@@ -570,7 +615,7 @@
             for k in range(1, Z):
                 z_copy(j4, k).wait()
             out[j4, x_rows, z_cols] = add(zsum[a, place.z], *[zrecv[a, k - 1] for k in range(1, Z)])
-            for k in range(1, Z):
+            for k in place.z_order():
                 zg_copy(j4, k).start()
 
         j5, ok5 = stage(1 + 4 * LAG)
@@ -617,22 +662,26 @@
     acc, gmid, act, slope = ref.acc, ref.gmid, ref.act_s, ref.slope_s
     spread = []
     for b in range(n_blocks):
-        goal = need[min(b + 1, n_blocks - 1)] + 3 * GLAG
-        start = spread[-1][1] if spread else ticked[0]
-        left = n_staged + 3 * GLAG - start
-        stop = min(max(goal, start + -(-left // max(1, n_blocks - 1 - b))), n_staged + 3 * GLAG)
-        spread.append((start, stop))
+        start = spread[-1][1] if spread else done[1]
+        goal, over = need[min(b + 1, n_blocks - 1)]
+        soon = need[min(b + 2, n_blocks - 1)][1]
+        spread.append((start, min(max(goal + 4, start + 2), last_step), over, soon))
 
     def block_step(b, _):
         slot = lax.rem(b, 2)
         for copy in block_loads(b):
             copy.wait()
 
-        for at, (start, stop) in enumerate(spread):
+        for at, (_, stop, over, soon) in enumerate(spread):
             @pl.when(b == at)
-            def _(start=start, stop=stop):
-                for t in range(start, stop):
-                    gather_tick(t)
+            def _(at=at, stop=stop, over=over, soon=soon):
+                gather_x(stop, 5)
+                for h in range(spread[at - 1][2] if at else need[0][1], over):
+                    if at == 0:
+                        direct_step(h)
+                    direct_arrived(h)
+                for h in range(spread[at - 1][3] if at else over, soon):
+                    direct_step(h)
 
         @pl.when(b + 1 < n_blocks)
         def _():
@@ -684,7 +733,7 @@
                     chunk(n)
         for p in range(shards):
             row, cols = spots[p]
-            small[0, 0, row, cols] = sums[p]
+            small[row, cols] = sums[p]
         return 0
 
     lax.fori_loop(0, n_blocks, block_step, 0)
@@ -692,14 +741,14 @@
     tok_out, tok_send = ref.tok_out, ref.tok_send
 
     def to_owner(t, value, kept, given):
-        if R >= TR:
-            lower = pl.ds(pl.multiple_of(lax.rem(t * TR, R), TR), TR)
-
-            @pl.when(t * TR < R)
+        if R >= TM:
+            lower = pl.ds(pl.multiple_of(lax.rem(t * TM, R), TM), TM)
+
+            @pl.when(t * TM < R)
             def _():
                 kept[mine, lower, :] = value.astype(kept.dtype)
 
-            @pl.when(t * TR >= R)
+            @pl.when(t * TM >= R)
             def _():
                 given[lower, :] = value.astype(BF)
         else:
@@ -707,7 +756,7 @@
             given[...] = value[R:].astype(BF)
 
     def middle_tile(t, _):
-        tile = pl.ds(pl.multiple_of(t * TR, TR), TR)
+        tile = pl.ds(pl.multiple_of(t * TM, TM), TM)
         low = branch[tile, :]
         middle = x_s[tile, :].astype(F32) + vector(ATTN_SCALE) * low
         feed = acc[tile, :] + vector(DOWN_B)
@@ -727,9 +776,21 @@
         gatt[tile, :] = matmul(grad, ref.proj_s[...], ((1,), (1,))).astype(BF)
         return 0
 
-    lax.fori_loop(0, rows // TR, middle_tile, 0)
+    def up_chunk(u):
+        i = n_down + u
+        b, n = lax.rem(u, blocks), lax.div(u, blocks)
+        produce(i, second, lambda p: p * other_rows + b * CB, columns(gpre, n))
+        tick(i)
+
+    early_up = rows // TM if n_up >= 2 * pairs else 0
+
+    def middle_step(t, _):
+        if early_up:
+            up_chunk(t)
+        return middle_tile(t, 0)
+
+    lax.fori_loop(0, rows // TM, middle_step, 0)
     tok_copy = send(tok_send, tok_out.at[mine], ref.ts.at[0], ref.tr.at[0], swap_peer)
-    tok_copy.start()
 
     def qkv_load(n):
         slot = lax.rem(n, 2)
@@ -755,18 +816,14 @@
             cols = pl.ds(pl.multiple_of((which + 1) * W + p * 128, 128), 128)
             G[:, cols] = whole.astype(BF)
 
-    def up_chunk(u):
-        i = n_down + u
-        b, n = lax.rem(u, blocks), lax.div(u, blocks)
-        produce(i, second, lambda p: p * other_rows + b * CB, columns(gpre, n))
-        tick(i)
-
     per_pair = n_up // pairs
 
     def pair_step(p, _):
         if per_pair:
             for m in range(max(1, per_pair - tiles + 1)):
-                up_chunk(p * per_pair + m)
+                @pl.when(p * per_pair + m >= early_up)
+                def _(m=m):
+                    up_chunk(p * per_pair + m)
         else:
             @pl.when(lax.rem(p, pairs // n_up) == 0)
             def _():
@@ -778,29 +835,27 @@
         key_t = key.T
         for t in range(tiles):
             tile = slice(t * QT, (t + 1) * QT)
-            q_tile, g_tile = query[tile, cols], gatt[tile, cols]
-            parts = []
-            for head in range(2):
-                owned = (lane < HEAD_DIM) if head == 0 else (lane >= HEAD_DIM)
-                own = jnp.where(owned, q_tile * BF(HEAD_DIM**-0.5), BF(0))
-                own_grad = jnp.where(owned, g_tile, BF(0))
-                probs = jnp.exp(matmul(key, own, ((1,), (1,))) - lse[p, head : head + 1, tile])
-                grad_probs = matmul(value, own_grad, ((1,), (1,)))
-                centre = jnp.sum(grad_probs * probs, axis=0, keepdims=True)
-                grad_scores = (probs * (grad_probs - centre)).astype(BF)
-                gv = matmul(probs.astype(BF), own_grad)
-                gk = matmul(grad_scores, own)
-                if t == 0 and head == 0:
-                    gv_acc[...], gk_acc[...] = gv, gk
-                else:
-                    gv_acc[...] += gv
-                    gk_acc[...] += gk
-                lanes = slice(head * HEAD_DIM, (head + 1) * HEAD_DIM)
-                parts.append(matmul(key_t[lanes, :], grad_scores))
-            whole = jnp.concatenate(parts, axis=0) * (HEAD_DIM**-0.5)
-            G[tile, cols] = whole.T.astype(BF)
+            own = both_heads(query[tile, cols] * BF(HEAD_DIM**-0.5), lane)
+            own_grad = both_heads(gatt[tile, cols], lane)
+            logs = jnp.concatenate([lse[p, :, tile], lse[p, :, rows + t * QT : rows + (t + 1) * QT]], axis=1)
+            probs = jnp.exp(matmul(key, own, ((1,), (1,))) - logs)
+            grad_probs = matmul(value, own_grad, ((1,), (1,)))
+            centre = jnp.sum(grad_probs * probs, axis=0, keepdims=True)
+            grad_scores = (probs * (grad_probs - centre)).astype(BF)
+            gv = matmul(probs.astype(BF), own_grad)
+            gk = matmul(grad_scores, own)
+            if t == 0:
+                gv_acc[...], gk_acc[...] = gv, gk
+            else:
+                gv_acc[...] += gv
+                gk_acc[...] += gk
+            G[tile, cols] = (own_heads(matmul(key_t, grad_scores)) * HEAD_DIM**-0.5).T.astype(BF)
             if per_pair and t < tiles - 1:
-                up_chunk(p * per_pair + max(1, per_pair - tiles + 1) + t)
+                u = p * per_pair + max(1, per_pair - tiles + 1) + t
+
+                @pl.when(u >= early_up)
+                def _(u=u):
+                    up_chunk(u)
         a = lax.rem(p, PAIR_SLOTS)
         pown[a, 0], pown[a, 1] = gk_acc[:rows], gv_acc[:rows]
         for k in range(1, half):
@@ -861,7 +916,7 @@
     gt_out, gt_send, gt_recv = ref.gt_out, ref.gt_send, ref.gt_recv
 
     def first_tile(t, _):
-        tile = pl.ds(pl.multiple_of(t * TR, TR), TR)
+        tile = pl.ds(pl.multiple_of(t * TM, TM), TM)
         unit, scale = norm_parts(x_s[tile, :].astype(F32))
         grad = acc[tile, :]
         note(ATTN_GAIN, jnp.sum(grad * unit, axis=0, keepdims=True))
@@ -871,44 +926,59 @@
         to_owner(t, gmid[tile, :] + norm_back(grad, unit, scale, vector(ATTN_GAIN)), gt_out, gt_send)
         return 0
 
-    lax.fori_loop(0, rows // TR, first_tile, 0)
-
-    small_steps = [
-        [place.at(c=1 - place.c)],
-        [place.at(y=place.ahead_y(k)) for k in range(1, Y)],
-        [place.at(x=1 - place.x)],
-        [place.at(z=place.ahead_z(k)) for k in range(1, Z)],
-    ]
-
-    def small_send(step):
-        return [
-            send(small.at[step, 0], small.at[step, k + 1], ref.ss.at[step, k], ref.sr.at[step, k], device)
-            for k, device in enumerate(small_steps[step])
-        ]
+    lax.fori_loop(0, rows // TM, first_tile, 0)
+
+    cw = W // shards
+    packs = ref.packs
+    for p in range(shards):
+        at = 0
+        for row, count in SMALL_ROWS:
+            for r in range(count):
+                t = p * count + r
+                line, col = row + t // shards, t % shards * cw
+                packs[p % 2, p // 2, at : at + 1, :] = small[line : line + 1, col : col + cw]
+                at += 1
+
+    sums = ref.sums
+    core_small = send(packs.at[1 - place.c], ref.core_pack, ref.ss.at[0], ref.sr.at[0], place.at(c=1 - place.c))
+    y_small = [send(packs.at[place.c, place.ahead_y(k)], sums.at[0, k], ref.ss.at[k], ref.sr.at[k],
+                    place.at(y=place.ahead_y(k))) for k in range(1, Y)]
+    x_small = [send(sums.at[1, 0], sums.at[1, 1], ref.ss.at[Y], ref.sr.at[Y], place.at(x=1 - place.x))]
+    z_small = [send(sums.at[2, 0], sums.at[2, k], ref.ss.at[Y + k], ref.sr.at[Y + k],
+                    place.at(z=place.near_z(k))) for k in range(1, Z)]
 
     def small_step(step):
-        for copy in small_send(step):
+        if step == 0:
+            core_small.wait()
+            for y in range(Y):
+                packs[place.c, y] = packs[place.c, y] + ref.core_pack[y]
+            for copy in y_small:
+                copy.start()
+            return
+        copies = (y_small, x_small, z_small)[step - 1]
+        for copy in copies:
             copy.wait()
-        whole = small[step, 0]
-        for k in range(len(small_steps[step])):
-            whole = whole + small[step, k + 1]
+        whole = packs[place.c, place.y] if step == 1 else sums[step - 1, 0]
+        for k in range(len(copies)):
+            whole = whole + sums[step - 1, k + 1]
         if step < 3:
-            small[step + 1, 0] = whole
-            for copy in small_send(step + 1):
+            sums[step, 0] = whole
+            for copy in (x_small, z_small)[step - 1]:
                 copy.start()
         else:
             ref.small_out[...] = whole
 
-    for copy in small_send(0):
-        copy.start()
+    core_small.start()
     gt_copy = send(gt_send, gt_recv, ref.ts.at[1], ref.tr.at[1], swap_peer)
     depth = 3 + 5 * LAG
+    small_after = {0: 0, 2 + LAG: 1, 2 + 2 * LAG: 2, 2 + 3 * LAG: 3}
     for lag in range(depth):
         tick(total + lag)
-        if lag == 1:
+        if lag in small_after:
+            small_step(small_after[lag])
+        if lag == 0:
             gt_copy.start()
-        if lag % 2 == 1 and lag < 8:
-            small_step(lag // 2)
+            tok_copy.start()
     tok_copy.wait()
     gt_copy.wait()
     gt_out[1 - mine] = gt_recv[...].astype(F32)
@@ -942,7 +1012,10 @@
         zsum=pltpu.VMEM((SLOTS, Z, HB, WZ), BF),
         zrecv=pltpu.VMEM((SLOTS, Z - 1, HB, WZ), BF),
         out=pltpu.VMEM((total, CB, CW), BF),
-        small_buf=pltpu.VMEM((4, peers, 16, W), F32),
+        small_buf=pltpu.VMEM((16, W), F32),
+        packs=pltpu.VMEM((2, Y, 16, W // shards), F32),
+        core_pack=pltpu.VMEM((Y, 16, W // shards), F32),
+        sums=pltpu.VMEM((3, peers, 16, W // shards), F32),
         kv=pltpu.VMEM((2, keys, W), BF),
         gpre=pltpu.VMEM((rows, FF), BF),
         act_s=pltpu.VMEM((rows, shards * BW), BF),
@@ -958,6 +1031,7 @@
         proj_s=pltpu.VMEM((W, W), BF),
         wd=pltpu.VMEM((2, shards * BW, W), BF),
         wu=pltpu.VMEM((2, W, shards * BW), BF),
+        wq=pltpu.VMEM((W, CW), BF),
         acc=pltpu.VMEM((rows, W), F32),
         gmid=pltpu.VMEM((rows, W), F32),
         gbranch=pltpu.VMEM((rows, W), BF),
@@ -973,8 +1047,8 @@
         gt_recv=pltpu.VMEM((R, W), BF),
         small_s=pltpu.VMEM((shards, 16, W // shards), F32),
         vec=pltpu.VMEM((16, W), F32),
-        lse=pltpu.VMEM((W // 128, 2, rows), F32),
-        lsem=dma((12,)), wsem=dma((2, 2, shards)), qsem=dma((2,)), osem=dma((SLOTS,)),
+        lse=pltpu.VMEM((W // 128, 1, 2 * rows), F32),
+        lsem=dma((12,)), wsem=dma((2, 2, shards)), qsem=dma((3,)), osem=dma((SLOTS,)),
         gys=dma((m, Y - 1)), gyr=dma((m, Y - 1)),
         gzs=dma((m, Y - 1, Z - 1)), gzr=dma((m, Y - 1, Z - 1)),
         gxs=dma((m, Y - 1)), gxr=dma((m, Y - 1)),
@@ -989,7 +1063,7 @@
         gs=dma((SLOTS, Z - 1)), gr=dma((SLOTS, Z - 1)),
         hs=dma((SLOTS,)), hr=dma((SLOTS,)),
         ps=dma((PAIR_SLOTS, half - 1)), pr=dma((PAIR_SLOTS, half - 1)),
-        ss=dma((4, peers - 1)), sr=dma((4, peers - 1)),
+        ss=dma((Y + Z,)), sr=dma((Y + Z,)),
         ts=dma((4,)), tr=dma((4,)),
     )
     if CB % 128:
@@ -999,7 +1073,7 @@
         o_up=jax.ShapeDtypeStruct((W // shards, FF), BF),
         o_proj=jax.ShapeDtypeStruct((W // shards, W), BF),
         o_qkv=jax.ShapeDtypeStruct((W // shards, 3 * W), BF),
-        small_out=jax.ShapeDtypeStruct((16, W), F32),
+        small_out=jax.ShapeDtypeStruct((16, W // shards), F32),
         tok_out=jax.ShapeDtypeStruct((2, R, W), BF),
         gt_out=jax.ShapeDtypeStruct((2, R, W), F32),
         g_qkv=jax.ShapeDtypeStruct((W, 3 * W), BF),
@@ -1021,26 +1095,83 @@
     return results[:7]
 
 
+def result_kernel(shards, n_vectors, *refs):
+    small, *ins = refs[:7]
+    outs = refs[7:13]
+    vectors = refs[13 : 13 + n_vectors]
+    low, wide, tok_s, gt_s, in_sem, out_sem = refs[13 + n_vectors :]
+    size, width = low.shape[1:]
+    blocks = []
+    for source, target in zip(ins[2:], outs[2:]):
+        for r in range(source.shape[0] // size):
+            for c in range(source.shape[1] // width):
+                at = (pl.ds(r * size, size), pl.ds(c * width, width))
+                blocks.append((source.at[at], target.at[at]))
+    n = len(blocks)
+    loads = [pltpu.make_async_copy(src, low.at[i], in_sem.at[i]) for i, (src, _) in enumerate(blocks)]
+    stores = [pltpu.make_async_copy(wide.at[i], dst, out_sem.at[i]) for i, (_, dst) in enumerate(blocks)]
+    for i, (source, middle, target) in enumerate(((ins[0], tok_s, outs[0]), (ins[1], gt_s, outs[1]))):
+        loads.append(pltpu.make_async_copy(source, middle, in_sem.at[n + i]))
+        stores.append(pltpu.make_async_copy(middle, target, out_sem.at[n + i]))
+    for copy in loads:
+        copy.start()
+    at = 0
+    for (_, count), vector in zip(SMALL_ROWS, vectors):
+        pieces = [small[at + r : at + r + 1, :] for r in range(count)]
+        vector[...] = jnp.concatenate(pieces, axis=1).reshape(vector.shape)
+        at += count
+    for i in range(n + 2):
+        loads[i].wait()
+        if i < n:
+            wide[i] = low[i].astype(F32)
+        stores[i].start()
+    for copy in stores:
+        copy.wait()
+
+
+def results(shards, small, tok, gt, grads):
+    _, R, W = tok.shape
+    size = W // shards
+    count = sum(grad.shape[0] * grad.shape[1] for grad in grads) // (size * W)
+    vmem, anywhere = pl.BlockSpec(memory_space=pltpu.VMEM), pl.BlockSpec(memory_space=pl.ANY)
+    shapes = [jax.ShapeDtypeStruct(tok.shape, BF), jax.ShapeDtypeStruct(gt.shape, F32)]
+    shapes += [jax.ShapeDtypeStruct(grad.shape, F32) for grad in grads]
+    n_vectors = len(SMALL_ROWS) if size % 128 == 0 else 0
+    for _, rows in SMALL_ROWS[:n_vectors]:
+        shapes.append(jax.ShapeDtypeStruct((rows * size,), F32))
+    dma = pltpu.SemaphoreType.DMA
+    tok, gt, *rest = pl.pallas_call(
+        functools.partial(result_kernel, shards, n_vectors),
+        in_specs=[vmem] + [anywhere] * 6,
+        out_specs=[anywhere] * 6 + [vmem] * n_vectors,
+        out_shape=shapes,
+        scratch_shapes=[
+            pltpu.VMEM((count, size, W), BF), pltpu.VMEM((count, size, W), F32),
+            pltpu.VMEM(tok.shape, BF), pltpu.VMEM(gt.shape, F32), dma((count + 2,)), dma((count + 2,)),
+        ],
+        compiler_params=pltpu.CompilerParams(vmem_limit_bytes=63 * MIB),
+    )(small, tok, gt, *grads)
+    vectors = rest[4:]
+    if not n_vectors:
+        at = 0
+        for _, rows in SMALL_ROWS:
+            vectors.append(small[at : at + rows].reshape(-1))
+            at += rows
+    return tok, gt, rest[:4], vectors
+
+
 def on_device(replicas, shards, tokens, qkv_weight, qv_bias, proj_weight, proj_bias, up_weight, up_bias,
               down_weight, down_bias, attn_gain, attn_shift, mlp_gain, mlp_shift, attn_scale, mlp_scale,
               cotangent, image_count):
     vectors = (qv_bias, proj_bias, up_bias, down_bias, attn_gain, attn_shift, mlp_gain, mlp_shift,
                attn_scale, mlp_scale)
-    shard = lax.axis_index("shard")
     *grads, small, output, grad_tokens = layer(
         replicas, shards, vectors, image_count, tokens, cotangent,
         (qkv_weight, proj_weight, up_weight, down_weight),
     )
-    grad_down, grad_up, grad_proj, grad_qkv = [grad.astype(F32) for grad in grads]
-
-    def own(row, count=1):
-        whole = small[row : row + count].reshape(-1)
-        size = whole.shape[0] // shards
-        return lax.dynamic_slice_in_dim(whole, shard * size, size)
-
-    return (output, grad_tokens, grad_qkv, own(QV, 2), grad_proj, own(PROJ_B), grad_up,
-            own(UP_B, DOWN_B - UP_B), grad_down, own(DOWN_B), own(ATTN_GAIN), own(ATTN_SHIFT), own(MLP_GAIN),
-            own(MLP_SHIFT), own(ATTN_SCALE), own(MLP_SCALE))
+    output, grad_tokens, (down, up, proj, qkv), small = results(shards, small, output, grad_tokens, grads)
+    qv_b, proj_b, up_b, down_b, *norms = small
+    return (output, grad_tokens, qkv, qv_b, proj, proj_b, up, up_b, down, down_b, *norms)
 
 
 def solution(mesh):

time: 316 us -> 263 us (0.83)
  Pallas kernels: 296 us -> 262 us
  other arithmetic: 9.83 us -> 0 us
  local copies, waits for them, and re-layouts: 8.5 us -> 0 us
    pallas_call x1, Pallas kernels: 296 us -> 251 us  [layer(): pl.pallas_call(functools.partial(layer_kernel, replicas, shards, multiple...]
    pallas_call x0 -> x1, Pallas kernels: none -> 10.7 us  [results(): pl.pallas_call(functools.partial(result_kernel, shards, n_vectors), in_sp...]
    convert_element_type x4 -> x0, other arithmetic: 9.83 us -> none  [on_device(): grad.astype(F32)]
    unnamed x16 -> x0, local copies, waits for them, and re-layouts: 3.84 us -> none
    dynamic_slice x6 -> x0, local copies, waits for them, and re-layouts: 3.52 us -> none  [own(): return lax.dynamic_slice_in_dim(whole, shard * size, size)]
where the time goes in v5:
time: 263 us
  Pallas kernels  262 us (100%)
    pallas_call x1, Pallas kernels, layer(): pl.pallas_call(functools.partial(layer_kernel, replicas, shards, multiple...  251 us
    pallas_call x1, Pallas kernels, results(): pl.pallas_call(functools.partial(result_kernel, shards, n_vectors), in_sp...  10.7 us

profile of v5, /device:TPU:0, one launch (start us, length us, event | category | flops | bytes accessed | tf_op | source)
XLA Modules:
  0.0 262.7 jit_solution(14748581100405808557)
XLA Ops:
  0.7 251.2 %shard_map.288 = (bf16[1024,1024]{1,0:T(8,128)(2,1)}, bf16[256,4096]{1,0:T(8,128)(2,1)}, bf16[256,1024]{1,0:T(8,128)(2,1)}, bf16[256,3072]{1,0:T(8,128)(2,1)}, f...) custom-call(bf16[512]{0:T(512)(128)(2,1)} %refs_0_.1, ...), custom_call_target="tpu_custom_call" | custom-call | tf_op jit(solution)/shard_map/pallas_call | solution.py:1085
  251.8 10.7 %shard_map.289 = (bf16[2,256,1024]{2,1,0:T(8,128)(2,1)}, f32[2,256,1024]{2,1,0:T(8,128)}, f32[1024,1024]{1,0:T(8,128)}, f32[256,4096]{1,0:T(8,128)}, f32[256,102...) custom-call(f32[16,256]{1,0:T(8,128)} %get-tuple-element.39.refs_0_,, ...), custom_call_target="tpu_custom_call" | custom-call | tf_op jit(solution)/shard_map/pallas_call | solution.py:1143

commit v6 on v5

--- a/solution.py
+++ b/solution.py
@@ -109,6 +109,8 @@
 
 FIRST = 6
 TAIL = 4
+EARLY = 2
+PACE = (5, 6, 7, 8, 9, 10, 11, 12, 14)
 
 
 def gather_items(replicas, shards, width, hidden):
@@ -128,6 +130,7 @@
         items.append((DOWN, b * BW, BW, 0, width))
         upto.append(len(items))
     straight = set(range(len(items) - TAIL, len(items)))
+    straight |= set(range(upto[0] - EARLY, upto[0]))
     staged = [item for n, item in enumerate(items) if n not in straight]
     direct = [item for n, item in enumerate(items) if n in straight]
     need = []
@@ -253,48 +256,45 @@
     halves = W // CW
     early = 3 * halves
 
-    def gather_y_step(m):
-        for k in range(1, Y):
-            gy_copy(m, k).wait()
-            for j in place.z_order():
-                gz_copy(m, k, j).start()
-
-    def gather_x_step(m):
-        if 0 <= m - 2 < n_staged:
+    done = [0, 0, 0, 0]
+
+    def gather_z(n):
+        for m in range(done[0], min(n, n_staged)):
             for k in range(1, Y):
-                gx_copy(m - 2, k).wait()
-                gc_copy(m - 2, k).start()
-        if m < n_staged:
+                gy_copy(m, k).wait()
+                for j in place.z_order():
+                    gz_copy(m, k, j).start()
+            done[0] = m + 1
+
+    def gather_x(n):
+        gather_z(n)
+        for m in range(done[1], min(n, n_staged)):
             for k in range(1, Y):
                 for j in range(1, Z):
                     gz_copy(m, k, j).wait()
                 gx_copy(m, k).start()
-        if 0 <= m - 4 < n_staged and m - 4 >= done[2]:
-            gather_c_step(m - 4)
-
-    def gather_c_step(m):
-        for k in range(1, Y):
-            gc_copy(m, k).wait()
-        done[2] = m + 1
-
-    last_step = n_staged + 4
-    done = [0, 0, 0]
-
-    def gather_y(n):
-        while done[0] < min(n, n_staged):
-            gather_y_step(done[0])
-            done[0] += 1
-
-    def gather_x(n, window=3):
-        while done[1] < min(n, last_step):
-            gather_y(done[1] + window)
-            gather_x_step(done[1])
-            done[1] += 1
-
-    def gather_until(m):
-        gather_x(m + 2)
-        while done[2] < min(m, n_staged):
-            gather_c_step(done[2])
+            done[1] = m + 1
+
+    def gather_c(n):
+        gather_x(n)
+        for m in range(done[2], min(n, n_staged)):
+            for k in range(1, Y):
+                gx_copy(m, k).wait()
+                gc_copy(m, k).start()
+            done[2] = m + 1
+
+    def gather_until(n):
+        gather_c(n)
+        for m in range(done[3], min(n, n_staged)):
+            for k in range(1, Y):
+                gc_copy(m, k).wait()
+            done[3] = m + 1
+
+    def gather_step(n):
+        gather_c(n - 3)
+        gather_x(n)
+        gather_z(n + 3)
+        gather_until(n - 5)
 
     def direct_step(h):
         for k in range(1, Y):
@@ -324,6 +324,8 @@
     for copy in own_sends:
         copy.start()
 
+    gather_z(3)
+
     for copy in small_sends:
         copy.wait()
     vec[...] = jnp.zeros_like(vec)
@@ -353,10 +355,12 @@
     for w in range(4):
         own_loads[w].wait()
         own_stores[w].start()
-    gather_x(3)
+    for m in range(3):
+        gather_x(m + 1)
+        gather_z(m + 4)
+        gather_c(m)
     x_swap.wait()
     lax.fori_loop(R // TR, rows // TR, norm_tile, 0)
-    gather_until(2)
     own_stores[QKV].wait()
     own_sends[QKV].wait()
 
@@ -374,15 +378,15 @@
         target = ref.wu.at[slot, :, pl.ds(0, CW)] if slot < 2 else ref.wq
         return load(ref.g_qkv.at[:, pl.ds(n * W + h * CW, CW)], target, ref.qsem.at[slot])
 
-    def project(h, ready=None):
+    def project(h, ready):
         here = slice(h * CW, (h + 1) * CW)
         tile_loads = [qkv_tile(1, h, 0), qkv_tile(2, h, 1), qkv_tile(0, h, 2)]
-        tile_loads[0].start()
-        tile_loads[1].start()
+        for n in range(2):
+            ready(n)
+            tile_loads[n].start()
         for n in range(3):
-            if n == 2:
-                if ready:
-                    ready()
+            if n == 1:
+                ready(2)
                 tile_loads[2].start()
             tile_loads[n].wait()
             for t in range(rows // MT):
@@ -403,7 +407,15 @@
             for k in range(1, half):
                 kv_copy(which, h, k).wait()
 
-    project(0, lambda: gather_until(3))
+    def first_ready(n):
+        gather_until(n + 1)
+        if n == 1:
+            gather_x(4)
+        elif n == 2:
+            gather_z(8)
+            gather_x(5)
+
+    project(0, first_ready)
     cot_swap.start()
     for h in range(len(direct)):
         gy_start(n_staged + h)
@@ -413,17 +425,27 @@
     def at_pair(p, act):
         plan.setdefault(p, []).append(act)
 
-    pace = (6, 7, 8, 9, 11, 12, 13, 14)
     for p in range(1, pairs):
-        at_pair(p, lambda p=p: gather_x(pace[p], 5))
+        at_pair(p, lambda p=p: gather_step(PACE[p]))
     if halves > 1:
         def second_half():
             gather_until(early)
-            project(1)
+            project(1, lambda n: None)
 
         at_pair(pairs // 2 - 1, second_half)
         at_pair(pairs // 2, lambda: exchanged(1))
-    gather_x(pace[0], 5)
+
+    proj_load = load(ref.g_proj, ref.proj_s, ref.lsem.at[10])
+
+    def proj_ready():
+        gather_until(early + halves)
+        own_stores[PROJ].wait()
+        own_stores[DOWN].wait()
+        own_sends[PROJ].wait()
+        proj_load.start()
+
+    at_pair(pairs - 1, proj_ready)
+    gather_step(PACE[0])
     exchanged(0)
 
     def both_heads(array, lane):
@@ -454,12 +476,6 @@
 
     lax.fori_loop(0, pairs, attend, 0)
 
-    gather_until(early + halves)
-    own_stores[PROJ].wait()
-    own_stores[DOWN].wait()
-    own_sends[PROJ].wait()
-    proj_load = load(ref.g_proj, ref.proj_s, ref.lsem.at[10])
-    proj_load.start()
     cot_load.wait()
     cot_swap.wait()
     small[...] = jnp.zeros_like(small)
@@ -473,17 +489,8 @@
 
     lax.fori_loop(0, rows // TR, feed_tile, 0)
     proj_load.wait()
-
-    def branch_tile(t, _):
-        tile = pl.ds(pl.multiple_of(t * MT, MT), MT)
-        low = matmul(attended[tile, :], ref.proj_s[...]) + vector(PROJ_B)
-        branch[tile, :] = low
-        unit, _ = norm_parts(x_s[tile, :].astype(F32) + vector(ATTN_SCALE) * low)
-        second[tile, :] = (unit * vector(MLP_GAIN) + vector(MLP_SHIFT)).astype(BF)
-        return 0
-
-    lax.fori_loop(0, rows // MT, branch_tile, 0)
-    gather_x(pace[-1] + 2, 5)
+    gather_step(PACE[-1])
+
     for w in (UP, DOWN):
         own_sends[w].wait()
     own_stores[UP].wait()
@@ -505,6 +512,15 @@
     for copy in block_loads(0):
         copy.start()
 
+    def branch_tile(t, _):
+        tile = pl.ds(pl.multiple_of(t * MT, MT), MT)
+        low = matmul(attended[tile, :], ref.proj_s[...]) + vector(PROJ_B)
+        branch[tile, :] = low
+        unit, _ = norm_parts(x_s[tile, :].astype(F32) + vector(ATTN_SCALE) * low)
+        second[tile, :] = (unit * vector(MLP_GAIN) + vector(MLP_SHIFT)).astype(BF)
+        return 0
+
+    lax.fori_loop(0, rows // MT, branch_tile, 0)
     def core_copy(i):
         a = lax.rem(i, CORE_SLOTS)
         return send(part.at[lax.rem(i, 2), 1 - place.c], crecv.at[a], ref.cs.at[a], ref.cr.at[a],
@@ -662,25 +678,24 @@
     acc, gmid, act, slope = ref.acc, ref.gmid, ref.act_s, ref.slope_s
     spread = []
     for b in range(n_blocks):
-        start = spread[-1][1] if spread else done[1]
         goal, over = need[min(b + 1, n_blocks - 1)]
-        soon = need[min(b + 2, n_blocks - 1)][1]
-        spread.append((start, min(max(goal + 4, start + 2), last_step), over, soon))
+        spread.append((goal, over, need[min(b + 2, n_blocks - 1)][1]))
 
     def block_step(b, _):
         slot = lax.rem(b, 2)
         for copy in block_loads(b):
             copy.wait()
 
-        for at, (_, stop, over, soon) in enumerate(spread):
+        for at, (goal, over, soon) in enumerate(spread):
             @pl.when(b == at)
-            def _(at=at, stop=stop, over=over, soon=soon):
-                gather_x(stop, 5)
-                for h in range(spread[at - 1][2] if at else need[0][1], over):
+            def _(at=at, goal=goal, over=over, soon=soon):
+                gather_until(goal)
+                gather_step(done[1] + 3)
+                for h in range(spread[at - 1][1] if at else need[0][1], over):
                     if at == 0:
                         direct_step(h)
                     direct_arrived(h)
-                for h in range(spread[at - 1][3] if at else over, soon):
+                for h in range(spread[at - 1][2] if at else over, soon):
                     direct_step(h)
 
         @pl.when(b + 1 < n_blocks)
@@ -738,7 +753,7 @@
 
     lax.fori_loop(0, n_blocks, block_step, 0)
 
-    tok_out, tok_send = ref.tok_out, ref.tok_send
+    tok_out, tok_send, tok_own = ref.tok_out, ref.tok_send, ref.tok_own
 
     def to_owner(t, value, kept, given):
         if R >= TM:
@@ -746,13 +761,13 @@
 
             @pl.when(t * TM < R)
             def _():
-                kept[mine, lower, :] = value.astype(kept.dtype)
+                kept[lower, :] = value.astype(kept.dtype)
 
             @pl.when(t * TM >= R)
             def _():
                 given[lower, :] = value.astype(BF)
         else:
-            kept[mine] = value[:R].astype(kept.dtype)
+            kept[...] = value[:R].astype(kept.dtype)
             given[...] = value[R:].astype(BF)
 
     def middle_tile(t, _):
@@ -760,7 +775,7 @@
         low = branch[tile, :]
         middle = x_s[tile, :].astype(F32) + vector(ATTN_SCALE) * low
         feed = acc[tile, :] + vector(DOWN_B)
-        to_owner(t, (middle + vector(MLP_SCALE) * feed) * vector(LIVE), tok_out, tok_send)
+        to_owner(t, (middle + vector(MLP_SCALE) * feed) * vector(LIVE), tok_own, tok_send)
         upstream = cot[tile, :].astype(F32) * vector(LIVE)
         note(MLP_SCALE, jnp.sum(upstream * feed, axis=0, keepdims=True))
         unit, scale = norm_parts(middle)
@@ -791,6 +806,8 @@
 
     lax.fori_loop(0, rows // TM, middle_step, 0)
     tok_copy = send(tok_send, tok_out.at[mine], ref.ts.at[0], ref.tr.at[0], swap_peer)
+    tok_store = load(tok_own, tok_out.at[mine], ref.lsem.at[11])
+    tok_store.start()
 
     def qkv_load(n):
         slot = lax.rem(n, 2)
@@ -913,7 +930,7 @@
 
     lax.fori_loop(0, 3 * W // CW, qkv_step, 0)
 
-    gt_out, gt_send, gt_recv = ref.gt_out, ref.gt_send, ref.gt_recv
+    gt_own, gt_send = ref.gt_own_s, ref.gt_send
 
     def first_tile(t, _):
         tile = pl.ds(pl.multiple_of(t * TM, TM), TM)
@@ -923,7 +940,7 @@
         note(ATTN_SHIFT, jnp.sum(grad, axis=0, keepdims=True))
         note(QV, jnp.sum(G[tile, :W].astype(F32), axis=0, keepdims=True))
         note(QV + 1, jnp.sum(G[tile, 2 * W :].astype(F32), axis=0, keepdims=True))
-        to_owner(t, gmid[tile, :] + norm_back(grad, unit, scale, vector(ATTN_GAIN)), gt_out, gt_send)
+        to_owner(t, gmid[tile, :] + norm_back(grad, unit, scale, vector(ATTN_GAIN)), gt_own, gt_send)
         return 0
 
     lax.fori_loop(0, rows // TM, first_tile, 0)
@@ -969,7 +986,9 @@
             ref.small_out[...] = whole
 
     core_small.start()
-    gt_copy = send(gt_send, gt_recv, ref.ts.at[1], ref.tr.at[1], swap_peer)
+    gt_copy = send(gt_send, ref.gt_low, ref.ts.at[1], ref.tr.at[1], swap_peer)
+    gt_store = load(gt_own, ref.gt_own, ref.lsem.at[10])
+    gt_store.start()
     depth = 3 + 5 * LAG
     small_after = {0: 0, 2 + LAG: 1, 2 + 2 * LAG: 2, 2 + 3 * LAG: 3}
     for lag in range(depth):
@@ -979,9 +998,8 @@
         if lag == 0:
             gt_copy.start()
             tok_copy.start()
-    tok_copy.wait()
-    gt_copy.wait()
-    gt_out[1 - mine] = gt_recv[...].astype(F32)
+    for copy in (tok_store, gt_store, gt_copy, tok_copy):
+        copy.wait()
 
 
 def layer(replicas, shards, vectors, count, tokens, cotangent, weights):
@@ -1044,7 +1062,8 @@
         gv_acc=pltpu.VMEM((keys, 128), F32),
         tok_send=pltpu.VMEM((R, W), BF),
         gt_send=pltpu.VMEM((R, W), BF),
-        gt_recv=pltpu.VMEM((R, W), BF),
+        tok_own=pltpu.VMEM((R, W), BF),
+        gt_own_s=pltpu.VMEM((R, W), F32),
         small_s=pltpu.VMEM((shards, 16, W // shards), F32),
         vec=pltpu.VMEM((16, W), F32),
         lse=pltpu.VMEM((W // 128, 1, 2 * rows), F32),
@@ -1075,7 +1094,8 @@
         o_qkv=jax.ShapeDtypeStruct((W // shards, 3 * W), BF),
         small_out=jax.ShapeDtypeStruct((16, W // shards), F32),
         tok_out=jax.ShapeDtypeStruct((2, R, W), BF),
-        gt_out=jax.ShapeDtypeStruct((2, R, W), F32),
+        gt_own=jax.ShapeDtypeStruct((R, W), F32),
+        gt_low=jax.ShapeDtypeStruct((R, W), BF),
         g_qkv=jax.ShapeDtypeStruct((W, 3 * W), BF),
         g_proj=jax.ShapeDtypeStruct((W, W), BF),
         g_up=jax.ShapeDtypeStruct((W, FF), BF),
@@ -1085,24 +1105,25 @@
     results = pl.pallas_call(
         functools.partial(layer_kernel, replicas, shards, multiples, names),
         in_specs=[vmem] * len(vectors) + [pl.BlockSpec(memory_space=pltpu.SMEM)] + [anywhere] * 6,
-        out_specs=[anywhere] * 4 + [vmem] * 3 + [anywhere] * 4,
+        out_specs=[anywhere] * 4 + [vmem] + [anywhere] * 7,
         out_shape=list(outs.values()),
         scratch_shapes=list(scratch.values()),
         compiler_params=pltpu.CompilerParams(
             collective_id=0, has_side_effects=True, vmem_limit_bytes=63 * MIB
         ),
     )(*vectors, *inputs.values())
-    return results[:7]
+    return results[:8]
 
 
 def result_kernel(shards, n_vectors, *refs):
-    small, *ins = refs[:7]
-    outs = refs[7:13]
-    vectors = refs[13 : 13 + n_vectors]
-    low, wide, tok_s, gt_s, in_sem, out_sem = refs[13 + n_vectors :]
+    small, tok, gt_own, gt_low, *ins = refs[:8]
+    tok_out, gt_out, *outs = refs[8:14]
+    vectors = refs[14 : 14 + n_vectors]
+    low, wide, tok_s, own_s, low_s, gt_s, in_sem, out_sem = refs[14 + n_vectors :]
+    mine = lax.div(lax.axis_index("shard"), shards // 2)
     size, width = low.shape[1:]
     blocks = []
-    for source, target in zip(ins[2:], outs[2:]):
+    for source, target in zip(ins, outs):
         for r in range(source.shape[0] // size):
             for c in range(source.shape[1] // width):
                 at = (pl.ds(r * size, size), pl.ds(c * width, width))
@@ -1110,9 +1131,13 @@
     n = len(blocks)
     loads = [pltpu.make_async_copy(src, low.at[i], in_sem.at[i]) for i, (src, _) in enumerate(blocks)]
     stores = [pltpu.make_async_copy(wide.at[i], dst, out_sem.at[i]) for i, (_, dst) in enumerate(blocks)]
-    for i, (source, middle, target) in enumerate(((ins[0], tok_s, outs[0]), (ins[1], gt_s, outs[1]))):
+    for i, (source, middle) in enumerate(((gt_low, low_s), (gt_own, own_s), (tok, tok_s))):
         loads.append(pltpu.make_async_copy(source, middle, in_sem.at[n + i]))
-        stores.append(pltpu.make_async_copy(middle, target, out_sem.at[n + i]))
+    stores += [
+        pltpu.make_async_copy(gt_s, gt_out.at[1 - mine], out_sem.at[n]),
+        pltpu.make_async_copy(own_s, gt_out.at[mine], out_sem.at[n + 1]),
+        pltpu.make_async_copy(tok_s, tok_out, out_sem.at[n + 2]),
+    ]
     for copy in loads:
         copy.start()
     at = 0
@@ -1120,21 +1145,23 @@
         pieces = [small[at + r : at + r + 1, :] for r in range(count)]
         vector[...] = jnp.concatenate(pieces, axis=1).reshape(vector.shape)
         at += count
-    for i in range(n + 2):
+    for i in range(n + 3):
         loads[i].wait()
         if i < n:
             wide[i] = low[i].astype(F32)
+        elif i == n:
+            gt_s[...] = low_s[...].astype(F32)
         stores[i].start()
     for copy in stores:
         copy.wait()
 
 
-def results(shards, small, tok, gt, grads):
+def results(shards, small, tok, gt_own, gt_low, grads):
     _, R, W = tok.shape
     size = W // shards
     count = sum(grad.shape[0] * grad.shape[1] for grad in grads) // (size * W)
     vmem, anywhere = pl.BlockSpec(memory_space=pltpu.VMEM), pl.BlockSpec(memory_space=pl.ANY)
-    shapes = [jax.ShapeDtypeStruct(tok.shape, BF), jax.ShapeDtypeStruct(gt.shape, F32)]
+    shapes = [jax.ShapeDtypeStruct(tok.shape, BF), jax.ShapeDtypeStruct(tok.shape, F32)]
     shapes += [jax.ShapeDtypeStruct(grad.shape, F32) for grad in grads]
     n_vectors = len(SMALL_ROWS) if size % 128 == 0 else 0
     for _, rows in SMALL_ROWS[:n_vectors]:
@@ -1142,15 +1169,16 @@
     dma = pltpu.SemaphoreType.DMA
     tok, gt, *rest = pl.pallas_call(
         functools.partial(result_kernel, shards, n_vectors),
-        in_specs=[vmem] + [anywhere] * 6,
+        in_specs=[vmem] + [anywhere] * 7,
         out_specs=[anywhere] * 6 + [vmem] * n_vectors,
         out_shape=shapes,
         scratch_shapes=[
             pltpu.VMEM((count, size, W), BF), pltpu.VMEM((count, size, W), F32),
-            pltpu.VMEM(tok.shape, BF), pltpu.VMEM(gt.shape, F32), dma((count + 2,)), dma((count + 2,)),
+            pltpu.VMEM(tok.shape, BF), pltpu.VMEM((R, W), F32), pltpu.VMEM((R, W), BF), pltpu.VMEM((R, W), F32),
+            dma((count + 3,)), dma((count + 3,)),
         ],
         compiler_params=pltpu.CompilerParams(vmem_limit_bytes=63 * MIB),
-    )(small, tok, gt, *grads)
+    )(small, tok, gt_own, gt_low, *grads)
     vectors = rest[4:]
     if not n_vectors:
         at = 0
@@ -1165,11 +1193,12 @@
               cotangent, image_count):
     vectors = (qv_bias, proj_bias, up_bias, down_bias, attn_gain, attn_shift, mlp_gain, mlp_shift,
                attn_scale, mlp_scale)
-    *grads, small, output, grad_tokens = layer(
+    *grads, small, output, grad_own, grad_low = layer(
         replicas, shards, vectors, image_count, tokens, cotangent,
         (qkv_weight, proj_weight, up_weight, down_weight),
     )
-    output, grad_tokens, (down, up, proj, qkv), small = results(shards, small, output, grad_tokens, grads)
+    output, grad_tokens, (down, up, proj, qkv), small = results(
+        shards, small, output, grad_own, grad_low, grads)
     qv_b, proj_b, up_b, down_b, *norms = small
     return (output, grad_tokens, qkv, qv_b, proj, proj_b, up, up_b, down, down_b, *norms)
 

time: 263 us -> 257 us (0.977)
  Pallas kernels: 262 us -> 256 us
    pallas_call x1, Pallas kernels: 251 us -> 246 us  [layer(): pl.pallas_call(functools.partial(layer_kernel, replicas, shards, multiple...]
where the time goes in v6:
time: 257 us
  Pallas kernels  256 us (100%)
    pallas_call x1, Pallas kernels, layer(): pl.pallas_call(functools.partial(layer_kernel, replicas, shards, multiple...  246 us
    pallas_call x1, Pallas kernels, results(): pl.pallas_call(functools.partial(result_kernel, shards, n_vectors), in_sp...  9.79 us

profile of v6, /device:TPU:0, one launch (start us, length us, event | category | flops | bytes accessed | tf_op | source)
XLA Modules:
  0.0 256.8 jit_solution(13041133188879262777)
XLA Ops:
  0.7 246.2 %shard_map.288 = (bf16[1024,1024]{1,0:T(8,128)(2,1)}, bf16[256,4096]{1,0:T(8,128)(2,1)}, bf16[256,1024]{1,0:T(8,128)(2,1)}, bf16[256,3072]{1,0:T(8,128)(2,1)}, f...) custom-call(bf16[512]{0:T(512)(128)(2,1)} %refs_0_.1, ...), custom_call_target="tpu_custom_call" | custom-call | tf_op jit(solution)/shard_map/pallas_call | solution.py:1105
  246.8 9.8 %shard_map.289 = (bf16[2,256,1024]{2,1,0:T(8,128)(2,1)}, f32[2,256,1024]{2,1,0:T(8,128)}, f32[1024,1024]{1,0:T(8,128)}, f32[256,4096]{1,0:T(8,128)}, f32[256,102...) custom-call(f32[16,256]{1,0:T(8,128)} %get-tuple-element.40.refs_0_,, ...), custom_call_target="tpu_custom_call" | custom-call | tf_op jit(solution)/shard_map/pallas_call | solution.py:1170

commit v7 on v6

--- a/solution.py
+++ b/solution.py
@@ -166,7 +166,7 @@
     kv, gpre, cot, gfeed, G = ref.kv, ref.gpre, ref.cot_s, ref.gfeed, ref.G
     second, first, query, x_s = ref.second_s, ref.first_s, ref.query_s, ref.x_s
     attended, branch, gbranch, gatt = ref.attended_s, ref.branch_s, ref.gbranch, ref.gatt
-    TR, MT, QT, TM = min(128, R), min(256, rows), min(256, rows), min(256, R)
+    TR, MT, QT, TM = min(128, R), min(512, rows), min(256, rows), min(256, R)
     pairs, tiles = W // 128, rows // QT
 
     def half_peer(k):

time: 257 us -> 257 us (level)
  no operation moved by 1% of the time
where the time goes in v7:
time: 257 us; the launch traced here: 256 us
  Pallas kernels  255 us (99%)
    pallas_call x1, Pallas kernels, layer(): pl.pallas_call(functools.partial(layer_kernel, replicas, shards, multiple...  246 us
    pallas_call x1, Pallas kernels, results(): pl.pallas_call(functools.partial(result_kernel, shards, n_vectors), in_sp...  9.79 us

profile of v7, /device:TPU:0, one launch (start us, length us, event | category | flops | bytes accessed | tf_op | source)
XLA Modules:
  0.0 256.2 jit_solution(18339316689956894986)
XLA Ops:
  0.7 245.6 %shard_map.288 = (bf16[1024,1024]{1,0:T(8,128)(2,1)}, bf16[256,4096]{1,0:T(8,128)(2,1)}, bf16[256,1024]{1,0:T(8,128)(2,1)}, bf16[256,3072]{1,0:T(8,128)(2,1)}, f...) custom-call(bf16[512]{0:T(512)(128)(2,1)} %refs_0_.1, ...), custom_call_target="tpu_custom_call" | custom-call | tf_op jit(solution)/shard_map/pallas_call | solution.py:1105
  246.3 9.8 %shard_map.289 = (bf16[2,256,1024]{2,1,0:T(8,128)(2,1)}, f32[2,256,1024]{2,1,0:T(8,128)}, f32[1024,1024]{1,0:T(8,128)}, f32[256,4096]{1,0:T(8,128)}, f32[256,102...) custom-call(f32[16,256]{1,0:T(8,128)} %get-tuple-element.40.refs_0_,, ...), custom_call_target="tpu_custom_call" | custom-call | tf_op jit(solution)/shard_map/pallas_call | solution.py:1170
